TPU v7x, 32 devices: a whole 2x2x4 slice. The times are simulated.
32 devices in a mesh: shard: 4 (over y, x), dp: 8 (over z, core).
Axes of the slice: x: 2, y: 2, z: 4, core: 2. Of those that a mesh axis runs over, the one named last changes fastest.
Arguments:
- tokens: bfloat16 [8192, 1024], P(('shard', 'dp')), may hold values from -6 to 6
- cotangent: bfloat16 [8192, 1024], P(('shard', 'dp')), may hold values from -6 to 6
- lengths: int32 [32, 4], P(('shard', 'dp')), may hold values from 0 to 256, as said below
- w_qkv: float32 [1024, 3072], P('shard'), may hold values from -0.1875 to 0.1875
- w_out: float32 [1024, 1024], P('shard'), may hold values from -0.75 to 0.75
- w_up: float32 [1024, 4096], P('shard'), may hold values from -0.1875 to 0.1875
- w_down: float32 [4096, 1024], P('shard'), may hold values from -0.09375 to 0.09375
- vectors: float32 [13, 1024], P(None, 'shard')
- m_qkv: float32 [1024, 3072], P('shard'), may hold values from -0.75 to 0.75
- m_out: float32 [1024, 1024], P('shard'), may hold values from -0.75 to 0.75
- m_up: float32 [1024, 4096], P('shard'), may hold values from -0.75 to 0.75
- m_down: float32 [4096, 1024], P('shard'), may hold values from -0.75 to 0.75
- m_vectors: float32 [13, 1024], P(None, 'shard'), may hold values from -0.75 to 0.75
- v_qkv: float32 [1024, 3072], P('shard'), may hold values from 0.002 to 0.02
- v_out: float32 [1024, 1024], P('shard'), may hold values from 0.002 to 0.02
- v_up: float32 [1024, 4096], P('shard'), may hold values from 0.002 to 0.02
- v_down: float32 [4096, 1024], P('shard'), may hold values from 0.002 to 0.02
- v_vectors: float32 [13, 1024], P(None, 'shard'), may hold values from 0.002 to 0.02
Outputs:
- output: bfloat16 [8192, 1024], P(('shard', 'dp'))
- input_grad: bfloat16 [8192, 1024], P(('shard', 'dp'))
- grad_qkv: float32 [1024, 3072], P('shard')
- grad_out: float32 [1024, 1024], P('shard')
- grad_up: float32 [1024, 4096], P('shard')
- grad_down: float32 [4096, 1024], P('shard')
- grad_vectors: float32 [13, 1024], P(None, 'shard')
- new_qkv: float32 [1024, 3072], P('shard')
- new_out: float32 [1024, 1024], P('shard')
- new_up: float32 [1024, 4096], P('shard')
- new_down: float32 [4096, 1024], P('shard')
- new_vectors: float32 [13, 1024], P(None, 'shard')
- first_qkv: float32 [1024, 3072], P('shard')
- first_out: float32 [1024, 1024], P('shard')
- first_up: float32 [1024, 4096], P('shard')
- first_down: float32 [4096, 1024], P('shard')
- first_vectors: float32 [13, 1024], P(None, 'shard')
- second_qkv: float32 [1024, 3072], P('shard')
- second_out: float32 [1024, 1024], P('shard')
- second_up: float32 [1024, 4096], P('shard')
- second_down: float32 [4096, 1024], P('shard')
- second_vectors: float32 [13, 1024], P(None, 'shard')
Inputs may be any that keep to these rules, and one draw needn't show every extreme that they name: Row b lists the lengths of the sequences packed from the first slot of token block b in order, 0 for an unused slot; a row sums to at most 256, and some row holds one sequence of exactly 256 tokens.
All inputs are finite; a program needn't handle non-finite values.
Results may differ from a plain program's by a relative error of at most 0.012.
The roundings to bfloat16 on the way count: a program that leaves them out, or rounds other values in their place, can miss the bound.
Values may be sent and summed in bfloat16 or wider, within the bound.
No kernel may reach another device: no remote copies, remote signals or barrier semaphores. Data moves between devices by JAX's collectives and lax.ppermute only.
A program may use at most 320 MiB of HBM per device.

v0:
```python
import math

import jax
import jax.numpy as jnp
from jax import lax
from jax.sharding import PartitionSpec as P

H = 16
HD = 64
ROT = 16
ADAM_STEP = 4


EPS_NORM = 1e-05
BETA_ONE = 0.9
BETA_TWO = 0.95
ADAM_EPS = 1e-08
LEARN_RATE = 0.01
VECTOR_RATE = 0.1
DECAY_RATE = 0.1
SQRT_HALF = 0.7071067811865476
INV_ROOT_TWO_PI = 0.3989422804014327


def matmul(left, right):
    return jnp.dot(left, right, preferred_element_type=jnp.float32)


def left_t(left, right):
    return lax.dot_general(
        left, right, (((0,), (0,)), ((), ())), preferred_element_type=jnp.float32
    )


def right_t(left, right):
    return lax.dot_general(
        left, right, (((1,), (1,)), ((), ())), preferred_element_type=jnp.float32
    )


def heads_mix(form, left, right):
    return jnp.einsum(form, left, right, preferred_element_type=jnp.float32)


def normalize(values):
    centred = values - jnp.mean(values, axis=-1, keepdims=True)
    inv_std = lax.rsqrt(jnp.mean(centred * centred, axis=-1, keepdims=True) + EPS_NORM)
    return (centred * inv_std, inv_std)


def rotary_tables(position):
    half_dims = ROT // 2
    freq = jnp.exp(-jnp.arange(half_dims, dtype=jnp.float32) * (2.0 * math.log(10000.0) / ROT))
    angles = position.astype(jnp.float32)[:, None] * freq[None, :]
    return (jnp.cos(angles)[:, None, :], jnp.sin(angles)[:, None, :])


def rotate(values, cosine, sine):
    half_dims = ROT // 2
    first = values[..., :half_dims]
    second = values[..., half_dims:ROT]
    return jnp.concatenate(
        [first * cosine - second * sine, second * cosine + first * sine, values[..., ROT:]], axis=-1
    )


def unrotate(values, cosine, sine):
    half_dims = ROT // 2
    first = values[..., :half_dims]
    second = values[..., half_dims:ROT]
    return jnp.concatenate(
        [first * cosine + second * sine, second * cosine - first * sine, values[..., ROT:]], axis=-1
    )


def gelu_value(values):
    return 0.5 * values * (1.0 + lax.erf(values * SQRT_HALF))


def gelu_slope(values):
    return (
        0.5 * (1.0 + lax.erf(values * SQRT_HALF))
        + values * jnp.exp(-0.5 * values * values) * INV_ROOT_TWO_PI
    )


def layer_pass(tokens, cotangent, counts, params):
    w_qkv, w_out, w_up, w_down, vectors = params
    rows = tokens.shape[0]
    width = tokens.shape[1]
    scale = HD ** (-0.5)
    vector_rows = vectors.astype(jnp.float32)
    index_rows = jnp.arange(rows, dtype=jnp.int32)
    ends = jnp.cumsum(counts)
    passed = ends[None, :] <= index_rows[:, None]
    segment = jnp.sum(passed.astype(jnp.int32), axis=1)
    starts = jnp.sum(jnp.where(passed, counts[None, :], 0), axis=1)
    position = index_rows - starts
    valid = (index_rows < ends[-1]).astype(jnp.float32)[:, None]
    allowed = (segment[:, None] == segment[None, :]) & (index_rows[None, :] <= index_rows[:, None])
    x_float = tokens.astype(jnp.float32)
    normed, inv_std = normalize(x_float)
    in_attn = (normed * vector_rows[0] + vector_rows[1]).astype(jnp.bfloat16)
    in_mlp = (normed * vector_rows[2] + vector_rows[3]).astype(jnp.bfloat16)
    qkv_bias = vector_rows[6:9].reshape(-1)
    up_bias = vector_rows[9:].reshape(-1)
    projected = matmul(in_attn, w_qkv) + qkv_bias
    cosine, sine = rotary_tables(position)
    query_b = rotate(projected[:, :width].reshape(rows, H, HD), cosine, sine).astype(jnp.bfloat16)
    key_b = rotate(projected[:, width : 2 * width].reshape(rows, H, HD), cosine, sine).astype(
        jnp.bfloat16
    )
    value_b = projected[:, 2 * width :].reshape(rows, H, HD).astype(jnp.bfloat16)
    scores = heads_mix("qhd,khd->hqk", query_b, key_b) * scale
    scores = jnp.where(allowed[None], scores, -1e30)
    top_score = jnp.max(scores, axis=-1, keepdims=True)
    log_total = top_score + jnp.log(jnp.sum(jnp.exp(scores - top_score), axis=-1, keepdims=True))
    probs = jnp.exp(scores - log_total)
    probs_b = probs.astype(jnp.bfloat16)
    heads_b = heads_mix("hqk,khd->qhd", probs_b, value_b).astype(jnp.bfloat16).reshape(rows, width)
    attn = matmul(heads_b, w_out) + vector_rows[4]
    up_pre = matmul(in_mlp, w_up) + up_bias
    act_b = gelu_value(up_pre).astype(jnp.bfloat16)
    mlp = matmul(act_b, w_down) + vector_rows[5]
    output = (x_float + valid * (attn + mlp)).astype(jnp.bfloat16)
    cot_float = cotangent.astype(jnp.float32)
    branch_grad = cot_float * valid
    branch_b = branch_grad.astype(jnp.bfloat16)
    grad_out = left_t(heads_b, branch_b)
    grad_down = left_t(act_b, branch_b)
    bias_out = jnp.sum(branch_grad, axis=0)
    d_heads = right_t(branch_b, w_out).astype(jnp.bfloat16).reshape(rows, H, HD)
    d_up = right_t(branch_b, w_down) * gelu_slope(up_pre)
    d_up_b = d_up.astype(jnp.bfloat16)
    grad_up = left_t(in_mlp, d_up_b)
    bias_up = jnp.sum(d_up, axis=0)
    d_mlp_in = right_t(d_up_b, w_up)
    d_probs = heads_mix("qhd,khd->hqk", d_heads, value_b)
    delta = jnp.sum(probs * d_probs, axis=-1, keepdims=True)
    d_scores = (probs * (d_probs - delta)).astype(jnp.bfloat16)
    d_query = heads_mix("hqk,khd->qhd", d_scores, key_b) * scale
    d_key = heads_mix("hqk,qhd->khd", d_scores, query_b) * scale
    d_value = heads_mix("hqk,qhd->khd", probs_b, d_heads)
    d_proj = jnp.concatenate(
        [
            unrotate(d_query, cosine, sine).reshape(rows, width),
            unrotate(d_key, cosine, sine).reshape(rows, width),
            d_value.reshape(rows, width),
        ],
        axis=1,
    )
    bias_qkv = jnp.sum(d_proj, axis=0)
    d_proj_b = d_proj.astype(jnp.bfloat16)
    grad_qkv = left_t(in_attn, d_proj_b)
    d_attn_in = right_t(d_proj_b, w_qkv)
    scaled = d_attn_in * vector_rows[0] + d_mlp_in * vector_rows[2]
    d_tokens = inv_std * (
        scaled
        - jnp.mean(scaled, axis=-1, keepdims=True)
        - normed * jnp.mean(scaled * normed, axis=-1, keepdims=True)
    )
    input_grad = (cot_float + d_tokens).astype(jnp.bfloat16)
    grad_vectors = jnp.concatenate(
        [
            jnp.sum(d_attn_in * normed, axis=0)[None],
            jnp.sum(d_attn_in, axis=0)[None],
            jnp.sum(d_mlp_in * normed, axis=0)[None],
            jnp.sum(d_mlp_in, axis=0)[None],
            bias_out[None],
            bias_out[None],
            bias_qkv.reshape(3, width),
            bias_up.reshape(-1, width),
        ],
        axis=0,
    )
    return (output, input_grad, (grad_qkv, grad_out, grad_up, grad_down, grad_vectors))


def adam_update(weight, first, second, grad, count, decay, rate):
    first_new = BETA_ONE * first + (1.0 - BETA_ONE) * grad
    second_new = BETA_TWO * second + (1.0 - BETA_TWO) * grad * grad
    corr_one = 1.0 - jnp.exp(count * math.log(BETA_ONE))
    corr_two = 1.0 - jnp.exp(count * math.log(BETA_TWO))
    step_size = first_new / corr_one / (jnp.sqrt(second_new / corr_two) + ADAM_EPS)
    return (weight - rate * (step_size + decay * weight), first_new, second_new)


def local(
    tokens,
    cotangent,
    lengths,
    w_qkv,
    w_out,
    w_up,
    w_down,
    vectors,
    m_qkv,
    m_out,
    m_up,
    m_down,
    m_vectors,
    v_qkv,
    v_out,
    v_up,
    v_down,
    v_vectors,
):
    masters = (w_qkv, w_out, w_up, w_down, vectors)
    firsts = (m_qkv, m_out, m_up, m_down, m_vectors)
    seconds = (v_qkv, v_out, v_up, v_down, v_vectors)
    split_dims = (0, 0, 0, 0, 1)
    decays = (DECAY_RATE, DECAY_RATE, DECAY_RATE, DECAY_RATE, 0.0)
    rates = (LEARN_RATE, LEARN_RATE, LEARN_RATE, LEARN_RATE, VECTOR_RATE)
    working = (
        lax.all_gather(w_qkv.astype(jnp.bfloat16), "shard", axis=0, tiled=True),
        lax.all_gather(w_out.astype(jnp.bfloat16), "shard", axis=0, tiled=True),
        lax.all_gather(w_up.astype(jnp.bfloat16), "shard", axis=0, tiled=True),
        lax.all_gather(w_down.astype(jnp.bfloat16), "shard", axis=0, tiled=True),
        lax.all_gather(vectors.astype(jnp.bfloat16), "shard", axis=1, tiled=True),
    )
    output, input_grad, local_grads = layer_pass(tokens, cotangent, lengths[0], working)
    token_total = tokens.shape[0] * lax.axis_size("shard") * lax.axis_size("dp")
    grad_scale = float(token_total) ** (-0.5)
    scaled_grads = tuple((item * grad_scale for item in local_grads))
    count = jnp.float32(ADAM_STEP)
    pieces = (
        lax.psum_scatter(scaled_grads[0], ("shard", "dp"), scatter_dimension=0, tiled=True),
        lax.psum_scatter(scaled_grads[1], ("shard", "dp"), scatter_dimension=0, tiled=True),
        lax.psum_scatter(scaled_grads[2], ("shard", "dp"), scatter_dimension=0, tiled=True),
        lax.psum_scatter(scaled_grads[3], ("shard", "dp"), scatter_dimension=0, tiled=True),
        lax.psum_scatter(scaled_grads[4], ("shard", "dp"), scatter_dimension=1, tiled=True),
    )
    dp_index = lax.axis_index("dp")
    part_w = []
    part_m = []
    part_v = []
    for which in range(5):
        along = split_dims[which]
        extent = pieces[which].shape[along]
        begin = dp_index * extent
        own_w = lax.dynamic_slice_in_dim(masters[which], begin, extent, along)
        own_m = lax.dynamic_slice_in_dim(firsts[which], begin, extent, along)
        own_v = lax.dynamic_slice_in_dim(seconds[which], begin, extent, along)
        result = adam_update(own_w, own_m, own_v, pieces[which], count, decays[which], rates[which])
        part_w.append(result[0])
        part_m.append(result[1])
        part_v.append(result[2])
    gathered = (
        lax.all_gather(part_w[0].astype(jnp.bfloat16), "dp", axis=0, tiled=True).astype(
            jnp.float32
        ),
        lax.all_gather(part_w[1].astype(jnp.bfloat16), "dp", axis=0, tiled=True).astype(
            jnp.float32
        ),
        lax.all_gather(part_w[2].astype(jnp.bfloat16), "dp", axis=0, tiled=True).astype(
            jnp.float32
        ),
        lax.all_gather(part_w[3].astype(jnp.bfloat16), "dp", axis=0, tiled=True).astype(
            jnp.float32
        ),
        lax.all_gather(part_w[4].astype(jnp.bfloat16), "dp", axis=1, tiled=True).astype(
            jnp.float32
        ),
        lax.all_gather(part_m[0].astype(jnp.bfloat16), "dp", axis=0, tiled=True).astype(
            jnp.float32
        ),
        lax.all_gather(part_m[1].astype(jnp.bfloat16), "dp", axis=0, tiled=True).astype(
            jnp.float32
        ),
        lax.all_gather(part_m[2].astype(jnp.bfloat16), "dp", axis=0, tiled=True).astype(
            jnp.float32
        ),
        lax.all_gather(part_m[3].astype(jnp.bfloat16), "dp", axis=0, tiled=True).astype(
            jnp.float32
        ),
        lax.all_gather(part_m[4].astype(jnp.bfloat16), "dp", axis=1, tiled=True).astype(
            jnp.float32
        ),
        lax.all_gather(part_v[0].astype(jnp.bfloat16), "dp", axis=0, tiled=True).astype(
            jnp.float32
        ),
        lax.all_gather(part_v[1].astype(jnp.bfloat16), "dp", axis=0, tiled=True).astype(
            jnp.float32
        ),
        lax.all_gather(part_v[2].astype(jnp.bfloat16), "dp", axis=0, tiled=True).astype(
            jnp.float32
        ),
        lax.all_gather(part_v[3].astype(jnp.bfloat16), "dp", axis=0, tiled=True).astype(
            jnp.float32
        ),
        lax.all_gather(part_v[4].astype(jnp.bfloat16), "dp", axis=1, tiled=True).astype(
            jnp.float32
        ),
        lax.all_gather(pieces[0].astype(jnp.bfloat16), "dp", axis=0, tiled=True).astype(
            jnp.float32
        ),
        lax.all_gather(pieces[1].astype(jnp.bfloat16), "dp", axis=0, tiled=True).astype(
            jnp.float32
        ),
        lax.all_gather(pieces[2].astype(jnp.bfloat16), "dp", axis=0, tiled=True).astype(
            jnp.float32
        ),
        lax.all_gather(pieces[3].astype(jnp.bfloat16), "dp", axis=0, tiled=True).astype(
            jnp.float32
        ),
        lax.all_gather(pieces[4].astype(jnp.bfloat16), "dp", axis=1, tiled=True).astype(
            jnp.float32
        ),
    )
    new_w = gathered[0:5]
    new_m = gathered[5:10]
    new_v = gathered[10:15]
    full_grads = gathered[15:20]
    return (
        output,
        input_grad,
        full_grads[0],
        full_grads[1],
        full_grads[2],
        full_grads[3],
        full_grads[4],
        new_w[0],
        new_w[1],
        new_w[2],
        new_w[3],
        new_w[4],
        new_m[0],
        new_m[1],
        new_m[2],
        new_m[3],
        new_m[4],
        new_v[0],
        new_v[1],
        new_v[2],
        new_v[3],
        new_v[4],
    )


def solution(mesh):
    placed = (
        P(("shard", "dp"), None),
        P(("shard", "dp"), None),
        P(("shard", "dp"), None),
        P("shard", None),
        P("shard", None),
        P("shard", None),
        P("shard", None),
        P(None, "shard"),
        P("shard", None),
        P("shard", None),
        P("shard", None),
        P("shard", None),
        P(None, "shard"),
        P("shard", None),
        P("shard", None),
        P("shard", None),
        P("shard", None),
        P(None, "shard"),
    )
    return jax.shard_map(
        local,
        mesh=mesh,
        in_specs=placed,
        out_specs=(
            P(("shard", "dp"), None),
            P(("shard", "dp"), None),
            P("shard", None),
            P("shard", None),
            P("shard", None),
            P("shard", None),
            P(None, "shard"),
            P("shard", None),
            P("shard", None),
            P("shard", None),
            P("shard", None),
            P(None, "shard"),
            P("shard", None),
            P("shard", None),
            P("shard", None),
            P("shard", None),
            P(None, "shard"),
            P("shard", None),
            P("shard", None),
            P("shard", None),
            P("shard", None),
            P(None, "shard"),
        ),
        check_vma=False,
    )
```

profile of v0, /device:TPU:0, one launch (start us, length us, event | category | flops | bytes accessed | tf_op | source)
XLA Modules:
  0.0 1479.7 jit_solution(1329294678345296736)
XLA Ops:
  20.7 9.9 all_gather.75
  34.7 13.9 all-gather.23.cloned.1.call-done
  52.0 69.3 %all-gather.21.cloned.1.call-done = bf16[1024,3072]{1,0:T(8,128)(2,1)} async-done(((bf16[256,3072]{1,0:T(8,128)(2,1)}), bf16[1024,3072]{1,0:T(8,128)(2,1)}) %all-gather.21.cloned.1.call-update) | async-done | bytes 6291472 | tf_op jit(solution)/shard_map/all_gather | solution.py:215
  151.3 60.0 %all-gather.25.cloned.1.call-done = bf16[1024,4096]{1,0:T(8,128)(2,1)} async-done(((bf16[256,4096]{1,0:T(8,128)(2,1)}), bf16[1024,4096]{1,0:T(8,128)(2,1)}) %all-gather.25.cloned.1.call-update) | async-done | bytes 8388624 | tf_op jit(solution)/shard_map/all_gather | solution.py:217
  211.4 7.9 convolution_add_fusion
  219.2 82.1 %all-gather.27.cloned.1.call-done = bf16[4096,1024]{1,0:T(8,128)(2,1)} async-done(((bf16[1024,1024]{1,0:T(8,128)(2,1)}), bf16[4096,1024]{1,0:T(8,128)(2,1)}) %all-gather.27.cloned.1.call-update) | async-done | bytes 8388624 | tf_op jit(solution)/shard_map/all_gather | solution.py:218
  309.2 9.2 convolution_multiply_fusion.1
  318.4 11.6 convolution_multiply_fusion
  342.7 7.6 fusion.74
  355.8 106.7 %reduce-scatter.8.cloned.1.call-done = f32[32,3072]{1,0:T(8,128)} async-done(((f32[1024,3072]{1,0:T(8,128)}), f32[32,3072]{1,0:T(8,128)}) %reduce-scatter.8.cloned.1.call-update) | async-done | bytes 393232 | tf_op jit(solution)/shard_map/reduce_scatter | solution.py:227
  467.4 183.1 %reduce-scatter.12.cloned.1.call-done = f32[32,4096]{1,0:T(8,128)} async-done(((f32[1024,4096]{1,0:T(8,128)}), f32[32,4096]{1,0:T(8,128)}) %reduce-scatter.12.cloned.1.call-update) | async-done | bytes 524304 | tf_op jit(solution)/shard_map/reduce_scatter | solution.py:229
  654.0 183.4 %reduce-scatter.14.cloned.1.call-done = f32[128,1024]{1,0:T(8,128)} async-done(((f32[4096,1024]{1,0:T(8,128)}), f32[128,1024]{1,0:T(8,128)}) %reduce-scatter.14.cloned.1.call-update) | async-done | bytes 524304 | tf_op jit(solution)/shard_map/reduce_scatter | solution.py:230
  853.2 118.5 %reduce-scatter.16.cloned.1.call-done = f32[32,13]{1,0:T(8,128)} async-done(((f32[1024,13]{1,0:T(8,128)}), f32[32,13]{1,0:T(8,128)}) %reduce-scatter.16.cloned.1.call-update) | async-done | bytes 1680
  972.6 14.0 all-gather
  987.3 14.0 all-gather.1
  1002.0 14.0 all-gather.2
  1016.7 14.0 all-gather.3
  1031.4 82.5 %reduce-scatter.10.cloned.1.call-done = f32[32,1024]{1,0:T(8,128)} async-done(((f32[1024,1024]{1,0:T(8,128)}), f32[32,1024]{1,0:T(8,128)}) %reduce-scatter.10.cloned.1.call-update) | async-done | bytes 131088 | tf_op jit(solution)/shard_map/reduce_scatter | solution.py:228
  1115.2 16.8 %all_gather.81 = bf16[256,1024]{1,0:T(8,128)(2,1)S(1)} all-gather(bf16[32,1024]{1,0:T(8,128)(2,1)S(1)} %get-tuple-element.63), channel_id=1, replica_groups=mesh['shard'=4,'dp'=8] {'dp'}, dimensions={0}, use_global_device_ids=true | all-gather | bytes 589824 | tf_op jit(solution)/shard_map/all_gather | solution.py:297
  1133.1 15.5 %all_gather.86 = bf16[256,1024]{1,0:T(8,128)(2,1)S(1)} all-gather(bf16[32,1024]{1,0:T(8,128)(2,1)S(1)} %get-tuple-element.48), channel_id=1, replica_groups=mesh['shard'=4,'dp'=8] {'dp'}, dimensions={0}, use_global_device_ids=true | all-gather | bytes 589824 | tf_op jit(solution)/shard_map/all_gather | solution.py:252
  1149.7 16.7 %all_gather.91 = bf16[256,1024]{1,0:T(8,128)(2,1)S(1)} all-gather(bf16[32,1024]{1,0:T(8,128)(2,1)S(1)} %get-tuple-element.49), channel_id=1, replica_groups=mesh['shard'=4,'dp'=8] {'dp'}, dimensions={0}, use_global_device_ids=true | all-gather | bytes 589824 | tf_op jit(solution)/shard_map/all_gather | solution.py:267
  1167.5 14.9 %all_gather.96 = bf16[256,1024]{1,0:T(8,128)(2,1)S(1)} all-gather(bf16[32,1024]{1,0:T(8,128)(2,1)S(1)} %get-tuple-element.47), channel_id=1, replica_groups=mesh['shard'=4,'dp'=8] {'dp'}, dimensions={0}, use_global_device_ids=true | all-gather | bytes 589824 | tf_op jit(solution)/shard_map/all_gather | solution.py:282
  1190.3 7.9 all-gather.41.cloned.1.call-done
  1201.7 23.4 %all-gather.47.cloned.1.call-done = bf16[256,3072]{1,0:T(8,128)(2,1)} async-done(((bf16[32,3072]{1,0:T(8,128)(2,1)}), bf16[256,3072]{1,0:T(8,128)(2,1)}) %all-gather.47.cloned.1.call-update) | async-done | bytes 1572880 | tf_op jit(solution)/shard_map/all_gather | solution.py:279
  1228.5 27.3 %all-gather.31.cloned.1.call-done = bf16[256,4096]{1,0:T(8,128)(2,1)} async-done(((bf16[32,4096]{1,0:T(8,128)(2,1)}), bf16[256,4096]{1,0:T(8,128)(2,1)}) %all-gather.31.cloned.1.call-update) | async-done | bytes 2097168 | tf_op jit(solution)/shard_map/all_gather | solution.py:300
  1259.8 26.5 %all-gather.33.cloned.1.call-done = bf16[1024,1024]{1,0:T(8,128)(2,1)} async-done(((bf16[128,1024]{1,0:T(8,128)(2,1)}), bf16[1024,1024]{1,0:T(8,128)(2,1)}) %all-gather.33.cloned.1.call-update) | async-done | bytes 2097168 | tf_op jit(solution)/shard_map/all_gather | solution.py:303
  1290.5 26.6 %all-gather.37.cloned.1.call-done = bf16[256,4096]{1,0:T(8,128)(2,1)} async-done(((bf16[32,4096]{1,0:T(8,128)(2,1)}), bf16[256,4096]{1,0:T(8,128)(2,1)}) %all-gather.37.cloned.1.call-update) | async-done | bytes 2097168 | tf_op jit(solution)/shard_map/all_gather | solution.py:255
  1321.2 26.0 %all-gather.39.cloned.1.call-done = bf16[1024,1024]{1,0:T(8,128)(2,1)} async-done(((bf16[128,1024]{1,0:T(8,128)(2,1)}), bf16[1024,1024]{1,0:T(8,128)(2,1)}) %all-gather.39.cloned.1.call-update) | async-done | bytes 2097168 | tf_op jit(solution)/shard_map/all_gather | solution.py:258
  1351.2 26.6 %all-gather.43.cloned.1.call-done = bf16[256,4096]{1,0:T(8,128)(2,1)} async-done(((bf16[32,4096]{1,0:T(8,128)(2,1)}), bf16[256,4096]{1,0:T(8,128)(2,1)}) %all-gather.43.cloned.1.call-update) | async-done | bytes 2097168 | tf_op jit(solution)/shard_map/all_gather | solution.py:270
  1381.9 26.1 %all-gather.45.cloned.1.call-done = bf16[1024,1024]{1,0:T(8,128)(2,1)} async-done(((bf16[128,1024]{1,0:T(8,128)(2,1)}), bf16[1024,1024]{1,0:T(8,128)(2,1)}) %all-gather.45.cloned.1.call-update) | async-done | bytes 2097168 | tf_op jit(solution)/shard_map/all_gather | solution.py:273
  1412.1 26.0 %all-gather.49.cloned.1.call-done = bf16[256,4096]{1,0:T(8,128)(2,1)} async-done(((bf16[32,4096]{1,0:T(8,128)(2,1)}), bf16[256,4096]{1,0:T(8,128)(2,1)}) %all-gather.49.cloned.1.call-update) | async-done | bytes 2097168 | tf_op jit(solution)/shard_map/all_gather | solution.py:285
  1442.2 26.1 %all-gather.51.cloned.1.call-done = bf16[1024,1024]{1,0:T(8,128)(2,1)} async-done(((bf16[128,1024]{1,0:T(8,128)(2,1)}), bf16[1024,1024]{1,0:T(8,128)(2,1)}) %all-gather.51.cloned.1.call-update) | async-done | bytes 2097168 | tf_op jit(solution)/shard_map/all_gather | solution.py:288
  (200 shorter events, 156.1 us)
Async XLA Ops:
  7.2 41.5 %all-gather.23.cloned.1.call-start = ((), (), s32[]{:S(2)}) async-start(), calls=%async_computation.6 | async-start | bytes 2621440 | tf_op jit(solution)/shard_map/all_gather | solution.py:216
  9.4 111.9 %all-gather.21.cloned.1.call-start = ((), (), s32[]{:S(2)}) async-start(), calls=%async_computation.5 | async-start | bytes 7864320 | tf_op jit(solution)/shard_map/all_gather | solution.py:215
  12.7 198.7 %all-gather.25.cloned.1.call-start = ((), (), s32[]{:S(2)}) async-start(), calls=%async_computation.7 | async-start | bytes 10485760 | tf_op jit(solution)/shard_map/all_gather | solution.py:217
  16.6 14.1 copy-start.31
  16.6 15.6 %copy-start.1 = (bf16[256,1024]{1,0:T(8,128)(2,1)S(1)}, bf16[256,1024]{1,0:T(8,128)(2,1)}, u32[]{:S(2)}) copy-start(bf16[256,1024]{1,0:T(8,128)(2,1)} %param.18) | copy-start | bytes 1572868
  16.6 32.1 %copy-start.2 = (bf16[256,1024]{1,0:T(8,128)(2,1)S(1)}, bf16[256,1024]{1,0:T(8,128)(2,1)}, u32[]{:S(2)}) copy-start(bf16[256,1024]{1,0:T(8,128)(2,1)} %param.19) | copy-start | bytes 1572868
  16.6 284.7 %all-gather.27.cloned.1.call-start = ((), (), s32[]{:S(2)}) async-start(), calls=%async_computation.8 | async-start | bytes 10485760 | tf_op jit(solution)/shard_map/all_gather | solution.py:218
  20.6 441.9 %reduce-scatter.8.cloned.1.call-start = ((), (), s32[]{:S(2)}) async-start(), calls=%async_computation.9 | async-start | bytes 12976128 | tf_op jit(solution)/shard_map/reduce_scatter | solution.py:227
  32.1 93.9 %copy-start.23 = (f32[256]{0:T(256)}, f32[256]{0:T(256)S(1)}, u32[]{:S(2)}) copy-start(f32[256]{0:T(256)S(1)} %compare_convert_fusion) | copy-start | bytes 3076
  32.3 93.7 %copy-start.17 = (f32[256]{0:T(256)}, f32[256]{0:T(256)S(1)}, u32[]{:S(2)}) copy-start(f32[256]{0:T(256)S(1)} %broadcast_multiply_fusion.3) | copy-start | bytes 3076
  32.7 93.4 %copy-start.21 = (f32[256]{0:T(256)}, f32[256]{0:T(256)S(1)}, u32[]{:S(2)}) copy-start(f32[256]{0:T(256)S(1)} %add_rsqrt_fusion) | copy-start | bytes 3076
  150.6 500.0 %reduce-scatter.12.cloned.1.call-start = ((), (), s32[]{:S(2)}) async-start(), calls=%async_computation.12 | async-start | bytes 17301504 | tf_op jit(solution)/shard_map/reduce_scatter | solution.py:229
  211.4 89.9 %copy-start.24 = (f32[256]{0:T(256)S(1)}, f32[256]{0:T(256)}, u32[]{:S(2)}) copy-start(f32[256]{0:T(256)} %copy-done.23) | copy-start | bytes 3076
  318.4 519.0 %reduce-scatter.14.cloned.1.call-start = ((), (), s32[]{:S(2)}) async-start(), calls=%async_computation.14 | async-start | bytes 17301504 | tf_op jit(solution)/shard_map/reduce_scatter | solution.py:230
  330.1 641.6 %reduce-scatter.16.cloned.1.call-start = ((), (), s32[]{:S(2)}) async-start(), calls=%async_computation.25 | async-start | bytes 540672
  352.9 761.0 %reduce-scatter.10.cloned.1.call-start = ((), (), s32[]{:S(2)}) async-start(), calls=%async_computation.11 | async-start | bytes 4325376 | tf_op jit(solution)/shard_map/reduce_scatter | solution.py:228
  355.8 827.6 %all-gather.29.cloned.1.call-start = ((), (), s32[]{:S(2)}) async-start(), calls=%async_computation.10 | async-start | bytes 1769472 | tf_op jit(solution)/shard_map/all_gather | solution.py:294
  465.3 721.6 %all-gather.35.cloned.1.call-start = ((), (), s32[]{:S(2)}) async-start(), calls=%async_computation.16 | async-start | bytes 1769472 | tf_op jit(solution)/shard_map/all_gather | solution.py:249
  466.1 732.2 %all-gather.41.cloned.1.call-start = ((), (), s32[]{:S(2)}) async-start(), calls=%async_computation.19 | async-start | bytes 1769472 | tf_op jit(solution)/shard_map/all_gather | solution.py:264
  466.6 758.4 %all-gather.47.cloned.1.call-start = ((), (), s32[]{:S(2)}) async-start(), calls=%async_computation.22 | async-start | bytes 1769472 | tf_op jit(solution)/shard_map/all_gather | solution.py:279
  467.4 377.0 %copy-start.30 = (f32[1,1024]{1,0:T(1,128)S(1)}, f32[1,1024]{1,0:T(1,128)}, u32[]{:S(2)}) copy-start(f32[1,1024]{1,0:T(1,128)} %get-tuple-element.69) | copy-start | bytes 12292
  467.4 788.4 %all-gather.31.cloned.1.call-start = ((), (), s32[]{:S(2)}) async-start(), calls=%async_computation.13 | async-start | bytes 2359296 | tf_op jit(solution)/shard_map/all_gather | solution.py:300
  653.9 632.5 %all-gather.33.cloned.1.call-start = ((), (), s32[]{:S(2)}) async-start(), calls=%async_computation.15 | async-start | bytes 2359296 | tf_op jit(solution)/shard_map/all_gather | solution.py:303
  840.6 476.5 %all-gather.37.cloned.1.call-start = ((), (), s32[]{:S(2)}) async-start(), calls=%async_computation.17 | async-start | bytes 2359296 | tf_op jit(solution)/shard_map/all_gather | solution.py:255
  841.2 506.0 %all-gather.39.cloned.1.call-start = ((), (), s32[]{:S(2)}) async-start(), calls=%async_computation.18 | async-start | bytes 2359296 | tf_op jit(solution)/shard_map/all_gather | solution.py:258
  841.7 536.0 %all-gather.43.cloned.1.call-start = ((), (), s32[]{:S(2)}) async-start(), calls=%async_computation.20 | async-start | bytes 2359296 | tf_op jit(solution)/shard_map/all_gather | solution.py:270
  842.3 565.7 %all-gather.45.cloned.1.call-start = ((), (), s32[]{:S(2)}) async-start(), calls=%async_computation.21 | async-start | bytes 2359296 | tf_op jit(solution)/shard_map/all_gather | solution.py:273
  843.1 595.0 %all-gather.49.cloned.1.call-start = ((), (), s32[]{:S(2)}) async-start(), calls=%async_computation.23 | async-start | bytes 2359296 | tf_op jit(solution)/shard_map/all_gather | solution.py:285
  843.7 624.7 %all-gather.51.cloned.1.call-start = ((), (), s32[]{:S(2)}) async-start(), calls=%async_computation.24 | async-start | bytes 2359296 | tf_op jit(solution)/shard_map/all_gather | solution.py:288
  851.6 120.9 %copy-start.27 = (f32[13,256]{1,0:T(8,128)S(1)}, f32[13,256]{1,0:T(8,128)}, u32[]{:S(2)}) copy-start(f32[13,256]{1,0:T(8,128)} %param.25) | copy-start | bytes 39940
  851.6 120.9 %copy-start.28 = (f32[13,256]{1,0:T(8,128)S(1)}, f32[13,256]{1,0:T(8,128)}, u32[]{:S(2)}) copy-start(f32[13,256]{1,0:T(8,128)} %param.35) | copy-start | bytes 39940
  851.6 120.9 %copy-start.29 = (f32[13,256]{1,0:T(8,128)S(1)}, f32[13,256]{1,0:T(8,128)}, u32[]{:S(2)}) copy-start(f32[13,256]{1,0:T(8,128)} %param.30) | copy-start | bytes 39940
  (21 other events, 62.8 us)
Sparse Core Ops, SparseCore 0:
  10.4 38.1 all-gather.22
  51.1 70.1 all-gather.20
  123.7 87.5 all-gather.24
  213.6 87.5 all-gather.26
  307.2 155.3 reduce-scatter.7
  464.8 185.7 reduce-scatter.11
  653.0 184.3 reduce-scatter.13
  840.3 131.3 reduce-scatter.15
  974.5 139.3 reduce-scatter.9
  1115.9 24.1 all-gather.28
  1142.3 29.5 all-gather.34
  1174.0 24.1 all-gather.40
  1200.4 24.5 all-gather.46
  1227.1 28.6 all-gather.30
  1257.8 28.5 all-gather.32
  1288.4 28.5 all-gather.36
  1318.5 28.5 all-gather.38
  1349.2 28.5 all-gather.42
  1379.4 28.5 all-gather.44
  1409.5 28.5 all-gather.48
  1439.7 28.5 all-gather.50
where the time goes:
time: 1490 us; the launch traced here: 1480 us
  waiting for transfers between devices  1150 us (77%)
  blocking collectives  130 us (9%)
  matrix products  84.1 us (6%)
  other arithmetic  83.8 us (6%)
  local copies, waits for them, and re-layouts  17.8 us (1%)
  between operations  15.4 us (1%)
    reduce_scatter x1, waiting for transfers between devices, local(): lax.psum_scatter(scaled_grads[3], ('shard', 'dp'), scatter_dimension=0, t...  183 us
    reduce_scatter x1, waiting for transfers between devices, local(): lax.psum_scatter(scaled_grads[2], ('shard', 'dp'), scatter_dimension=0, t...  183 us
    unnamed x22, waiting for transfers between devices  124 us
    reduce_scatter x1, waiting for transfers between devices, local(): lax.psum_scatter(scaled_grads[0], ('shard', 'dp'), scatter_dimension=0, t...  107 us
    reduce_scatter x1, waiting for transfers between devices, local(): lax.psum_scatter(scaled_grads[1], ('shard', 'dp'), scatter_dimension=0, t...  82.5 us
    all_gather x1, waiting for transfers between devices, local(): lax.all_gather(w_down.astype(jnp.bfloat16), 'shard', axis=0, tiled=True)  82.1 us
    all_gather x1, waiting for transfers between devices, local(): lax.all_gather(w_qkv.astype(jnp.bfloat16), 'shard', axis=0, tiled=True)  69.3 us
    all_gather x1, waiting for transfers between devices, local(): lax.all_gather(w_up.astype(jnp.bfloat16), 'shard', axis=0, tiled=True)  60 us
  transfers between devices with their start and end apart: 21, of which 19 were waited for; matrix products, arithmetic and copies ran while one was open for 12% of the time, Pallas kernels for 0%

commit v1 on v0

v1 whole, which is shorter than its diff:
```python
import math

import jax
import jax.numpy as jnp
from jax import lax
from jax.sharding import PartitionSpec as P

H = 16
HD = 64
ROT = 16
ADAM_STEP = 4


EPS_NORM = 1e-05
BETA_ONE = 0.9
BETA_TWO = 0.95
ADAM_EPS = 1e-08
LEARN_RATE = 0.01
VECTOR_RATE = 0.1
DECAY_RATE = 0.1
SQRT_HALF = 0.7071067811865476
INV_ROOT_TWO_PI = 0.3989422804014327

BF = jnp.bfloat16
F32 = jnp.float32
EXTRA = 16


def matmul(left, right):
    return jnp.dot(left, right, preferred_element_type=F32)


def left_t(left, right):
    return lax.dot_general(left, right, (((0,), (0,)), ((), ())), preferred_element_type=F32)


def right_t(left, right):
    return lax.dot_general(left, right, (((1,), (1,)), ((), ())), preferred_element_type=F32)


def heads_mix(form, left, right):
    return jnp.einsum(form, left, right, preferred_element_type=F32)


def normalize(values):
    centred = values - jnp.mean(values, axis=-1, keepdims=True)
    inv_std = lax.rsqrt(jnp.mean(centred * centred, axis=-1, keepdims=True) + EPS_NORM)
    return (centred * inv_std, inv_std)


def rotate(values, cosine, sine):
    half_dims = ROT // 2
    first = values[..., :half_dims]
    second = values[..., half_dims:ROT]
    return jnp.concatenate(
        [first * cosine - second * sine, second * cosine + first * sine, values[..., ROT:]], axis=-1
    )


def gelu_parts(values):
    gate = 0.5 * (1.0 + lax.erf(values * SQRT_HALF))
    slope = gate + values * jnp.exp(-0.5 * values * values) * INV_ROOT_TWO_PI
    return values * gate, slope


def adam_update(weight, first, second, grad, decay, rate):
    count = jnp.float32(ADAM_STEP)
    first_new = BETA_ONE * first + (1.0 - BETA_ONE) * grad
    second_new = BETA_TWO * second + (1.0 - BETA_TWO) * grad * grad
    corr_one = 1.0 - jnp.exp(count * math.log(BETA_ONE))
    corr_two = 1.0 - jnp.exp(count * math.log(BETA_TWO))
    step_size = first_new / corr_one / (jnp.sqrt(second_new / corr_two) + ADAM_EPS)
    return (weight - rate * (step_size + decay * weight), first_new, second_new)


def shard_swap(value, step):
    size = lax.axis_size("shard")
    return lax.ppermute(value, "shard", [(i, i ^ step) for i in range(size)])


def core_swap(value):
    size = lax.axis_size("dp")
    return lax.ppermute(value, "dp", [(i, i ^ 1) for i in range(size)])


def chain_sum(value):
    places = lax.axis_size("dp") // 2
    if places == 1:
        return value
    place = lax.axis_index("dp") // 2
    half = places // 2

    def send(item, pairs):
        return lax.ppermute(
            item, "dp", [(2 * a + core, 2 * b + core) for a, b in pairs for core in range(2)]
        )

    total = value
    for step in range(half - 1):
        got = send(total, [(step, step + 1), (places - 1 - step, places - 2 - step)])
        total = total + got
    total = total + send(total, [(half - 1, half), (half, half - 1)])
    for step in reversed(range(half - 1)):
        got = send(total, [(step + 1, step), (places - 2 - step, places - 1 - step)])
        mine = (place == step) | (place == places - 1 - step)
        total = jnp.where(mine, got, total)
    return total


def local(
    tokens, cotangent, lengths,
    w_qkv, w_out, w_up, w_down, vectors,
    m_qkv, m_out, m_up, m_down, m_vectors,
    v_qkv, v_out, v_up, v_down, v_vectors,
):
    groups = lax.axis_size("shard")
    me = lax.axis_index("shard")
    core = lax.axis_index("dp") % 2
    rows, width = tokens.shape
    hidden = w_up.shape[1]
    wide = width // groups
    half = wide // 2
    ff = hidden // groups
    heads = H // groups
    n_vec = vectors.shape[0]
    others = range(1, groups)

    def piece(matrix, parts, owner, first, count):
        block = lax.dynamic_slice_in_dim(matrix, first, count, 0)
        block = block.reshape(count, parts, groups, -1)
        block = lax.dynamic_slice_in_dim(block, owner, 1, 2)
        return block.reshape(count, -1).astype(BF)

    small = jnp.concatenate(
        [vectors.astype(BF), jnp.pad(lengths.astype(BF), ((0, 0), (0, wide - lengths.shape[1])))]
    )
    small = jnp.pad(small, ((0, EXTRA - n_vec - 1), (0, 3 * wide + ff - wide)))

    def payload(step):
        owner = me ^ step
        both = jnp.concatenate(
            [piece(w_qkv, 3, owner, core * half, half), piece(w_up, 1, owner, core * half, half)], axis=1
        )
        return jnp.concatenate([both, small])

    got_w = [shard_swap(payload(step), step) for step in others]
    got_x = [tokens] + [shard_swap(tokens, step) for step in others]
    got_c = [cotangent] + [shard_swap(cotangent, step) for step in others]
    stacked = jnp.stack([item[:half] for item in got_w])
    other_half = core_swap(stacked)
    own_rows = jnp.concatenate([piece(w_qkv, 3, me, 0, wide), piece(w_up, 1, me, 0, wide)], axis=1)
    full = jnp.zeros((groups, 2, half, 3 * wide + ff), BF)
    full = lax.dynamic_update_slice(full, own_rows.reshape(1, 2, half, -1), (me, 0, 0, 0))
    for step in others:
        at = me ^ step
        full = lax.dynamic_update_slice(full, stacked[step - 1][None, None], (at, core, 0, 0))
        full = lax.dynamic_update_slice(full, other_half[step - 1][None, None], (at, 1 - core, 0, 0))
    full = full.reshape(width, 3 * wide + ff)
    qkv_w = full[:, : 3 * wide]
    up_w = full[:, 3 * wide :]
    out_w = w_out.astype(BF)
    down_w = w_down.astype(BF)

    smalls = [small[:, :wide]] + [item[half:, :wide] for item in got_w]
    vec = jnp.zeros((n_vec, groups, wide), BF)
    counts = []
    for step in range(groups):
        vec = lax.dynamic_update_slice(vec, smalls[step][:n_vec, None], (0, me ^ step, 0))
        counts.append(smalls[step][n_vec, : lengths.shape[1]].astype(jnp.int32))
    vec = vec.reshape(n_vec, width).astype(F32)
    counts = jnp.stack(counts)

    index_rows = jnp.arange(rows, dtype=jnp.int32)
    ends = jnp.cumsum(counts, axis=1)
    passed = ends[:, None, :] <= index_rows[None, :, None]
    segment = jnp.sum(passed.astype(jnp.int32), axis=2)
    starts = jnp.sum(jnp.where(passed, counts[:, None, :], 0), axis=2)
    position = index_rows[None] - starts
    valid = (index_rows[None] < ends[:, -1:]).astype(F32)
    allowed = (segment[:, :, None] == segment[:, None, :]) & (
        index_rows[None, None, :] <= index_rows[None, :, None]
    )

    x_all = jnp.concatenate(got_x).astype(F32)
    normed, inv_std = normalize(x_all)
    in_attn = (normed * vec[0] + vec[1]).astype(BF)
    in_mlp = (normed * vec[2] + vec[3]).astype(BF)
    cot_all = jnp.concatenate(got_c).astype(F32)
    branch_b = (cot_all * valid.reshape(-1, 1)).astype(BF)

    qkv_bias = lax.dynamic_slice_in_dim(vec[6:9].reshape(3, groups, wide), me, 1, 1).reshape(-1)
    up_bias = lax.dynamic_slice_in_dim(vec[9:].reshape(-1), me * ff, ff)

    up_pre = matmul(in_mlp, up_w) + up_bias
    act, slope = gelu_parts(up_pre)
    act_b = act.astype(BF)
    d_up = right_t(branch_b, down_w) * slope
    d_up_b = d_up.astype(BF)
    token_total = rows * groups * lax.axis_size("dp")
    grad_scale = float(token_total) ** (-0.5)
    grad_down = (left_t(act_b, branch_b) * grad_scale).astype(BF)
    grad_up = (left_t(in_mlp, d_up_b) * grad_scale).astype(BF)
    bias_up = jnp.sum(d_up, axis=0)
    d_mlp_in = right_t(d_up_b, up_w)
    mlp = matmul(act_b, down_w)

    scale = HD ** (-0.5)
    projected = (matmul(in_attn, qkv_w) + qkv_bias).reshape(groups, rows, 3, heads, HD)
    half_dims = ROT // 2
    freq = jnp.exp(-jnp.arange(half_dims, dtype=F32) * (2.0 * math.log(10000.0) / ROT))
    angles = position.astype(F32)[:, :, None, None] * freq
    cosine, sine = jnp.cos(angles), jnp.sin(angles)
    query_b = rotate(projected[:, :, 0], cosine, sine).astype(BF)
    key_b = rotate(projected[:, :, 1], cosine, sine).astype(BF)
    value_b = projected[:, :, 2].astype(BF)
    scores = heads_mix("bqhd,bkhd->bhqk", query_b, key_b) * scale
    scores = jnp.where(allowed[:, None], scores, -1e30)
    top_score = jnp.max(scores, axis=-1, keepdims=True)
    log_total = top_score + jnp.log(jnp.sum(jnp.exp(scores - top_score), axis=-1, keepdims=True))
    probs = jnp.exp(scores - log_total)
    probs_b = probs.astype(BF)
    heads_b = heads_mix("bhqk,bkhd->bqhd", probs_b, value_b).astype(BF).reshape(groups * rows, wide)
    attn = matmul(heads_b, out_w)
    grad_out = (left_t(heads_b, branch_b) * grad_scale).astype(BF)
    d_heads = right_t(branch_b, out_w).astype(BF).reshape(groups, rows, heads, HD)
    d_probs = heads_mix("bqhd,bkhd->bhqk", d_heads, value_b)
    delta = jnp.sum(probs * d_probs, axis=-1, keepdims=True)
    d_scores = (probs * (d_probs - delta)).astype(BF)
    d_query = heads_mix("bhqk,bkhd->bqhd", d_scores, key_b) * scale
    d_key = heads_mix("bhqk,bqhd->bkhd", d_scores, query_b) * scale
    d_value = heads_mix("bhqk,bqhd->bkhd", probs_b, d_heads)
    d_proj = jnp.stack([rotate(d_query, cosine, -sine), rotate(d_key, cosine, -sine), d_value], axis=2)
    d_proj = d_proj.reshape(groups * rows, 3 * wide)
    bias_qkv = jnp.sum(d_proj, axis=0)
    d_proj_b = d_proj.astype(BF)
    grad_qkv = (left_t(in_attn, d_proj_b) * grad_scale).astype(BF)
    d_attn_in = right_t(d_proj_b, qkv_w)

    branch_out = attn + mlp
    scaled = d_attn_in * vec[0] + d_mlp_in * vec[2]

    def owners_sum(value):
        value = value.reshape(groups, rows, width)
        total = value[0]
        for step in others:
            total = total + shard_swap(value[step].astype(BF), step).astype(F32)
        return total

    branch_sum = owners_sum(branch_out) + vec[4] + vec[5]
    output = (tokens.astype(F32) + valid[0][:, None] * branch_sum).astype(BF)
    scaled_sum = owners_sum(scaled)
    own_normed, own_inv = normed[:rows], inv_std[:rows]
    d_tokens = own_inv * (
        scaled_sum
        - jnp.mean(scaled_sum, axis=-1, keepdims=True)
        - own_normed * jnp.mean(scaled_sum * own_normed, axis=-1, keepdims=True)
    )
    cot_float = cotangent.astype(F32)
    input_grad = (cot_float + d_tokens).astype(BF)

    bias_out = jnp.sum(cot_float * valid[0][:, None], axis=0)
    row_qkv = lax.dynamic_update_slice(
        jnp.zeros((3, groups, wide), F32), bias_qkv.reshape(3, 1, wide), (0, me, 0)
    ).reshape(3, width)
    row_up = lax.dynamic_update_slice(jnp.zeros((hidden,), F32), bias_up, (me * ff,)).reshape(-1, width)
    vec_grad = jnp.concatenate(
        [
            jnp.sum(d_attn_in * normed, axis=0)[None],
            jnp.sum(d_attn_in, axis=0)[None],
            jnp.sum(d_mlp_in * normed, axis=0)[None],
            jnp.sum(d_mlp_in, axis=0)[None],
            bias_out[None],
            bias_out[None],
            row_qkv,
            row_up,
        ]
    )
    vec_grad = jnp.pad((vec_grad * grad_scale).astype(BF), ((0, EXTRA - n_vec), (0, 0)))
    vec_grad = vec_grad.reshape(2, EXTRA // 2, groups, wide).transpose(2, 0, 1, 3)
    vec_grad = jnp.pad(vec_grad, ((0, 0), (0, 0), (0, EXTRA // 2), (0, 2 * wide)))

    def core_sum(value, axis):
        keep = lax.dynamic_index_in_dim(value, core, axis, keepdims=False)
        away = lax.dynamic_index_in_dim(value, 1 - core, axis, keepdims=False)
        return keep + core_swap(away)

    def core_join(value, axis):
        other = core_swap(value)
        return jnp.where(
            core == 0, jnp.stack([value, other], axis=axis), jnp.stack([other, value], axis=axis)
        )

    def to_owners(value):
        pieces = [lax.dynamic_index_in_dim(value, me, 0, keepdims=False)]
        for step in others:
            pieces.append(
                shard_swap(lax.dynamic_index_in_dim(value, me ^ step, 0, keepdims=False), step)
            )
        return jnp.stack(pieces)

    def natural(value):
        result = jnp.zeros(value.shape, value.dtype)
        for step in range(groups):
            result = lax.dynamic_update_slice_in_dim(result, value[step : step + 1], me ^ step, 0)
        return result

    sum_down = core_join(chain_sum(core_sum(grad_down.reshape(2, ff // 2, width), 0)), 0)
    sum_up = to_owners(core_sum(grad_up.reshape(groups, 2, half, ff), 1))
    sum_up = core_join(chain_sum(sum_up), 1)
    sum_out = core_join(chain_sum(core_sum(grad_out.reshape(2, half, width), 0)), 0)
    grad_qkv = jnp.concatenate([grad_qkv.reshape(groups, 2, half, 3 * wide), vec_grad], axis=2)
    sum_qkv = to_owners(core_sum(grad_qkv, 1))
    sum_qkv = core_join(chain_sum(sum_qkv), 1)
    sum_vec = jnp.sum(sum_qkv[:, :, half : half + EXTRA // 2, :wide].astype(F32), axis=0)
    sum_vec = sum_vec.reshape(EXTRA, wide)[:n_vec]

    full_grads = (
        natural(sum_qkv[:, :, :half])
        .reshape(groups, wide, 3, wide)
        .transpose(1, 2, 0, 3)
        .reshape(wide, 3 * width)
        .astype(F32),
        sum_out.reshape(wide, width).astype(F32),
        natural(sum_up).reshape(groups, wide, ff).transpose(1, 0, 2).reshape(wide, hidden).astype(F32),
        sum_down.reshape(ff, width).astype(F32),
        sum_vec,
    )
    masters = (w_qkv, w_out, w_up, w_down, vectors)
    firsts = (m_qkv, m_out, m_up, m_down, m_vectors)
    seconds = (v_qkv, v_out, v_up, v_down, v_vectors)
    decays = (DECAY_RATE, DECAY_RATE, DECAY_RATE, DECAY_RATE, 0.0)
    rates = (LEARN_RATE, LEARN_RATE, LEARN_RATE, LEARN_RATE, VECTOR_RATE)
    results = [
        adam_update(masters[i], firsts[i], seconds[i], full_grads[i], decays[i], rates[i]) for i in range(5)
    ]
    return (
        (output, input_grad)
        + full_grads
        + tuple(r[0] for r in results)
        + tuple(r[1] for r in results)
        + tuple(r[2] for r in results)
    )


def solution(mesh):
    by_token = P(("shard", "dp"), None)
    params = (P("shard", None),) * 4 + (P(None, "shard"),)
    return jax.shard_map(
        local,
        mesh=mesh,
        in_specs=(by_token,) * 3 + params * 3,
        out_specs=(by_token,) * 2 + params * 4,
        check_vma=False,
    )
```

time: 1490 us -> 510 us (0.34)
  waiting for transfers between devices: 1150 us -> 166 us
  blocking collectives: 130 us -> 0 us
  local copies, waits for them, and re-layouts: 17.8 us -> 146 us
  starting transfers between devices: 1.31 us -> 52.6 us
  matrix products: 84.1 us -> 61.5 us
    reduce_scatter x4 -> x0, waiting for transfers between devices: 556 us -> none  [the longest x1 183 us: local(): lax.psum_scatter(scaled_grads[3], ('shard', 'dp'), scatter_dimension=0, t...]
    all_gather x16 -> x0, waiting for transfers between devices: 468 us -> none  [the longest x1 82.1 us: local(): lax.all_gather(w_down.astype(jnp.bfloat16), 'shard', axis=0, tiled=True)]
    ppermute x0 -> x42, waiting for transfers between devices: none -> 166 us  [the longest x12 112 us: send(): lax.ppermute(item, 'dp', [(2 * a + core, 2 * b + core) for a, b in pairs...]
    all_gather x9 -> x0, blocking collectives: 130 us -> none  [the longest x1 16.8 us: local(): lax.all_gather(pieces[1].astype(jnp.bfloat16), 'dp', axis=0, tiled=True)]
    unnamed x22 -> x0, waiting for transfers between devices: 124 us -> none
    convert_element_type x33 -> x8, other arithmetic: 76.3 us -> 5.71 us  [the longest x1 2.62 us: local(): natural(sum_up).reshape(groups, wide, ff).transpose(1, 0, 2)]
    unnamed x68 -> x96, local copies, waits for them, and re-layouts: 6.61 us -> 70.5 us
    ppermute x0 -> x42, starting transfers between devices: none -> 52.6 us  [the longest x21 26.4 us: shard_swap(): return lax.ppermute(value, 'shard', [(i, i ^ step) for i in range(size)])]
  transfers between devices with their start and end apart: 21 -> 42, of which waited for: 19 -> 20; matrix products, arithmetic and copies ran while one was open for 12% -> 32% of each run, Pallas kernels for 0% -> 0%
where the time goes in v1:
time: 510 us; the launch traced here: 503 us
  waiting for transfers between devices  166 us (33%)
  local copies, waits for them, and re-layouts  146 us (29%)
  other arithmetic  74.2 us (15%)
  matrix products  61.5 us (12%)
  starting transfers between devices  52.6 us (10%)
    ppermute x12, waiting for transfers between devices, send(): lax.ppermute(item, 'dp', [(2 * a + core, 2 * b + core) for a, b in pairs...  112 us
    unnamed x96, local copies, waits for them, and re-layouts  70.5 us
    ppermute x21, waiting for transfers between devices, shard_swap(): return lax.ppermute(value, 'shard', [(i, i ^ step) for i in range(size)])  53.3 us
    sub x5, other arithmetic, adam_update(): return (weight - rate * (step_size + decay * weight), first_new, second_new)  30.5 us
    ppermute x21, starting transfers between devices, shard_swap(): return lax.ppermute(value, 'shard', [(i, i ^ step) for i in range(size)])  26.4 us
    ppermute x12, starting transfers between devices, send(): lax.ppermute(item, 'dp', [(2 * a + core, 2 * b + core) for a, b in pairs...  25.3 us
    dot_general x4, matrix products, right_t(): lax.dot_general(left, right, (((1,), (1,)), ((), ())), preferred_element_...  22.4 us
    dot_general x4, matrix products, left_t(): lax.dot_general(left, right, (((0,), (0,)), ((), ())), preferred_element_...  16.5 us
  transfers between devices with their start and end apart: 42, of which 20 were waited for; matrix products, arithmetic and copies ran while one was open for 32% of the time, Pallas kernels for 0%

profile of v1, /device:TPU:0, one launch (start us, length us, event | category | flops | bytes accessed | tf_op | source)
XLA Modules:
  0.0 503.0 jit_solution(7013269891564873148)
XLA Ops:
  6.7 5.6 %copy.301 = f32[256,4096]{0,1:T(8,128)} copy(f32[256,4096]{1,0:T(8,128)} %param.23) | data formatting | bytes 8388608 | tf_op args[5]
  43.9 7.0 %collective-permute-done = bf16[144,1792]{1,0:T(8,128)(2,1)} collective-permute-done((bf16[144,1792]{1,0:T(8,128)(2,1)}, bf16[144,1792]{1,0:T(8,128)(2,1)}, u32[]{:S(2)}, u32[]{:S(2)}) %collective-permute-start) | collective-permute-done | bytes 516128 | tf_op jit(solution)/shard_map/ppermute | solution.py:78
  67.6 8.0 %collective-permute-done.11 = bf16[256,1024]{1,0:T(8,128)(2,1)} collective-permute-done((bf16[256,1024]{1,0:T(8,128)(2,1)}, bf16[256,1024]{1,0:T(8,128)(2,1)}, u32[]{:S(2)}, u32[]{:S(2)}) %collective-permute-start.11) | collective-permute-done | bytes 524320 | tf_op jit(solution)/shard_map/ppermute | solution.py:78
  80.6 5.2 %collective-permute-done.3 = bf16[256,1024]{1,0:T(8,128)(2,1)S(1)} collective-permute-done((bf16[256,1024]{1,0:T(8,128)(2,1)S(1)}, bf16[256,1024]{1,0:T(8,128)(2,1)S(1)}, u32[]{:S(2)}, u32[]{:S(2)}) %collective-permute-start.3) | collective-permute-done | bytes 524320 | tf_op jit(solution)/shard_map/ppermute | solution.py:78
  98.0 5.5 %convolution_add_fusion.1 = f32[1024,768]{1,0:T(8,128)} fusion(f32[768]{0:T(1024)S(1)} %add.352, bf16[1024,1792]{1,0:T(8,128)(2,1)} %bitcast.24, f32[1024]{0:T(1024)S(1)} %bitcast.295, f32[1024]{0:T(1024)S(1)} %bitcast.297, f32[1024]{0:T(1024)S(1)} %add_rsqrt_fusion, f32[1024]{0:T(1024)S(1)} %broadcast_multiply_fusion, ...), kind=kOutput, calls=%fused_computation.60 | convolution fusion | flops 1625030656 | bytes 6835200 | tf_op jit(solution)/shard_map/dot_general | solution.py:30
  103.5 6.3 %reshape.348 = f32[4,256,3,4,64]{4,3,2,1,0:T(4,128)} reshape(f32[1024,768]{1,0:T(8,128)} %convolution_add_fusion.1) | data formatting | bytes 6291456 | tf_op jit(solution)/shard_map/reshape | solution.py:208
  142.4 5.2 %multiply_convert_fusion.4 = (bf16[1024,1024]{1,0:T(8,128)(2,1)S(1)}, f32[1024,1024]{1,0:T(8,128)S(1)}) fusion(f32[1024]{0:T(1024)S(1)} %dynamic_slice.105, bf16[1024,1792]{1,0:T(8,128)(2,1)} %bitcast.24, f32[1024]{0:T(1024)S(1)} %bitcast.300, f32[1024]{0:T(1024)S(1)} %bitcast.292, f32[1024]{0:T(1024)S(1)} %add_rsqrt_fusion, ...), kind=kOutput, calls=%fused_computation.29 | convolution fusion | flops 2167406592 | bytes 10506240 | tf_op jit(solution)/shard_map/dot_general | solution.py:30
  147.7 6.9 %fusion.94 = (f32[1024]{0:T(1024)S(1)}, bf16[1024,1024]{1,0:T(8,128)(2,1)S(1)}) fusion(f32[1024,1024]{1,0:T(8,128)S(1)} %get-tuple-element.226, f32[1024]{0:T(1024)S(1)} %dynamic_slice.105, f32[1024,1024]{1,0:T(8,128)S(1)} %copy-done.4, bf16[256,1024]{1,0:T(8,128)(2,1)} %collective-permute-done.12, bf16[256,1024]{1,0:T(8,128)(2,1)} %collective-permute-done.11, ...), kind=kOutput, calls=%fused_computation.242 | convolution fusion | flops 2171599872 | bytes 12595200 | tf_op jit(solution)/shard_map/dot_general | solution.py:38
  154.6 9.4 %fusion.79 = (f32[1024]{0:T(1024)S(1)}, f32[1024]{0:T(1024)S(1)}, bf16[1024,1024]{1,0:T(8,128)(2,1)S(1)}, f32[1024,1024]{1,0:T(8,128)}, f32[1024]{0:T(1024)S(1)}, /*index=5*/f32[1024]{0:T(1024)S(1)}, f32[1024,1024]{1,0:T(8,128)}) fusion(f32[1024]{0:T(1024)S(1)} %add_rsqrt_fusion, f32[1024]{0:T(1024)S(1)} %broadcast_multiply_fusion, ...), kind=kOutput, calls=%fused_computation.233 | convolution fusion | flops 2168451072 | bytes 21004288 | tf_op jit(solution)/shard_map/dot_general | solution.py:38
  178.3 4.7 multiply_convert_fusion.1
  185.4 4.8 multiply_convert_fusion.5
  194.6 9.1 %collective-permute-done.9 = bf16[256,1024]{1,0:T(8,128)(2,1)} collective-permute-done((bf16[256,1024]{1,0:T(8,128)(2,1)}, bf16[256,1024]{1,0:T(8,128)(2,1)}, u32[]{:S(2)}, u32[]{:S(2)}) %collective-permute-start.9) | collective-permute-done | bytes 524320 | tf_op jit(solution)/shard_map/ppermute | solution.py:78
  203.7 7.6 %collective-permute-done.8 = bf16[256,1024]{1,0:T(8,128)(2,1)} collective-permute-done((bf16[256,1024]{1,0:T(8,128)(2,1)}, bf16[256,1024]{1,0:T(8,128)(2,1)}, u32[]{:S(2)}, u32[]{:S(2)}) %collective-permute-start.8) | collective-permute-done | bytes 524320 | tf_op jit(solution)/shard_map/ppermute | solution.py:78
  216.6 4.7 multiply_convert_fusion
  252.8 7.6 %collective-permute-done.20 = bf16[4,144,768]{2,1,0:T(8,128)(2,1)S(1)} collective-permute-done((bf16[4,144,768]{2,1,0:T(8,128)(2,1)S(1)}, bf16[4,144,768]{2,1,0:T(8,128)(2,1)S(1)}, u32[]{:S(2)}, u32[]{:S(2)}) %collective-permute-start.20) | collective-permute-done | bytes 884768 | tf_op jit(solution)/shard_map/ppermute | solution.py:94
  261.4 7.2 %collective-permute-start.25 = (bf16[128,1024]{1,0:T(8,128)(2,1)S(1)}, bf16[128,1024]{1,0:T(8,128)(2,1)S(1)}, u32[]{:S(2)}, u32[]{:S(2)}) collective-permute-start(bf16[128,1024]{1,0:T(8,128)(2,1)S(1)} %bitcast_add_fusion.3), channel_id=1, source_target_pairs={{0,2},{1,3},{6,4},{7,5},{8,10},{9,11},{14,12},{15,13},{16,18},{17,... | collective-permute-start | bytes 786440 | tf_op jit(solution)/shard_map/ppermute | solution.py:94
  268.6 14.4 %collective-permute-done.38 = bf16[512,1024]{1,0:T(8,128)(2,1)S(1)} collective-permute-done((bf16[512,1024]{1,0:T(8,128)(2,1)S(1)}, bf16[512,1024]{1,0:T(8,128)(2,1)S(1)}, u32[]{:S(2)}, u32[]{:S(2)}) %collective-permute-start.38) | collective-permute-done | bytes 1048608 | tf_op jit(solution)/shard_map/ppermute | solution.py:94
  285.0 20.4 %collective-permute-done.33 = bf16[4,128,1024]{2,1,0:T(8,128)(2,1)S(1)} collective-permute-done((bf16[4,128,1024]{2,1,0:T(8,128)(2,1)S(1)}, bf16[4,128,1024]{2,1,0:T(8,128)(2,1)S(1)}, u32[]{:S(2)}, u32[]{:S(2)}) %collective-permute-start.33) | collective-permute-done | bytes 1048608 | tf_op jit(solution)/shard_map/ppermute | solution.py:94
  321.9 5.7 %copy.342 = f32[256,4096]{0,1:T(8,128)} copy(f32[256,4096]{1,0:T(8,128)} %param.28) | data formatting | bytes 8388608 | tf_op args[10]
  327.6 5.6 %copy.343 = f32[256,4096]{0,1:T(8,128)} copy(f32[256,4096]{1,0:T(8,128)} %param.33) | data formatting | bytes 8388608 | tf_op args[15]
  333.2 15.3 %collective-permute-done.27 = bf16[128,1024]{1,0:T(8,128)(2,1)} collective-permute-done((bf16[128,1024]{1,0:T(8,128)(2,1)}, bf16[128,1024]{1,0:T(8,128)(2,1)}, u32[]{:S(2)}, u32[]{:S(2)}) %collective-permute-start.27) | collective-permute-done | bytes 262176 | tf_op jit(solution)/shard_map/ppermute | solution.py:94
  355.6 7.7 %collective-permute-done.22 = bf16[4,144,768]{2,1,0:T(8,128)(2,1)} collective-permute-done((bf16[4,144,768]{2,1,0:T(8,128)(2,1)}, bf16[4,144,768]{2,1,0:T(8,128)(2,1)}, u32[]{:S(2)}, u32[]{:S(2)}) %collective-permute-start.22) | collective-permute-done | bytes 884768 | tf_op jit(solution)/shard_map/ppermute | solution.py:94
  367.1 24.5 %collective-permute-done.40 = bf16[512,1024]{1,0:T(8,128)(2,1)S(1)} collective-permute-done((bf16[512,1024]{1,0:T(8,128)(2,1)S(1)}, bf16[512,1024]{1,0:T(8,128)(2,1)S(1)}, u32[]{:S(2)}, u32[]{:S(2)}) %collective-permute-start.40) | collective-permute-done | bytes 1048608 | tf_op jit(solution)/shard_map/ppermute | solution.py:94
  392.6 21.2 %collective-permute-done.35 = bf16[4,128,1024]{2,1,0:T(8,128)(2,1)S(1)} collective-permute-done((bf16[4,128,1024]{2,1,0:T(8,128)(2,1)S(1)}, bf16[4,128,1024]{2,1,0:T(8,128)(2,1)S(1)}, u32[]{:S(2)}, u32[]{:S(2)}) %collective-permute-start.35) | collective-permute-done | bytes 1048608 | tf_op jit(solution)/shard_map/ppermute | solution.py:94
  427.8 6.9 %multiply_subtract_fusion.2 = (f32[256,3072]{0,1:T(8,128)}, f32[256,3072]{0,1:T(8,128)}, f32[256,3072]{0,1:T(8,128)}) fusion(f32[256,3072]{0,1:T(8,128)} %copy-done, f32[256,3,4,256]{0,3,2,1:T(8,128)S(1)} %copy.332, f32[256,3072]{0,1:T(8,128)} %copy.338, f32[256,3072]{0,1:T(8,128)} %copy.339), kind=kLoop, calls=%fused_computation.41 | loop fusion | flops 11796480 | bytes 22020096 | tf_op jit(solution)/shard_map/sub | solution.py:73
  448.4 9.0 %multiply_subtract_fusion = (f32[1024,1024]{1,0:T(8,128)}, f32[1024,1024]{1,0:T(8,128)}, f32[1024,1024]{1,0:T(8,128)}, f32[1024,1024]{1,0:T(8,128)}) fusion(f32[1024,1024]{1,0:T(8,128)S(1)} %copy-done.5, f32[1024,1024]{1,0:T(8,128)} %param.29, f32[1024,1024]{1,0:T(8,128)} %param.34, bf16[2,512,1024]{2,1,0:T(8,128)(2,1)S(1)} %maximum_select_fusion.1), kind=kLoop, calls=%fused_computation.17 | loop fusion | flops 16777216 | bytes 31457280 | tf_op jit(solution)/shard_map/sub | solution.py:73
  463.1 5.4 %copy.337 = f32[256,4,1024]{0,2,1:T(8,128)} copy(f32[256,4,1024]{2,0,1:T(8,128)} %convert_bitcast_fusion) | data formatting | bytes 8388608 | tf_op jit(solution)/shard_map/convert_element_type | solution.py:324
  468.4 5.6 %copy.347 = f32[256,4096]{1,0:T(8,128)} copy(f32[256,4096]{0,1:T(8,128)} %bitcast.220) | data formatting | bytes 8388608
  474.0 11.7 %multiply_subtract_fusion.1 = (f32[256,4096]{0,1:T(8,128)}, f32[256,4096]{0,1:T(8,128)}, f32[256,4096]{0,1:T(8,128)}) fusion(f32[256,4096]{0,1:T(8,128)} %copy.301, f32[256,4,1024]{0,2,1:T(8,128)} %copy.337, f32[256,4096]{0,1:T(8,128)} %copy.342, f32[256,4096]{0,1:T(8,128)} %copy.343), kind=kLoop, calls=%fused_computation.19 | loop fusion | flops 15728640 | bytes 29360128 | tf_op jit(solution)/shard_map/sub | solution.py:73
  485.7 5.6 %copy.349 = f32[256,4096]{1,0:T(8,128)} copy(f32[256,4096]{0,1:T(8,128)} %get-tuple-element.148) | data formatting | bytes 8388608
  491.3 5.6 %copy.351 = f32[256,4096]{1,0:T(8,128)} copy(f32[256,4096]{0,1:T(8,128)} %get-tuple-element.149) | data formatting | bytes 8388608
  496.9 5.6 %copy.353 = f32[256,4096]{1,0:T(8,128)} copy(f32[256,4096]{0,1:T(8,128)} %get-tuple-element.150) | data formatting | bytes 8388608
  (323 shorter events, 225.9 us)
Async XLA Ops:
  0.7 79.9 %collective-permute-start.5 = (bf16[256,1024]{1,0:T(8,128)(2,1)}, bf16[256,1024]{1,0:T(8,128)(2,1)}, u32[]{:S(2)}, u32[]{:S(2)}) collective-permute-start(bf16[256,1024]{1,0:T(8,128)(2,1)} %param.18), channel_id=1, source_target_pairs={{0,24},{8,16},{16,8},{24,0},{1,25},{9,17},{17,9},{25,1},{2,26},{10... | collective-permute-start | bytes 1572872 | tf_op jit(solution)/shard_map/ppermute | solution.py:78
  4.6 76.0 %collective-permute-start.4 = (bf16[256,1024]{1,0:T(8,128)(2,1)}, bf16[256,1024]{1,0:T(8,128)(2,1)}, u32[]{:S(2)}, u32[]{:S(2)}) collective-permute-start(bf16[256,1024]{1,0:T(8,128)(2,1)} %param.18), channel_id=1, source_target_pairs={{0,16},{8,24},{16,0},{24,8},{1,17},{9,25},{17,1},{25,9},{2,18},{10... | collective-permute-start | bytes 1572872 | tf_op jit(solution)/shard_map/ppermute | solution.py:78
  25.7 28.8 %collective-permute-start.2 = (bf16[144,1792]{1,0:T(8,128)(2,1)}, bf16[144,1792]{1,0:T(8,128)(2,1)S(1)}, u32[]{:S(2)}, u32[]{:S(2)}) collective-permute-start(bf16[144,1792]{1,0:T(8,128)(2,1)} %copy.305), channel_id=1, source_target_pairs={{0,24},{8,16},{16,8},{24,0},{1,25},{9,17},{17,9},{25,1},{2,26},{10... | collective-permute-start | bytes 1548296 | tf_op jit(solution)/shard_map/ppermute | solution.py:78
  29.4 22.7 %collective-permute-start.1 = (bf16[144,1792]{1,0:T(8,128)(2,1)}, bf16[144,1792]{1,0:T(8,128)(2,1)}, u32[]{:S(2)}, u32[]{:S(2)}) collective-permute-start(bf16[144,1792]{1,0:T(8,128)(2,1)} %copy.304), channel_id=1, source_target_pairs={{0,16},{8,24},{16,0},{24,8},{1,17},{9,25},{17,1},{25,9},{2,18},{10... | collective-permute-start | bytes 1548296 | tf_op jit(solution)/shard_map/ppermute | solution.py:78
  31.7 19.2 %collective-permute-start = (bf16[144,1792]{1,0:T(8,128)(2,1)}, bf16[144,1792]{1,0:T(8,128)(2,1)}, u32[]{:S(2)}, u32[]{:S(2)}) collective-permute-start(bf16[144,1792]{1,0:T(8,128)(2,1)} %copy.303), channel_id=1, source_target_pairs={{0,8},{8,0},{16,24},{24,16},{1,9},{9,1},{17,25},{25,17},{2,10},{10... | collective-permute-start | bytes 1548296 | tf_op jit(solution)/shard_map/ppermute | solution.py:78
  51.0 16.1 %collective-permute-start.12 = (bf16[256,1024]{1,0:T(8,128)(2,1)}, bf16[256,1024]{1,0:T(8,128)(2,1)}, u32[]{:S(2)}, u32[]{:S(2)}) collective-permute-start(bf16[256,1024]{1,0:T(8,128)(2,1)} %param.19), channel_id=1, source_target_pairs={{0,24},{8,16},{16,8},{24,0},{1,25},{9,17},{17,9},{25,1},{2,26},{10... | collective-permute-start | bytes 1572872 | tf_op jit(solution)/shard_map/ppermute | solution.py:78
  52.0 23.5 %collective-permute-start.11 = (bf16[256,1024]{1,0:T(8,128)(2,1)}, bf16[256,1024]{1,0:T(8,128)(2,1)}, u32[]{:S(2)}, u32[]{:S(2)}) collective-permute-start(bf16[256,1024]{1,0:T(8,128)(2,1)} %param.19), channel_id=1, source_target_pairs={{0,16},{8,24},{16,0},{24,8},{1,17},{9,25},{17,1},{25,9},{2,18},{10... | collective-permute-start | bytes 1572872 | tf_op jit(solution)/shard_map/ppermute | solution.py:78
  54.5 22.9 %collective-permute-start.10 = (bf16[256,1024]{1,0:T(8,128)(2,1)}, bf16[256,1024]{1,0:T(8,128)(2,1)}, u32[]{:S(2)}, u32[]{:S(2)}) collective-permute-start(bf16[256,1024]{1,0:T(8,128)(2,1)} %param.19), channel_id=1, source_target_pairs={{0,8},{8,0},{16,24},{24,16},{1,9},{9,1},{17,25},{25,17},{2,10},{10... | collective-permute-start | bytes 1572872 | tf_op jit(solution)/shard_map/ppermute | solution.py:78
  67.0 18.8 %collective-permute-start.3 = (bf16[256,1024]{1,0:T(8,128)(2,1)S(1)}, bf16[256,1024]{1,0:T(8,128)(2,1)S(1)}, u32[]{:S(2)}, u32[]{:S(2)}) collective-permute-start(bf16[256,1024]{1,0:T(8,128)(2,1)S(1)} %copy-done.3), channel_id=1, source_target_pairs={{0,8},{8,0},{16,24},{24,16},{1,9},{9,1},{17,25},{25,17},{2,10},{10... | collective-permute-start | bytes 1572872 | tf_op jit(solution)/shard_map/ppermute | solution.py:78
  165.1 25.1 %collective-permute-start.15 = (bf16[256,1024]{1,0:T(8,128)(2,1)}, bf16[256,1024]{1,0:T(8,128)(2,1)}, u32[]{:S(2)}, u32[]{:S(2)}) collective-permute-start(bf16[256,1024]{1,0:T(8,128)(2,1)} %get-tuple-element.169), channel_id=1, source_target_pairs={{0,24},{8,16},{16,8},{24,0},{1,25},{9,17},{17,9},{25,1},{2,26},{10... | collective-permute-start | bytes 1572872 | tf_op jit(solution)/shard_map/ppermute | solution.py:78
  166.6 25.9 %collective-permute-start.14 = (bf16[256,1024]{1,0:T(8,128)(2,1)}, bf16[256,1024]{1,0:T(8,128)(2,1)}, u32[]{:S(2)}, u32[]{:S(2)}) collective-permute-start(bf16[256,1024]{1,0:T(8,128)(2,1)} %get-tuple-element.170), channel_id=1, source_target_pairs={{0,16},{8,24},{16,0},{24,8},{1,17},{9,25},{17,1},{25,9},{2,18},{10... | collective-permute-start | bytes 1572872 | tf_op jit(solution)/shard_map/ppermute | solution.py:78
  167.3 25.1 %collective-permute-start.13 = (bf16[256,1024]{1,0:T(8,128)(2,1)}, bf16[256,1024]{1,0:T(8,128)(2,1)}, u32[]{:S(2)}, u32[]{:S(2)}) collective-permute-start(bf16[256,1024]{1,0:T(8,128)(2,1)} %get-tuple-element.168), channel_id=1, source_target_pairs={{0,8},{8,0},{16,24},{24,16},{1,9},{9,1},{17,25},{25,17},{2,10},{10... | collective-permute-start | bytes 1572872 | tf_op jit(solution)/shard_map/ppermute | solution.py:78
  175.4 28.3 %collective-permute-start.9 = (bf16[256,1024]{1,0:T(8,128)(2,1)}, bf16[256,1024]{1,0:T(8,128)(2,1)}, u32[]{:S(2)}, u32[]{:S(2)}) collective-permute-start(bf16[256,1024]{1,0:T(8,128)(2,1)} %get-tuple-element.172), channel_id=1, source_target_pairs={{0,24},{8,16},{16,8},{24,0},{1,25},{9,17},{17,9},{25,1},{2,26},{10... | collective-permute-start | bytes 1572872 | tf_op jit(solution)/shard_map/ppermute | solution.py:78
  176.9 34.4 %collective-permute-start.8 = (bf16[256,1024]{1,0:T(8,128)(2,1)}, bf16[256,1024]{1,0:T(8,128)(2,1)}, u32[]{:S(2)}, u32[]{:S(2)}) collective-permute-start(bf16[256,1024]{1,0:T(8,128)(2,1)} %get-tuple-element.173), channel_id=1, source_target_pairs={{0,16},{8,24},{16,0},{24,8},{1,17},{9,25},{17,1},{25,9},{2,18},{10... | collective-permute-start | bytes 1572872 | tf_op jit(solution)/shard_map/ppermute | solution.py:78
  190.2 21.2 %collective-permute-start.7 = (bf16[256,1024]{1,0:T(8,128)(2,1)}, bf16[256,1024]{1,0:T(8,128)(2,1)S(1)}, u32[]{:S(2)}, u32[]{:S(2)}) collective-permute-start(bf16[256,1024]{1,0:T(8,128)(2,1)} %get-tuple-element.171), channel_id=1, source_target_pairs={{0,8},{8,0},{16,24},{24,16},{1,9},{9,1},{17,25},{25,17},{2,10},{10... | collective-permute-start | bytes 1572872 | tf_op jit(solution)/shard_map/ppermute | solution.py:78
  192.5 33.2 %collective-permute-start.29 = (bf16[4,128,1024]{2,1,0:T(8,128)(2,1)}, bf16[4,128,1024]{2,1,0:T(8,128)(2,1)}, u32[]{:S(2)}, u32[]{:S(2)}) collective-permute-start(bf16[4,128,1024]{2,1,0:T(8,128)(2,1)} %dynamic-slice_bitcast_fusion.1), channel_id=1, source_target_pairs={{0,1},{1,0},{2,3},{3,2},{4,5},{5,4},{6,7},{7,6},{8,9},{9,8},{10,11... | collective-permute-start | bytes 3145736 | tf_op jit(solution)/shard_map/ppermute | solution.py:83
  221.4 19.0 %collective-permute-start.37 = (bf16[512,1024]{1,0:T(8,128)(2,1)S(1)}, bf16[512,1024]{1,0:T(8,128)(2,1)S(1)}, u32[]{:S(2)}, u32[]{:S(2)}) collective-permute-start(bf16[512,1024]{1,0:T(8,128)(2,1)S(1)} %dynamic-slice_bitcast_fusion), channel_id=1, source_target_pairs={{0,1},{1,0},{2,3},{3,2},{4,5},{5,4},{6,7},{7,6},{8,9},{9,8},{10,11... | collective-permute-start | bytes 3145736 | tf_op jit(solution)/shard_map/ppermute | solution.py:83
  231.4 15.0 %collective-permute-start.31 = (bf16[128,1024]{1,0:T(8,128)(2,1)S(1)}, bf16[128,1024]{1,0:T(8,128)(2,1)S(1)}, u32[]{:S(2)}, u32[]{:S(2)}) collective-permute-start(bf16[128,1024]{1,0:T(8,128)(2,1)S(1)} %get-tuple-element.188), channel_id=1, source_target_pairs={{0,16},{8,24},{16,0},{24,8},{1,17},{9,25},{17,1},{25,9},{2,18},{10... | collective-permute-start | bytes 786440 | tf_op jit(solution)/shard_map/ppermute | solution.py:78
  237.3 23.1 %collective-permute-start.20 = (bf16[4,144,768]{2,1,0:T(8,128)(2,1)S(1)}, bf16[4,144,768]{2,1,0:T(8,128)(2,1)S(1)}, u32[]{:S(2)}, u32[]{:S(2)}) collective-permute-start(bf16[4,144,768]{2,1,0:T(8,128)(2,1)S(1)} %pad_maximum_fusion.4), channel_id=1, source_target_pairs={{0,2},{1,3},{6,4},{7,5},{8,10},{9,11},{14,12},{15,13},{16,18},{17,... | collective-permute-start | bytes 2654216 | tf_op jit(solution)/shard_map/ppermute | solution.py:94
  240.6 42.3 %collective-permute-start.38 = (bf16[512,1024]{1,0:T(8,128)(2,1)S(1)}, bf16[512,1024]{1,0:T(8,128)(2,1)S(1)}, u32[]{:S(2)}, u32[]{:S(2)}) collective-permute-start(bf16[512,1024]{1,0:T(8,128)(2,1)S(1)} %bitcast_add_fusion), channel_id=1, source_target_pairs={{0,2},{1,3},{6,4},{7,5},{8,10},{9,11},{14,12},{15,13},{16,18},{17,... | collective-permute-start | bytes 3145736 | tf_op jit(solution)/shard_map/ppermute | solution.py:94
  246.6 58.8 %collective-permute-start.33 = (bf16[4,128,1024]{2,1,0:T(8,128)(2,1)S(1)}, bf16[4,128,1024]{2,1,0:T(8,128)(2,1)S(1)}, u32[]{:S(2)}, u32[]{:S(2)}) collective-permute-start(bf16[4,128,1024]{2,1,0:T(8,128)(2,1)S(1)} %pad_maximum_fusion.3), channel_id=1, source_target_pairs={{0,2},{1,3},{6,4},{7,5},{8,10},{9,11},{14,12},{15,13},{16,18},{17,... | collective-permute-start | bytes 3145736 | tf_op jit(solution)/shard_map/ppermute | solution.py:94
  260.6 51.7 %collective-permute-start.21 = (bf16[4,144,768]{2,1,0:T(8,128)(2,1)S(1)}, bf16[4,144,768]{2,1,0:T(8,128)(2,1)S(1)}, u32[]{:S(2)}, u32[]{:S(2)}) collective-permute-start(bf16[4,144,768]{2,1,0:T(8,128)(2,1)S(1)} %fusion.77), channel_id=1, source_target_pairs={{2,4},{3,5},{4,2},{5,3},{10,12},{11,13},{12,10},{13,11},{18,20},{1... | collective-permute-start | bytes 2654216 | tf_op jit(solution)/shard_map/ppermute | solution.py:94
  261.4 48.1 %collective-permute-start.25 = (bf16[128,1024]{1,0:T(8,128)(2,1)S(1)}, bf16[128,1024]{1,0:T(8,128)(2,1)S(1)}, u32[]{:S(2)}, u32[]{:S(2)}) collective-permute-start(bf16[128,1024]{1,0:T(8,128)(2,1)S(1)} %bitcast_add_fusion.3), channel_id=1, source_target_pairs={{0,2},{1,3},{6,4},{7,5},{8,10},{9,11},{14,12},{15,13},{16,18},{17,... | collective-permute-start | bytes 786440 | tf_op jit(solution)/shard_map/ppermute | solution.py:94
  283.3 66.2 %collective-permute-start.39 = (bf16[512,1024]{1,0:T(8,128)(2,1)S(1)}, bf16[512,1024]{1,0:T(8,128)(2,1)}, u32[]{:S(2)}, u32[]{:S(2)}) collective-permute-start(bf16[512,1024]{1,0:T(8,128)(2,1)S(1)} %add.395), channel_id=1, source_target_pairs={{2,4},{3,5},{4,2},{5,3},{10,12},{11,13},{12,10},{13,11},{18,20},{1... | collective-permute-start | bytes 3145736 | tf_op jit(solution)/shard_map/ppermute | solution.py:94
  306.5 46.1 %collective-permute-start.34 = (bf16[4,128,1024]{2,1,0:T(8,128)(2,1)}, bf16[4,128,1024]{2,1,0:T(8,128)(2,1)}, u32[]{:S(2)}, u32[]{:S(2)}) collective-permute-start(bf16[4,128,1024]{2,1,0:T(8,128)(2,1)} %fusion.78), channel_id=1, source_target_pairs={{2,4},{3,5},{4,2},{5,3},{10,12},{11,13},{12,10},{13,11},{18,20},{1... | collective-permute-start | bytes 3145736 | tf_op jit(solution)/shard_map/ppermute | solution.py:94
  311.0 37.5 %collective-permute-start.27 = (bf16[128,1024]{1,0:T(8,128)(2,1)}, bf16[128,1024]{1,0:T(8,128)(2,1)}, u32[]{:S(2)}, u32[]{:S(2)}) collective-permute-start(bf16[128,1024]{1,0:T(8,128)(2,1)} %add.390), channel_id=1, source_target_pairs={{2,0},{3,1},{4,6},{5,7},{10,8},{11,9},{12,14},{13,15},{18,16},{19,... | collective-permute-start | bytes 786440 | tf_op jit(solution)/shard_map/ppermute | solution.py:94
  313.5 49.9 %collective-permute-start.22 = (bf16[4,144,768]{2,1,0:T(8,128)(2,1)}, bf16[4,144,768]{2,1,0:T(8,128)(2,1)}, u32[]{:S(2)}, u32[]{:S(2)}) collective-permute-start(bf16[4,144,768]{2,1,0:T(8,128)(2,1)} %fusion.108), channel_id=1, source_target_pairs={{2,0},{3,1},{4,6},{5,7},{10,8},{11,9},{12,14},{13,15},{18,16},{19,... | collective-permute-start | bytes 2654216 | tf_op jit(solution)/shard_map/ppermute | solution.py:94
  351.2 40.4 %collective-permute-start.40 = (bf16[512,1024]{1,0:T(8,128)(2,1)S(1)}, bf16[512,1024]{1,0:T(8,128)(2,1)S(1)}, u32[]{:S(2)}, u32[]{:S(2)}) collective-permute-start(bf16[512,1024]{1,0:T(8,128)(2,1)S(1)} %add.396), channel_id=1, source_target_pairs={{2,0},{3,1},{4,6},{5,7},{10,8},{11,9},{12,14},{13,15},{18,16},{19,... | collective-permute-start | bytes 3145736 | tf_op jit(solution)/shard_map/ppermute | solution.py:94
  354.3 59.6 %collective-permute-start.35 = (bf16[4,128,1024]{2,1,0:T(8,128)(2,1)S(1)}, bf16[4,128,1024]{2,1,0:T(8,128)(2,1)S(1)}, u32[]{:S(2)}, u32[]{:S(2)}) collective-permute-start(bf16[4,128,1024]{2,1,0:T(8,128)(2,1)S(1)} %fusion.107), channel_id=1, source_target_pairs={{2,0},{3,1},{4,6},{5,7},{10,8},{11,9},{12,14},{13,15},{18,16},{19,... | collective-permute-start | bytes 3145736 | tf_op jit(solution)/shard_map/ppermute | solution.py:94
  364.6 50.3 %collective-permute-start.23 = (bf16[4,144,768]{2,1,0:T(8,128)(2,1)S(1)}, bf16[4,144,768]{2,1,0:T(8,128)(2,1)S(1)}, u32[]{:S(2)}, u32[]{:S(2)}) collective-permute-start(bf16[4,144,768]{2,1,0:T(8,128)(2,1)S(1)} %broadcast_select_fusion.2), channel_id=1, source_target_pairs={{0,1},{1,0},{2,3},{3,2},{4,5},{5,4},{6,7},{7,6},{8,9},{9,8},{10,11... | collective-permute-start | bytes 2654216 | tf_op jit(solution)/shard_map/ppermute | solution.py:83
  392.6 53.2 %collective-permute-start.41 = (bf16[512,1024]{1,0:T(8,128)(2,1)}, bf16[512,1024]{1,0:T(8,128)(2,1)}, u32[]{:S(2)}, u32[]{:S(2)}) collective-permute-start(bf16[512,1024]{1,0:T(8,128)(2,1)} %broadcast_select_fusion), channel_id=1, source_target_pairs={{0,1},{1,0},{2,3},{3,2},{4,5},{5,4},{6,7},{7,6},{8,9},{9,8},{10,11... | collective-permute-start | bytes 3145736 | tf_op jit(solution)/shard_map/ppermute | solution.py:83
  414.9 42.5 %collective-permute-start.36 = (bf16[4,128,1024]{2,1,0:T(8,128)(2,1)}, bf16[4,128,1024]{2,1,0:T(8,128)(2,1)}, u32[]{:S(2)}, u32[]{:S(2)}) collective-permute-start(bf16[4,128,1024]{2,1,0:T(8,128)(2,1)} %broadcast_select_fusion.1), channel_id=1, source_target_pairs={{0,1},{1,0},{2,3},{3,2},{4,5},{5,4},{6,7},{7,6},{8,9},{9,8},{10,11... | collective-permute-start | bytes 3145736 | tf_op jit(solution)/shard_map/ppermute | solution.py:83
  (43 other events, 633.9 us)

commit v2 on v1

v2 whole, which is shorter than its diff:
```python
import functools
import math

import jax
import jax.numpy as jnp
from jax import lax
from jax.experimental import pallas as pl
from jax.experimental.pallas import tpu as pltpu
from jax.sharding import PartitionSpec as P

H = 16
HD = 64
ROT = 16
ADAM_STEP = 4


EPS_NORM = 1e-05
BETA_ONE = 0.9
BETA_TWO = 0.95
ADAM_EPS = 1e-08
LEARN_RATE = 0.01
VECTOR_RATE = 0.1
DECAY_RATE = 0.1
SQRT_HALF = 0.7071067811865476
INV_ROOT_TWO_PI = 0.3989422804014327

BF = jnp.bfloat16
F32 = jnp.float32
EXTRA = 16
LANES = 128
MIB = 2**20


def dot(left, right):
    return jnp.dot(left, right, preferred_element_type=F32)


def dot_lt(left, right):
    return lax.dot_general(left, right, (((0,), (0,)), ((), ())), preferred_element_type=F32)


def dot_rt(left, right):
    return lax.dot_general(left, right, (((1,), (1,)), ((), ())), preferred_element_type=F32)


def part(start, size, multiple=None):
    return pl.ds(pl.multiple_of(start, multiple or size), size)


def shard_swap(value, step):
    size = lax.axis_size("shard")
    return lax.ppermute(value, "shard", [(i, i ^ step) for i in range(size)])


def core_swap(value):
    size = lax.axis_size("dp")
    return lax.ppermute(value, "dp", [(i, i ^ 1) for i in range(size)])


def chain_stages():
    places = lax.axis_size("dp") // 2
    half = places // 2
    if places == 1:
        return []
    stages = []
    for step in range(half - 1):
        stages.append(([(step, step + 1), (places - 1 - step, places - 2 - step)], None))
    stages.append(([(half - 1, half), (half, half - 1)], None))
    for step in reversed(range(half - 1)):
        stages.append(
            ([(step + 1, step), (places - 2 - step, places - 1 - step)], (step, places - 1 - step))
        )
    return stages


def place_send(value, pairs):
    return lax.ppermute(
        value, "dp", [(2 * a + core, 2 * b + core) for a, b in pairs for core in range(2)]
    )


def after(value, *earlier):
    return lax.optimization_barrier((value, earlier))[0]


def combine(items):
    def body(flag_ref, *refs):
        count = len(items)
        for i, (_, _, taker) in enumerate(items):
            value, got, out = refs[2 * i], refs[2 * i + 1], refs[2 * count + i]
            if taker is None:
                out[...] = value[...] + got[...]
            else:
                out[...] = jnp.where(flag_ref[i] > 0, got[...], value[...])

    flags = [jnp.int32(0) if taker is None else taker.astype(jnp.int32) for _, _, taker in items]
    vmem = pl.BlockSpec(memory_space=pltpu.VMEM)
    return pl.pallas_call(
        body,
        out_shape=[jax.ShapeDtypeStruct(value.shape, value.dtype) for value, _, _ in items],
        in_specs=[pl.BlockSpec(memory_space=pltpu.SMEM)] + [vmem] * (2 * len(items)),
        out_specs=[vmem] * len(items),
        compiler_params=pltpu.CompilerParams(vmem_limit_bytes=12 * MIB),
        cost_estimate=pl.CostEstimate(flops=0, bytes_accessed=int(3.2e6), transcendentals=0),
    )(jnp.stack(flags), *[item for value, got, _ in items for item in (value, got)])


def advance(*moves):
    values = [value for value, _ in moves]
    depth = max(len(stages) for _, stages in moves)
    for step in range(depth):
        active = [i for i, (_, stages) in enumerate(moves) if step < len(stages)]
        items = []
        for i in active:
            pairs, takers = moves[i][1][step]
            flag = None
            if takers is not None:
                place = lax.axis_index("dp") // 2
                flag = functools.reduce(jnp.logical_or, [place == taker for taker in takers])
            items.append((values[i], place_send(values[i], pairs), flag))
        for i, item in zip(active, combine(items), strict=True):
            values[i] = item
    return values


def chain_parts():
    stages = chain_stages()
    half = (len(stages) + 1) // 2
    if not stages:
        return [], [], []
    return stages[: half - 1], stages[half - 1 : half], stages[half:]


def gather_rest(block, near):
    groups = lax.axis_size("shard")
    rows = block.shape[0]
    got = [[block], [near[0]], [near[1]]]
    got.append([shard_swap(near[0][: rows // 2], 2), shard_swap(near[1][rows // 2 :], 1)])
    for step in range(4, groups):
        got.append([shard_swap(block, step)])
    return got


def whole():
    return pl.BlockSpec(memory_space=pltpu.VMEM)


def full(shape):
    return pl.BlockSpec(memory_space=pltpu.VMEM)


def block_of(shape):
    return pl.BlockSpec(shape, lambda *_: (0,) * len(shape))


def by_row(shape):
    return pl.BlockSpec(shape, lambda i, *_: (i,) + (0,) * (len(shape) - 1))


def kernel_call(body, grid, in_specs, outs, scratch=(), time=1.0, limit=20):
    return pl.pallas_call(
        body,
        out_shape=[jax.ShapeDtypeStruct(shape, dtype) for shape, dtype, _ in outs],
        grid_spec=pltpu.PrefetchScalarGridSpec(
            num_scalar_prefetch=1,
            grid=grid,
            in_specs=in_specs,
            out_specs=[spec for _, _, spec in outs],
            scratch_shapes=list(scratch),
        ),
        compiler_params=pltpu.CompilerParams(vmem_limit_bytes=limit * MIB),
        cost_estimate=pl.CostEstimate(flops=0, bytes_accessed=int(3.2e6 * time), transcendentals=0),
    )


def flat(blocks):
    return [piece for block in blocks for piece in block]


def load_block(block, blocks, refs, scratch):
    at = 0
    for step, pieces in enumerate(blocks):
        mine = refs[at : at + len(pieces)]
        at += len(pieces)

        @pl.when(block == step)
        def _(mine=mine):
            row = 0
            for ref in mine:
                scratch[row : row + ref.shape[0], :] = ref[...]
                row += ref.shape[0]


def halves(value, core):
    size = value.shape[0] // 2
    first, second = value[:size], value[size:]
    return jnp.where(core == 0, first, second), jnp.where(core == 0, second, first)


def ends_of(lens_ref, block, slots):
    lengths = [lens_ref[block, 0:1, k : k + 1] for k in range(slots)]
    ends = []
    for item in lengths:
        ends.append(item if not ends else ends[-1] + item)
    return lengths, ends


def segments(index, ends):
    total = jnp.zeros(index.shape, F32)
    for end in ends:
        total = total + jnp.where(jnp.broadcast_to(end, index.shape) <= index, 1.0, 0.0)
    return total


def index_of(shape, axis):
    return lax.broadcasted_iota(jnp.int32, shape, axis).astype(F32)


def gelu_parts(values):
    gate = 0.5 * (1.0 + lax.erf(values * SQRT_HALF))
    slope = gate + values * jnp.exp(-0.5 * values * values) * INV_ROOT_TWO_PI
    return values * gate, slope


def adam_terms(weight, first, second, grad, decay, rate):
    corr_one = 1.0 - math.exp(ADAM_STEP * math.log(BETA_ONE))
    corr_two = 1.0 - math.exp(ADAM_STEP * math.log(BETA_TWO))
    first_new = BETA_ONE * first + (1.0 - BETA_ONE) * grad
    second_new = BETA_TWO * second + (1.0 - BETA_TWO) * grad * grad
    step_size = (first_new * (1.0 / corr_one)) / (jnp.sqrt(second_new * (1.0 / corr_two)) + ADAM_EPS)
    return weight - rate * (step_size + decay * weight), first_new, second_new


def pack(groups, sc, w_up, w_qkv, w_down, w_out, vectors, lengths):
    wide, hidden = w_up.shape
    half, ff = wide // 2, hidden // groups
    n_vec, slots = vectors.shape[0], lengths.shape[1]

    def body(s_ref, up_hbm, qkv_hbm, down_hbm, out_hbm, vec_ref, len_ref, *refs):
        out, (down_out, out_out) = refs[: 2 * groups], refs[2 * groups : 2 * groups + 2]
        up_scr, qkv_scr, down_scr, out_scr, sems, more = refs[2 * groups + 2 :]
        me, core = s_ref[0], s_ref[1]
        rest = [
            pltpu.make_async_copy(down_hbm, down_scr, more.at[0]),
            pltpu.make_async_copy(out_hbm, out_scr, more.at[1]),
        ]
        copies = []
        for step in range(groups):
            size = wide if step == 0 else half
            rows = pl.ds(0, wide) if step == 0 else part(core * half, half)
            owner = me ^ step
            at = pl.ds(0 if step == 0 else wide + (step - 1) * half, size)
            mine = [pltpu.make_async_copy(up_hbm.at[rows, part(owner * ff, ff)], up_scr.at[at], sems.at[step, 0])]
            for p in range(3):
                mine.append(
                    pltpu.make_async_copy(
                        qkv_hbm.at[rows, part(p * groups * wide + owner * wide, wide)],
                        qkv_scr.at[at, pl.ds(p * wide, wide)],
                        sems.at[step, 1 + p],
                    )
                )
            copies.append(mine)
        order = list(range(1, groups)) + [0]
        for step in order:
            for copy in copies[step]:
                copy.start()
        for copy in rest:
            copy.start()
        for step in order:
            for copy in copies[step]:
                copy.wait()
            up_out, qkv_out = out[2 * step], out[2 * step + 1]
            if step == 0:
                up_out[...] = up_scr[:wide].astype(BF)
                qkv_out[...] = qkv_scr[:wide].astype(BF)
                continue
            at = wide + (step - 1) * half
            up_out[:half, :] = up_scr[at : at + half].astype(BF)
            up_out[half:, :] = jnp.zeros((EXTRA, ff), BF)
            up_out[half : half + n_vec, :wide] = vec_ref[...].astype(BF)
            up_out[half + n_vec : half + n_vec + 1, :slots] = len_ref[...].astype(F32).astype(BF)
            qkv_out[...] = qkv_scr[at : at + half].astype(BF)
        for copy in rest:
            copy.wait()
        down_out[...] = down_scr[...].astype(BF)
        out_out[...] = out_scr[...].astype(BF)

    in_specs = [pl.BlockSpec(memory_space=pltpu.HBM)] * 4 + [full(vectors.shape), full(lengths.shape)]
    outs = []
    for step in range(groups):
        size = wide if step == 0 else half
        extra = 0 if step == 0 else EXTRA
        outs.append(((size + extra, ff), BF, full(None)))
        outs.append(((size, 3 * wide), BF, full(None)))
    outs += [(w_down.shape, BF, full(None)), (w_out.shape, BF, full(None))]
    rows = wide + (groups - 1) * half
    scratch = [pltpu.VMEM((rows, ff), F32), pltpu.VMEM((rows, 3 * wide), F32)]
    scratch += [pltpu.VMEM(w_down.shape, F32), pltpu.VMEM(w_out.shape, F32)]
    scratch += [pltpu.SemaphoreType.DMA((groups, 4)), pltpu.SemaphoreType.DMA((2,))]
    got = kernel_call(body, (1,), in_specs, outs, scratch, 7.0, 60)(sc, w_up, w_qkv, w_down, w_out, vectors, lengths)
    return got[0 : 2 * groups : 2], got[1 : 2 * groups : 2], got[2 * groups], got[2 * groups + 1]


def tables(sc, lens, groups, rows, slots):
    def body(s_ref, lens_ref, cos_ref, sin_ref):
        block = pl.program_id(0)
        lengths, ends = ends_of(lens_ref, block, slots)
        index = index_of((rows, LANES), 0)
        start = jnp.zeros((rows, LANES), F32)
        for length, end in zip(lengths, ends, strict=True):
            start = start + jnp.where(jnp.broadcast_to(end, index.shape) <= index, length, 0.0)
        lane = lax.broadcasted_iota(jnp.int32, (rows, LANES), 1) % HD
        pair = (lane % (ROT // 2)).astype(F32)
        freq = jnp.where(lane < ROT, jnp.exp(-pair * (2.0 * math.log(10000.0) / ROT)), 0.0)
        angle = (index - start) * freq
        cos_ref[...] = jnp.cos(angle)
        sin_ref[...] = jnp.sin(angle)

    out = ((groups * rows, LANES), F32, by_row((rows, LANES)))
    return kernel_call(body, (groups,), [full(lens.shape)], [out, out], (), 3.0)(sc, lens)


def forward_up(sc, xs, own, mine, other, vectors, lengths):
    groups, n_x = len(xs), len(flat(xs))
    rows, width = xs[0][0].shape
    wide, ff = own.shape
    half = wide // 2
    n_vec, slots = vectors.shape[0], lengths.shape[1]
    tok = groups * rows

    def body(s_ref, *refs):
        x_refs, refs = refs[:n_x], refs[n_x:]
        own_ref = refs[0]
        mine_refs = refs[1:groups]
        other_refs = refs[groups : 2 * groups - 1]
        vec_in, len_in = refs[2 * groups - 1 : 2 * groups + 1]
        attn_ref, mlp_ref, act_ref, slope_ref, stats_ref, w_ref, vec_ref, lens_ref, x_scr = refs[2 * groups + 1 :]
        me, core = s_ref[0], s_ref[1]
        block = pl.program_id(0)

        @pl.when(block == 0)
        def _():
            w_ref[part(me * wide, wide), :] = own_ref[...]
            vec_ref[...] = jnp.zeros_like(vec_ref)
            lens_ref[...] = jnp.zeros_like(lens_ref)
            vec_ref[0:n_vec, part(me * wide, wide)] = vec_in[...].astype(BF).astype(F32)
            lens_ref[0, 0:1, 0:slots] = len_in[...].astype(F32)
            for step in range(1, groups):
                at = (me ^ step) * wide
                w_ref[part(at + core * half, half), :] = mine_refs[step - 1][:half, :]
                w_ref[part(at + (1 - core) * half, half), :] = other_refs[step - 1][:half, :]
                vec_ref[0:n_vec, part(at, wide)] = mine_refs[step - 1][half : half + n_vec, :wide].astype(F32)
                lens_ref[step, 0:1, 0:slots] = mine_refs[step - 1][
                    half + n_vec : half + n_vec + 1, :slots
                ].astype(F32)

        load_block(block, xs, x_refs, x_scr)
        x = x_scr[...].astype(F32)
        mean = jnp.mean(x, axis=1, keepdims=True)
        centred = x - mean
        inv = lax.rsqrt(jnp.mean(centred * centred, axis=1, keepdims=True) + EPS_NORM)
        normed = centred * inv
        lane = lax.broadcasted_iota(jnp.int32, (rows, LANES), 1)
        stats_ref[...] = jnp.where(lane == 0, mean, inv)
        attn_ref[...] = (normed * vec_ref[0:1, :] + vec_ref[1:2, :]).astype(BF)
        in_mlp = (normed * vec_ref[2:3, :] + vec_ref[3:4, :]).astype(BF)
        mlp_ref[...] = in_mlp
        first = me * ff
        bias = vec_ref[pl.ds(9 + first // width, 1), part(lax.rem(me, width // ff) * ff, ff, LANES)]
        act, slope = gelu_parts(dot(in_mlp, w_ref[...]) + bias)
        act_ref[...] = act.astype(BF)
        slope_ref[...] = slope

    piece = (half + EXTRA, ff)
    in_specs = (
        [full(item.shape) for item in flat(xs)]
        + [full(own.shape)]
        + [full(piece)] * (2 * (groups - 1))
        + [full(vectors.shape), full(lengths.shape)]
    )
    outs = [
        ((tok, width), BF, by_row((rows, width))),
        ((tok, width), BF, by_row((rows, width))),
        ((tok, ff), BF, by_row((rows, ff))),
        ((tok, ff), F32, by_row((rows, ff))),
        ((tok, LANES), F32, by_row((rows, LANES))),
        ((width, ff), BF, full((width, ff))),
        ((EXTRA, width), F32, full((EXTRA, width))),
        ((groups, 8, LANES), F32, full((groups, 8, LANES))),
    ]
    return kernel_call(
        body, (groups,), in_specs, outs, [pltpu.VMEM((rows, width), BF)], 6.5
    )(sc, *flat(xs), own, *mine, *other, vectors, lengths)


def grad_of_down(sc, cots, lens, act, slots, scale):
    groups, n_c = len(cots), len(flat(cots))
    rows, width = cots[0][0].shape
    ff = act.shape[1]

    def body(s_ref, *refs):
        cot_refs = iter(refs[:n_c])
        lens_ref, act_ref, branch_ref, bias_ref, away_ref, keep_ref = refs[n_c:]
        core = s_ref[1]
        for step, pieces in enumerate(cots):
            _, ends = ends_of(lens_ref, step, slots)
            row = 0
            for piece in pieces:
                size = piece.shape[0]
                index = index_of((size, 1), 0) + float(row)
                valid = jnp.where(index < jnp.broadcast_to(ends[-1], (size, 1)), 1.0, 0.0)
                branch = next(cot_refs)[...].astype(F32) * valid
                at = step * rows + row
                branch_ref[at : at + size, :] = branch.astype(BF)
                row += size
                if step == 0:
                    bias_ref[...] = jnp.broadcast_to(jnp.sum(branch, axis=0, keepdims=True), bias_ref.shape)
        size = ff // 2
        for ref, which in ((away_ref, 1 - core), (keep_ref, core)):
            ref[...] = (dot_lt(act_ref[:, part(which * size, size)], branch_ref[...]) * scale).astype(BF)

    outs = [
        ((groups * rows, width), BF, full((groups * rows, width))),
        ((8, width), F32, full((8, width))),
        ((ff // 2, width), BF, full((ff // 2, width))),
        ((ff // 2, width), BF, full((ff // 2, width))),
    ]
    return kernel_call(
        body,
        (1,),
        [full(item.shape) for item in flat(cots) + [lens, act]],
        outs,
        (),
        3.5,
    )(sc, *flat(cots), lens, act)


def backward_up(sc, branch, slope, w_down, in_mlp, scale, groups):
    tok, width = branch.shape
    rows = tok // groups
    ff = slope.shape[1]
    half = width // groups // 2

    def body(s_ref, branch_ref, slope_ref, wd_ref, mlp_ref, away_ref, keep_ref, up_ref, bias_ref):
        me, core = s_ref[0], s_ref[1]
        block = pl.program_id(0)

        @pl.when(block == 0)
        def _():
            bias_ref[...] = jnp.zeros_like(bias_ref)

        d_up = dot_rt(branch_ref[...], wd_ref[...]) * slope_ref[...]
        bias_ref[0:1, :] += jnp.sum(d_up, axis=0, keepdims=True)
        up_ref[part(block * rows, rows), :] = d_up.astype(BF)

        @pl.when(block == groups - 1)
        def _():
            def piece(i, carry):
                grad = (dot_lt(mlp_ref[:, part((me ^ i) * (2 * half), 2 * half)], up_ref[...]) * scale).astype(BF)
                keep_ref[i], away_ref[i] = halves(grad, core)
                return carry

            lax.fori_loop(0, groups, piece, 0)

    in_specs = [by_row((rows, width)), by_row((rows, ff)), full(w_down.shape), full(in_mlp.shape)]
    outs = [
        ((groups, half, ff), BF, full((groups, half, ff))),
        ((groups, half, ff), BF, full((groups, half, ff))),
        ((tok, ff), BF, full((tok, ff))),
        ((8, ff), F32, full((8, ff))),
    ]
    return kernel_call(body, (groups,), in_specs, outs, (), 6.8)(
        sc, branch, slope, w_down, in_mlp
    )


def attention(sc, in_attn, branch, cosine, sine, lens, vec, own, mine, other, w_out, groups, slots):
    tok, width = in_attn.shape
    rows = tok // groups
    wide = width // groups
    half = wide // 2
    scale = HD ** (-0.5)

    def body(s_ref, *refs):
        a_ref, branch_ref, cos_ref, sin_ref, lens_ref, vec_ref = refs[:6]
        own_ref = refs[6]
        mine_refs = refs[7 : 6 + groups]
        other_refs = refs[6 + groups : 5 + 2 * groups]
        wo_ref, heads_ref, proj_ref, bias_ref, w_ref = refs[5 + 2 * groups :]
        me, core = s_ref[0], s_ref[1]
        block = pl.program_id(0)

        @pl.when(block == 0)
        def _():
            w_ref[part(me * wide, wide), :] = own_ref[...]
            for step in range(1, groups):
                at = (me ^ step) * wide
                w_ref[part(at + core * half, half), :] = mine_refs[step - 1][...]
                w_ref[part(at + (1 - core) * half, half), :] = other_refs[step - 1][...]
            bias_ref[...] = jnp.zeros_like(bias_ref)

        bias = [vec_ref[6 + p : 7 + p, part(me * wide, wide)] for p in range(3)]
        projected = dot(a_ref[...], w_ref[...])
        d_heads = dot_rt(branch_ref[...], wo_ref[...]).astype(BF)
        _, ends = ends_of(lens_ref, block, slots)
        key_index = index_of((rows, 1), 0)
        query_index = index_of((1, rows), 1)
        allowed = (segments(key_index, ends) == segments(query_index, ends)) & (key_index <= query_index)
        lane = lax.broadcasted_iota(jnp.int32, (rows, LANES), 1)
        cosine, sine = cos_ref[...], sin_ref[...]
        low = jnp.where(lane % HD < ROT // 2, sine, 0.0)
        high = jnp.where(lane % HD >= ROT // 2, sine, 0.0)

        def turn(values, sign):
            ahead = pltpu.roll(values, LANES - ROT // 2, 1)
            behind = pltpu.roll(values, ROT // 2, 1)
            return values * cosine + sign * (behind * high - ahead * low)

        first_half = lane < HD
        for pair in range(wide // LANES):
            lo, hi = pair * LANES, (pair + 1) * LANES
            query = turn(projected[:, lo:hi] + bias[0][:, lo:hi], 1.0).astype(BF)
            key = turn(projected[:, wide + lo : wide + hi] + bias[1][:, lo:hi], 1.0).astype(BF)
            value = (projected[:, 2 * wide + lo : 2 * wide + hi] + bias[2][:, lo:hi]).astype(BF)
            d_out = d_heads[:, lo:hi]
            key_t, value_t = key.T, value.T
            heads_t, query_t, d_keys, d_values = [], [], [], []
            for head in range(2):
                mask = first_half if head == 0 else ~first_half
                only_key = jnp.where(mask, key, jnp.zeros_like(key))
                only_value = jnp.where(mask, value, jnp.zeros_like(value))
                scores = jnp.where(allowed, dot_rt(only_key, query) * scale, -1e30)
                top = jnp.max(scores, axis=0, keepdims=True)
                weights = jnp.exp(scores - top)
                probs = weights * (1.0 / jnp.sum(weights, axis=0, keepdims=True))
                probs_b = probs.astype(BF)
                d_probs = dot_rt(only_value, d_out)
                delta = jnp.sum(probs * d_probs, axis=0, keepdims=True)
                d_scores = (probs * (d_probs - delta)).astype(BF)
                heads_t.append(dot(value_t[head * HD : (head + 1) * HD], probs_b))
                query_t.append(dot(key_t[head * HD : (head + 1) * HD], d_scores))
                d_keys.append(dot(d_scores, query))
                d_values.append(dot(probs_b, d_out))
            heads_ref[:, lo:hi] = jnp.concatenate(heads_t, axis=0).T.astype(BF)
            d_query = turn(jnp.concatenate(query_t, axis=0).T * scale, -1.0)
            d_key = turn(jnp.where(first_half, d_keys[0], d_keys[1]) * scale, -1.0)
            d_value = jnp.where(first_half, d_values[0], d_values[1])
            for p, item in enumerate((d_query, d_key, d_value)):
                proj_ref[:, p * wide + lo : p * wide + hi] = item.astype(BF)
                bias_ref[0:1, p * wide + lo : p * wide + hi] += jnp.sum(item, axis=0, keepdims=True)

    in_specs = (
        [by_row((rows, width)), by_row((rows, width)), by_row((rows, LANES)), by_row((rows, LANES))]
        + [full(lens.shape), full(vec.shape)]
        + [full((half, 3 * wide))] * (1 + 2 * (groups - 1))
        + [full(w_out.shape)]
    )
    outs = [
        ((tok, wide), BF, by_row((rows, wide))),
        ((tok, 3 * wide), BF, by_row((rows, 3 * wide))),
        ((8, 3 * wide), F32, full((8, 3 * wide))),
        ((width, 3 * wide), BF, full((width, 3 * wide))),
    ]
    return kernel_call(body, (groups,), in_specs, outs, (), 11.3)(
        sc, in_attn, branch, cosine, sine, lens, vec, own, *mine, *other, w_out
    )


def back_to_tokens(sc, xs, heads, act, d_proj, d_up, stats, vec, w_out, w_down, w_qkv, w_up, bias_up, bias_qkv, bias_out):
    groups, n_x = len(xs), len(flat(xs))
    rows, width = xs[0][0].shape
    wide = width // groups
    ff = act.shape[1]

    def body(s_ref, *refs):
        x_refs, refs = refs[:n_x], refs[n_x:]
        (
            heads_ref, act_ref, proj_ref, d_up_ref, stats_ref, vec_ref, wo_ref, wd_ref, wq_ref, wu_ref,
            up_ref, qkv_ref, out_ref,
        ) = refs[:13]
        own_ref = refs[13]
        piece_refs = refs[14 : 13 + groups]
        grad_ref, x_scr = refs[13 + groups :]
        me = s_ref[0]
        block = pl.program_id(0)
        load_block(block, xs, x_refs, x_scr)

        @pl.when(block == 0)
        def _():
            grad_ref[...] = jnp.zeros_like(grad_ref)
            grad_ref[4:6, :] = out_ref[0:2, :]
            for p in range(3):
                grad_ref[6 + p : 7 + p, part(me * wide, wide)] = qkv_ref[0:1, p * wide : (p + 1) * wide]
            first = me * ff
            grad_ref[pl.ds(9 + first // width, 1), part(lax.rem(me, width // ff) * ff, ff, LANES)] = up_ref[0:1, :]

        normed = (x_scr[...].astype(F32) - stats_ref[:, 0:1]) * stats_ref[:, 1:2]
        branch_out = dot(heads_ref[...], wo_ref[...]) + dot(act_ref[...], wd_ref[...])
        total = None
        for row, left, right in ((0, proj_ref, wq_ref), (2, d_up_ref, wu_ref)):
            d_in = dot_rt(left[...], right[...])
            grad_ref[row : row + 1, :] += jnp.sum(d_in * normed, axis=0, keepdims=True)
            grad_ref[row + 1 : row + 2, :] += jnp.sum(d_in, axis=0, keepdims=True)
            term = d_in * vec_ref[row : row + 1, :]
            total = term if total is None else total + term

        @pl.when(block == 0)
        def _():
            own_ref[:, :width] = branch_out
            own_ref[:, width:] = total

        for step in range(1, groups):

            @pl.when(block == step)
            def _(step=step):
                piece_refs[step - 1][:, :width] = branch_out.astype(BF)
                piece_refs[step - 1][:, width:] = total.astype(BF)

    constant = [vec, w_out, w_down, w_qkv, w_up, bias_up, bias_qkv, bias_out]
    in_specs = (
        [block_of(item.shape) for item in flat(xs)]
        + [by_row((rows, item.shape[1])) for item in (heads, act, d_proj, d_up, stats)]
        + [block_of(item.shape) for item in constant]
    )
    outs = [((rows, 2 * width), F32, full((rows, 2 * width)))]
    outs += [((rows, 2 * width), BF, full((rows, 2 * width)))] * (groups - 1)
    outs += [((EXTRA, width), F32, full((EXTRA, width)))]
    got = kernel_call(
        body,
        (groups,),
        in_specs,
        outs,
        [pltpu.VMEM((rows, width), BF)],
        9.4,
        58,
    )(sc, *flat(xs), heads, act, d_proj, d_up, stats, *constant)
    return got[0], got[1:groups], got[groups]


def grads_of_attention(sc, in_attn, d_proj, heads, branch, scale, groups):
    tok, width = in_attn.shape
    wide = heads.shape[1]
    half = wide // 2

    def body(s_ref, a_ref, proj_ref, heads_ref, branch_ref, out_away, out_keep, qkv_away, qkv_keep):
        me, core = s_ref[0], s_ref[1]

        def piece(i, carry):
            grad = (dot_lt(a_ref[:, part((me ^ i) * wide, wide)], proj_ref[...]) * scale).astype(BF)
            qkv_keep[i], qkv_away[i] = halves(grad, core)
            return carry

        lax.fori_loop(0, groups, piece, 0)
        grad = (dot_lt(heads_ref[...], branch_ref[...]) * scale).astype(BF)
        out_keep[...], out_away[...] = halves(grad, core)

    ops = (in_attn, d_proj, heads, branch)
    out = ((half, width), BF, full((half, width)))
    qkv = ((groups, half, 3 * wide), BF, full((groups, half, 3 * wide)))
    return kernel_call(
        body, (1,), [full(item.shape) for item in ops], [out, out, qkv, qkv], (), 4.0
    )(sc, *ops)


def finish(sc, own, got, tokens, cotangent, lens, stats, vec, slots):
    rows, width = tokens.shape

    def body(s_ref, own_ref, *refs):
        got_refs = refs[: len(got)]
        tok_ref, cot_ref, lens_ref, stats_ref, vec_ref, out_ref, grad_ref = refs[len(got) :]
        branch = own_ref[:, :width]
        scaled = own_ref[:, width:]
        for ref in got_refs:
            branch = branch + ref[:, :width].astype(F32)
            scaled = scaled + ref[:, width:].astype(F32)
        size = branch.shape[0]
        _, ends = ends_of(lens_ref, 0, slots)
        index = index_of((size, 1), 0) + (pl.program_id(0) * size).astype(F32)
        valid = jnp.where(index < jnp.broadcast_to(ends[-1], (size, 1)), 1.0, 0.0)
        x = tok_ref[...].astype(F32)
        out_ref[...] = (x + valid * (branch + vec_ref[4:5, :] + vec_ref[5:6, :])).astype(BF)
        inv = stats_ref[:, 1:2]
        normed = (x - stats_ref[:, 0:1]) * inv
        d_tokens = inv * (
            scaled
            - jnp.mean(scaled, axis=1, keepdims=True)
            - normed * jnp.mean(scaled * normed, axis=1, keepdims=True)
        )
        grad_ref[...] = (cot_ref[...].astype(F32) + d_tokens).astype(BF)

    size = rows // 2
    in_specs = [by_row((size, 2 * width))] * (1 + len(got)) + [by_row((size, width))] * 2
    in_specs += [full(lens.shape), by_row((size, LANES)), full(vec.shape)]
    out = ((rows, width), BF, by_row((size, width)))
    return kernel_call(body, (2,), in_specs, [out, out], (), 2.4)(
        sc, own, *got, tokens, cotangent, lens, stats, vec
    )


def assemble(shape, arrays, plan):
    def body(*refs):
        ins, out = refs[: len(arrays)], refs[len(arrays)]
        me, core = lax.axis_index("shard"), lax.rem(lax.axis_index("dp"), 2)
        for which, index, row, column, size in plan(me, core):
            out[part(row, size[0]), part(column, size[1])] = ins[which][index]

    return pl.pallas_call(
        body,
        out_shape=jax.ShapeDtypeStruct(shape, arrays[0].dtype),
        in_specs=[pl.BlockSpec(memory_space=pltpu.VMEM)] * len(arrays),
        out_specs=pl.BlockSpec(memory_space=pltpu.VMEM),
        compiler_params=pltpu.CompilerParams(vmem_limit_bytes=20 * MIB),
        cost_estimate=pl.CostEstimate(flops=0, bytes_accessed=0, transcendentals=0),
    )(*arrays)


def adam(masters, grad, decay=DECAY_RATE, rate=LEARN_RATE):
    weight, first, second = masters
    grad = grad.astype(F32)
    return (grad,) + adam_terms(weight, first, second, grad, decay, rate)


def local(
    tokens, cotangent, lengths,
    w_qkv, w_out, w_up, w_down, vectors,
    m_qkv, m_out, m_up, m_down, m_vectors,
    v_qkv, v_out, v_up, v_down, v_vectors,
):
    groups = lax.axis_size("shard")
    me = lax.axis_index("shard")
    core = lax.axis_index("dp") % 2
    rows, width = tokens.shape
    hidden = w_up.shape[1]
    wide = width // groups
    half = wide // 2
    ff = hidden // groups
    n_vec = vectors.shape[0]
    slots = lengths.shape[1]
    others = range(1, groups)
    sc = jnp.stack([me, core]).astype(jnp.int32)
    scale = float(rows * groups * lax.axis_size("dp")) ** (-0.5)

    size = ff // 2
    inward, across, outward = chain_parts()
    fence = lax.optimization_barrier

    up_parts, qkv_parts, down_w, out_w = pack(groups, sc, w_up, w_qkv, w_down, w_out, vectors, lengths)
    near = [shard_swap(tokens, step) for step in (1, 2)]
    near, up_parts = fence((near, up_parts))
    up_mine = [shard_swap(item, step) for item, step in zip(up_parts[1:], others, strict=True)]
    xs = gather_rest(tokens, near)
    cot_near = [shard_swap(after(cotangent, near), step) for step in (1, 2)]
    up_other = [core_swap(item) for item in up_mine]
    in_attn, in_mlp, act, slope, stats, up_w, vec, lens = forward_up(
        sc, xs, up_parts[0], up_mine, up_other, vectors, lengths
    )
    cot_near, act = fence((cot_near, act))
    cots = gather_rest(cotangent, cot_near)
    qkv_mine = [shard_swap(item, step) for item, step in zip(after(qkv_parts[1:], cot_near), others, strict=True)]
    cosine, sine = tables(sc, after(lens, cot_near), groups, rows, slots)
    cots, cosine = fence((cots, cosine))

    branch, bias_out, down_away, down_keep = grad_of_down(sc, cots, lens, act, slots, scale)
    down_got = core_swap(down_away)
    up_away, up_keep, d_up, bias_up = backward_up(sc, branch, slope, down_w, in_mlp, scale, groups)
    down_got, d_up, up_away, qkv_mine = fence((down_got, d_up, up_away, qkv_mine))
    down = down_keep + down_got
    up_got = core_swap(up_away)
    qkv_other = [core_swap(item) for item in qkv_mine]
    down, up_got, qkv_other, branch_a = fence((down, up_got, qkv_other, branch))
    up_sums = [up_keep[i] + up_got[i] for i in range(groups)]
    up_sums, down, branch_a = fence((up_sums, down, branch_a))

    [down] = advance((down, inward))
    up_rows = [up_sums[0]] + [shard_swap(up_sums[step], step) for step in others]
    heads, d_proj, bias_qkv, qkv_w = attention(
        sc, in_attn, branch_a, cosine, sine, lens, vec, qkv_parts[0], qkv_mine, qkv_other, out_w, groups, slots
    )
    out_away, out_keep, qkv_away, qkv_keep = grads_of_attention(sc, in_attn, d_proj, heads, branch, scale, groups)
    down, up_rows, qkv_away, out_away = fence((down, up_rows, qkv_away, out_away))
    qkv_got = core_swap(qkv_away)
    up = jnp.stack(up_rows)
    qkv_got, up, down = fence((qkv_got, up, down))
    qkv_sums = [qkv_keep[i] + qkv_got[i] for i in range(groups)]
    qkv_sums, up, down, d_proj = fence((qkv_sums, up, down, d_proj))

    down, up = advance((down, across), (up, inward))
    qkv_rows = [qkv_sums[0]] + [shard_swap(qkv_sums[step], step) for step in others]
    own, pieces, vec_grad = back_to_tokens(
        sc, xs, heads, act, d_proj, d_up, stats, vec, out_w, down_w, qkv_w, up_w, bias_up, bias_qkv, bias_out
    )
    down, up, qkv_rows, vec_grad, pieces = fence((down, up, qkv_rows, vec_grad, pieces))
    qkv = jnp.stack(qkv_rows)
    vec_grad = (vec_grad * scale).reshape(EXTRA, groups, wide)
    vec_parts = [lax.dynamic_index_in_dim(vec_grad, me ^ step, 1, keepdims=False) for step in range(groups)]
    down, up, qkv, vec_parts, pieces = fence((down, up, qkv, vec_parts, pieces))

    down, up, qkv = advance((down, outward), (up, across), (qkv, inward))
    vec_rows = [vec_parts[0]] + [shard_swap(vec_parts[step], step) for step in others]
    got = [shard_swap(pieces[0], 1)]
    down, up, qkv, vec_rows, got, pieces = fence((down, up, qkv, vec_rows, got, pieces))
    vec_sum = jnp.pad(sum(vec_rows).astype(BF), ((0, 0), (0, width - wide)))
    out_away, out_keep = (jnp.concatenate([item, vec_sum]) for item in (out_away, out_keep))
    out_got = core_swap(out_away)
    down_other = core_swap(down)
    out_got, down_other, up, qkv, pieces = fence((out_got, down_other, up, qkv, pieces))
    out = out_keep + out_got
    out, down_other, up, qkv, pieces = fence((out, down_other, up, qkv, pieces))

    up, qkv, out = advance((up, outward), (qkv, across), (out, inward))
    got.append(shard_swap(pieces[1], 2))
    down_grad = assemble(
        (ff, width),
        [down, down_other],
        lambda me, core: [(side, slice(None), (core ^ side) * size, 0, (size, width)) for side in range(2)],
    )
    new_down = adam((w_down, m_down, v_down), down_grad)
    up, qkv, out, new_down, got, pieces = fence((up, qkv, out, new_down, got, pieces))
    up_other = core_swap(up)
    up_other, qkv, out, pieces = fence((up_other, qkv, out, pieces))

    qkv, out = advance((qkv, outward), (out, across))
    got += [shard_swap(item, step) for item, step in zip(pieces[2:], others[2:], strict=True)]
    up_grad = assemble(
        (wide, hidden),
        [up, up_other],
        lambda me, core: [
            (side, step, (core ^ side) * half, (me ^ step) * ff, (half, ff))
            for side in range(2)
            for step in range(groups)
        ],
    )
    new_up = adam((w_up, m_up, v_up), up_grad)
    qkv, out, new_up, got = fence((qkv, out, new_up, got))
    qkv_other = core_swap(qkv)
    qkv_other, out = fence((qkv_other, out))

    [out] = advance((out, outward))
    qkv_grad = assemble(
        (wide, 3 * width),
        [qkv, qkv_other],
        lambda me, core: [
            (
                side,
                (step, slice(None), slice(p * wide, (p + 1) * wide)),
                (core ^ side) * half,
                p * width + (me ^ step) * wide,
                (half, wide),
            )
            for side in range(2)
            for step in range(groups)
            for p in range(3)
        ],
    )
    new_qkv = adam((w_qkv, m_qkv, v_qkv), qkv_grad)
    output, input_grad = finish(sc, own, got, tokens, cotangent, lens, stats, vec, slots)
    out, new_qkv, output, input_grad = fence((out, new_qkv, output, input_grad))
    out_other = core_swap(out)
    out_grad = jnp.where(
        (jnp.arange(2) == core)[:, None, None], out[None, :half], out_other[None, :half]
    ).reshape(wide, width)
    vec_total = out[half : half + n_vec, :wide]

    news = (
        new_qkv,
        adam((w_out, m_out, v_out), out_grad),
        new_up,
        new_down,
        adam((vectors, m_vectors, v_vectors), vec_total, 0.0, VECTOR_RATE),
    )
    return (output, input_grad) + tuple(item[kind] for kind in range(4) for item in news)


def solution(mesh):
    by_token = P(("shard", "dp"), None)
    params = (P("shard", None),) * 4 + (P(None, "shard"),)
    return jax.shard_map(
        local,
        mesh=mesh,
        in_specs=(by_token,) * 3 + params * 3,
        out_specs=(by_token,) * 2 + params * 4,
        check_vma=False,
    )
```

time: 510 us -> 268 us (0.53); the launches traced: 503 us -> 267 us
  local copies, waits for them, and re-layouts: 146 us -> 12 us
  waiting for transfers between devices: 166 us -> 91.3 us
  Pallas kernels: 0 us -> 66.7 us
  matrix products: 61.5 us -> 0 us
  other arithmetic: 74.2 us -> 32.5 us
  starting transfers between devices: 52.6 us -> 62.7 us
    pallas_call x0 -> x18, Pallas kernels: none -> 66.7 us  [the longest x1 16 us: back_to_tokens(): kernel_call(body, (groups,), in_specs, outs, [pltpu.VMEM((rows, width), B...]
    ppermute x12, waiting for transfers between devices: 112 us -> 48.9 us  [place_send(): lax.ppermute(value, 'dp', [(2 * a + core, 2 * b + core) for a, b in pairs...]
    dot_general x18 -> x0, matrix products: 61.5 us -> none  [the longest x4 22.4 us: right_t(): lax.dot_general(left, right, (((1,), (1,)), ((), ())), preferred_element_...]
    unnamed x96 -> x112, local copies, waits for them, and re-layouts: 70.5 us -> 11.7 us
    ppermute x21 -> x26, waiting for transfers between devices: 53.3 us -> 31.5 us  [shard_swap(): return lax.ppermute(value, 'shard', [(i, i ^ step) for i in range(size)])]
    convert_element_type x11 -> x0, local copies, waits for them, and re-layouts: 16.1 us -> none  [the longest x1 5.36 us: local(): natural(sum_up).reshape(groups, wide, ff).transpose(1, 0, 2)]
    slice x20 -> x6, local copies, waits for them, and re-layouts: 15.9 us -> 0.11 us  [the longest x2 0.04 us: gather_rest(): near[0][:rows // 2]]
    dynamic_update_slice x20 -> x0, local copies, waits for them, and re-layouts: 12.3 us -> none  [the longest x3 5.45 us: local(): lax.dynamic_update_slice(full, other_half[step - 1][None, None], (at, 1 -...]
  transfers between devices with their start and end apart: 42 -> 52, of which waited for: 20 -> 26; matrix products, arithmetic and copies ran while one was open for 32% -> 11% of each run, Pallas kernels for 0% -> 24%
where the time goes in v2:
time: 268 us; the launch traced here: 267 us
  waiting for transfers between devices  91.3 us (34%)
  Pallas kernels  66.7 us (25%)
  starting transfers between devices  62.7 us (23%)
  other arithmetic  32.5 us (12%)
  local copies, waits for them, and re-layouts  12 us (4%)
    ppermute x12, waiting for transfers between devices, place_send(): lax.ppermute(value, 'dp', [(2 * a + core, 2 * b + core) for a, b in pairs...  48.9 us
    ppermute x26, waiting for transfers between devices, shard_swap(): return lax.ppermute(value, 'shard', [(i, i ^ step) for i in range(size)])  31.5 us
    ppermute x12, starting transfers between devices, place_send(): lax.ppermute(value, 'dp', [(2 * a + core, 2 * b + core) for a, b in pairs...  31 us
    ppermute x26, starting transfers between devices, shard_swap(): return lax.ppermute(value, 'shard', [(i, i ^ step) for i in range(size)])  29.4 us
    sub x5, other arithmetic, adam_terms(): return (weight - rate * (step_size + decay * weight), first_new, second_new)  21.2 us
    pallas_call x1, Pallas kernels, back_to_tokens(): kernel_call(body, (groups,), in_specs, outs, [pltpu.VMEM((rows, width), B...  16 us
    unnamed x112, local copies, waits for them, and re-layouts  11.7 us
    pallas_call x1, Pallas kernels, attention(): kernel_call(body, (groups,), in_specs, outs, (), 11.3)  11.2 us
  transfers between devices with their start and end apart: 52, of which 26 were waited for; matrix products, arithmetic and copies ran while one was open for 11% of the time, Pallas kernels for 24%

profile of v2, /device:TPU:0, one launch (start us, length us, event | category | flops | bytes accessed | tf_op | source)
XLA Modules:
  0.0 266.8 jit_solution(11122958344873770910)
XLA Ops:
  0.7 3.0 %collective-permute-start.1 = (bf16[256,1024]{1,0:T(8,128)(2,1)}, bf16[256,1024]{1,0:T(8,128)(2,1)S(1)}, u32[]{:S(2)}, u32[]{:S(2)}) collective-permute-start(bf16[256,1024]{1,0:T(8,128)(2,1)} %refs_3_.1), channel_id=1, source_target_pairs={{0,16},{8,24},{16,0},{24,8},{1,17},{9,25},{17,1},{25,9},{2,18},{10... | collective-permute-start | bytes 1572872 | tf_op jit(solution)/shard_map/ppermute | solution.py:52
  5.8 7.8 %shard_map.345 = (bf16[256,1024]{1,0:T(8,128)(2,1)}, bf16[256,768]{1,0:T(8,128)(2,1)}, bf16[144,1024]{1,0:T(8,128)(2,1)}, bf16[128,768]{1,0:T(8,128)(2,1)}, bf16...) custom-call(s32[2]{0:T(128)} %pad_add_fusion.1.s_ref, ...), custom_call_target="tpu_custom_call" | custom-call | bytes 22400000 | tf_op jit(solution)/shard_map/pallas_call | solution.py:300
  13.6 2.3 collective-permute-done.1.refs_2_
  23.0 3.7 %collective-permute-done.3.refs_4_ = bf16[128,1024]{1,0:T(8,128)(2,1)S(1)} collective-permute-done((bf16[128,1024]{1,0:T(8,128)(2,1)S(1)}, bf16[128,1024]{1,0:T(8,128)(2,1)S(1)}, u32[]{:S(2)}, u32[]{:S(2)}) %collective-permute-start.3) | collective-permute-done | bytes 262176 | tf_op jit(solution)/shard_map/ppermute | solution.py:52
  28.7 4.2 %collective-permute-done.4.refs_6_ = bf16[144,1024]{1,0:T(8,128)(2,1)S(1)} collective-permute-done((bf16[144,1024]{1,0:T(8,128)(2,1)}, bf16[144,1024]{1,0:T(8,128)(2,1)S(1)}, u32[]{:S(2)}, u32[]{:S(2)}) %collective-permute-start.4) | collective-permute-done | bytes 294944 | tf_op jit(solution)/shard_map/ppermute | solution.py:52
  32.9 7.9 %collective-permute-done.5.refs_7_ = bf16[144,1024]{1,0:T(8,128)(2,1)S(1)} collective-permute-done((bf16[144,1024]{1,0:T(8,128)(2,1)}, bf16[144,1024]{1,0:T(8,128)(2,1)S(1)}, u32[]{:S(2)}, u32[]{:S(2)}) %collective-permute-start.5) | collective-permute-done | bytes 294944 | tf_op jit(solution)/shard_map/ppermute | solution.py:52
  45.0 6.4 %shard_map.346 = (bf16[1024,1024]{1,0:T(8,128)(2,1)S(1)}, bf16[1024,1024]{1,0:T(8,128)(2,1)S(1)}, bf16[1024,1024]{1,0:T(8,128)(2,1)S(1)}, f32[1024,1024]{1,0:T(8...) custom-call(s32[2]{0:T(128)S(1)} %copy-done.31, ...), custom_call_target="tpu_custom_call" | custom-call | bytes 20800000 | tf_op jit(solution)/shard_map/pallas_call | solution.py:391
  53.9 3.1 %shard_map.347 = (f32[1024,128]{1,0:T(8,128)S(1)}, f32[1024,128]{1,0:T(8,128)S(1)}) custom-call(s32[2]{0:T(128)S(1)} %copy-done.31, f32[4,8,128]{2,1,0:T(8,128)S(1)} %get-tuple-element.220.lens_ref.refs_5_.refs_4_), custom_call_target="tpu_custom_call" | custom-call | bytes 9600000 | tf_op jit(solution)/shard_map/pallas_call | solution.py:320
  56.9 4.3 %collective-permute-done.13.refs_4_ = bf16[128,1024]{1,0:T(8,128)(2,1)S(1)} collective-permute-done((bf16[128,1024]{1,0:T(8,128)(2,1)S(1)}, bf16[128,1024]{1,0:T(8,128)(2,1)S(1)}, u32[]{:S(2)}, u32[]{:S(2)}) %collective-permute-start.13) | collective-permute-done | bytes 262176 | tf_op jit(solution)/shard_map/ppermute | solution.py:52
  61.5 3.5 %shard_map.348 = (bf16[1024,1024]{1,0:T(8,128)(2,1)S(1)}, f32[8,1024]{1,0:T(8,128)S(1)}, bf16[512,1024]{1,0:T(8,128)(2,1)S(1)}, bf16[512,1024]{1,0:T(8,128)(2,1)S(1)}) custom-call(s32[2]{0:T(128)S(1)} %copy-done.31, bf16[256,1024]{1,0:T(8,128)(2,1)S(1)} %copy-done.13, bf16[256,1024]{1,0:T(8,128)(2,1)S(1)} %collective-permute-done.10.refs_1_, ...), custom_call_target="tpu_custom_call" | custom-call | bytes 11200000 | tf_op jit(solution)/shard_map/pallas_call | solution.py:428
  68.6 6.7 %shard_map.349 = (bf16[4,128,1024]{2,1,0:T(8,128)(2,1)S(1)}, bf16[4,128,1024]{2,1,0:T(8,128)(2,1)S(1)}, bf16[1024,1024]{1,0:T(8,128)(2,1)S(1)}, f32[8,1024]{1,0:T(8,128)S(1)}) custom-call(s32[2]{0:T(128)S(1)} %copy-done.31, bf16[1024,1024]{1,0:T(8,128)(2,1)S(1)} %get-tuple-element.251.branch_ref.refs_1_, f32[1024,1024]{1,0:T(8,128)S(1)} %get-tuple-element.229.slope_ref, ...), custom_call_target="tpu_custom_call" | custom-call | bytes 21760000 | tf_op jit(solution)/shard_map/pallas_call | solution.py:472
  75.5 2.4 collective-permute-done.16.refs_8_
  81.5 3.7 %collective-permute-start.22 = (bf16[512,1024]{1,0:T(8,128)(2,1)S(1)}, bf16[512,1024]{1,0:T(8,128)(2,1)S(1)}, u32[]{:S(2)}, u32[]{:S(2)}) collective-permute-start(bf16[512,1024]{1,0:T(8,128)(2,1)S(1)} %add.161.refs_0_), channel_id=1, source_target_pairs={{0,2},{1,3},{6,4},{7,5},{8,10},{9,11},{14,12},{15,13},{16,18},{17,... | collective-permute-start | bytes 3145736 | tf_op jit(solution)/shard_map/ppermute | solution.py:77
  88.8 11.2 %shard_map.350 = (bf16[1024,256]{1,0:T(8,128)(2,1)S(1)}, bf16[1024,768]{1,0:T(8,128)(2,1)S(1)}, f32[8,768]{1,0:T(8,128)S(1)}, bf16[1024,768]{1,0:T(8,128)(2,1)S(1)}) custom-call(s32[2]{0:T(128)S(1)} %copy-done.31, bf16[1024,1024]{1,0:T(8,128)(2,1)S(1)} %get-tuple-element.214.refs_0_.a_ref, bf16[1024,1024]{1,0:T(8,128)(2,1)S(1)} %get-tuple-element.251.branch_ref.refs_1_, ...), custom_call_target="tpu_custom_call" | custom-call | bytes 36160000 | tf_op jit(solution)/shard_map/pallas_call | solution.py:564
  101.7 3.9 %shard_map.351 = (bf16[128,1024]{1,0:T(8,128)(2,1)S(1)}, bf16[128,1024]{1,0:T(8,128)(2,1)S(1)}, bf16[4,128,768]{2,1,0:T(8,128)(2,1)S(1)}, bf16[4,128,768]{2,1,0:T(8,128)(2,1)S(1)}) custom-call(s32[2]{0:T(128)S(1)} %copy-done.31, bf16[1024,1024]{1,0:T(8,128)(2,1)S(1)} %get-tuple-element.214.refs_0_.a_ref, ...), custom_call_target="tpu_custom_call" | custom-call | bytes 12800000 | tf_op jit(solution)/shard_map/pallas_call | solution.py:660
  112.6 7.2 %collective-permute-start.28 = (bf16[4,128,1024]{2,1,0:T(8,128)(2,1)S(1)}, bf16[4,128,1024]{2,1,0:T(8,128)(2,1)}, u32[]{:S(2)}, u32[]{:S(2)}) collective-permute-start(bf16[4,128,1024]{2,1,0:T(8,128)(2,1)S(1)} %pad_maximum_fusion.refs_2_), channel_id=1, source_target_pairs={{0,2},{1,3},{6,4},{7,5},{8,10},{9,11},{14,12},{15,13},{16,18},{17,... | collective-permute-start | bytes 3145736 | tf_op jit(solution)/shard_map/ppermute | solution.py:77
  123.3 16.0 %shard_map.354 = (f32[256,2048]{1,0:T(8,128)}, bf16[256,2048]{1,0:T(8,128)(2,1)}, bf16[256,2048]{1,0:T(8,128)(2,1)}, bf16[256,2048]{1,0:T(8,128)(2,1)}, f32[16,1024]{1,0:T(8,128)}) custom-call(s32[2]{0:T(128)} %pad_add_fusion.1.s_ref, bf16[256,1024]{1,0:T(8,128)(2,1)} %refs_3_.1, bf16[256,1024]{1,0:T(8,128)(2,1)} %copy-done.6, bf16[256,1024]{1,0:T(8,128)(2,1)} %copy-done.5, ...), custom_call_target="tpu_custom_call" | custom-call | bytes 30080000 | tf_op jit(solution)/shard_map/pallas_call | solution.py:628
  149.7 5.4 %collective-permute-start.34 = (bf16[4,128,768]{2,1,0:T(8,128)(2,1)S(1)}, bf16[4,128,768]{2,1,0:T(8,128)(2,1)S(1)}, u32[]{:S(2)}, u32[]{:S(2)}) collective-permute-start(bf16[4,128,768]{2,1,0:T(8,128)(2,1)S(1)} %pad_maximum_fusion.1.refs_4_), channel_id=1, source_target_pairs={{0,2},{1,3},{6,4},{7,5},{8,10},{9,11},{14,12},{15,13},{16,18},{17,... | collective-permute-start | bytes 2359304 | tf_op jit(solution)/shard_map/ppermute | solution.py:77
  156.7 13.7 %collective-permute-done.34.refs_5_ = bf16[4,128,768]{2,1,0:T(8,128)(2,1)S(1)} collective-permute-done((bf16[4,128,768]{2,1,0:T(8,128)(2,1)S(1)}, bf16[4,128,768]{2,1,0:T(8,128)(2,1)S(1)}, u32[]{:S(2)}, u32[]{:S(2)}) %collective-permute-start.34) | collective-permute-done | bytes 786464 | tf_op jit(solution)/shard_map/ppermute | solution.py:77
  183.0 4.4 %collective-permute-start.43 = (bf16[144,1024]{1,0:T(8,128)(2,1)S(1)}, bf16[144,1024]{1,0:T(8,128)(2,1)S(1)}, u32[]{:S(2)}, u32[]{:S(2)}) collective-permute-start(bf16[144,1024]{1,0:T(8,128)(2,1)S(1)} %fusion.8.refs_4_), channel_id=1, source_target_pairs={{0,2},{1,3},{6,4},{7,5},{8,10},{9,11},{14,12},{15,13},{16,18},{17,... | collective-permute-start | bytes 884744 | tf_op jit(solution)/shard_map/ppermute | solution.py:77
  190.3 7.6 %multiply_subtract_fusion.1 = (f32[1024,1024]{1,0:T(8,128)}, f32[1024,1024]{1,0:T(8,128)}, f32[1024,1024]{1,0:T(8,128)}) fusion(f32[1024,1024]{1,0:T(8,128)S(1)} %copy-done.37, bf16[1024,1024]{1,0:T(8,128)(2,1)S(1)} %shard_map.357, f32[1024,1024]{1,0:T(8,128)S(1)} %copy-done.41, f32[1024,1024]{1,0:T(8,128)} %param.34), kind=kLoop, calls=%fused_computation.7 | loop fusion | flops 16777216 | bytes 27262976 | tf_op jit(solution)/shard_map/sub | solution.py:231
  197.9 2.6 convert_element_type.25
  200.5 14.5 %collective-permute-done.41.refs_1_ = bf16[4,128,1024]{2,1,0:T(8,128)(2,1)S(1)} collective-permute-done((bf16[4,128,1024]{2,1,0:T(8,128)(2,1)S(1)}, bf16[4,128,1024]{2,1,0:T(8,128)(2,1)S(1)}, u32[]{:S(2)}, u32[]{:S(2)}) %collective-permute-start.41) | collective-permute-done | bytes 1048608 | tf_op jit(solution)/shard_map/ppermute | solution.py:77
  215.9 2.6 collective-permute-done.45.refs_1_
  221.9 5.8 %multiply_subtract_fusion = (f32[256,4096]{1,0:T(8,128)}, f32[256,4096]{1,0:T(8,128)}, f32[256,4096]{1,0:T(8,128)}) fusion(f32[256,4096]{1,0:T(8,128)S(1)} %copy-done.38, bf16[256,4096]{1,0:T(8,128)(2,1)S(1)} %shard_map.359, f32[256,4096]{1,0:T(8,128)S(1)} %copy-done.42, f32[256,4096]{1,0:T(8,128)S(1)} %copy-done.43), kind=kLoop, calls=%fused_computation.5 | loop fusion | flops 16777216 | bytes 27262976 | tf_op jit(solution)/shard_map/sub | solution.py:231
  227.7 2.6 convert_element_type.26
  230.4 11.9 %collective-permute-done.46.refs_1_ = bf16[4,128,768]{2,1,0:T(8,128)(2,1)S(1)} collective-permute-done((bf16[4,128,768]{2,1,0:T(8,128)(2,1)S(1)}, bf16[4,128,768]{2,1,0:T(8,128)(2,1)S(1)}, u32[]{:S(2)}, u32[]{:S(2)}) %collective-permute-start.46) | collective-permute-done | bytes 786464 | tf_op jit(solution)/shard_map/ppermute | solution.py:77
  242.9 3.9 %collective-permute-done.48.refs_2_ = bf16[256,2048]{1,0:T(8,128)(2,1)S(1)} collective-permute-done((bf16[256,2048]{1,0:T(8,128)(2,1)S(1)}, bf16[256,2048]{1,0:T(8,128)(2,1)S(1)}, u32[]{:S(2)}, u32[]{:S(2)}) %collective-permute-start.48) | collective-permute-done | bytes 1048608 | tf_op jit(solution)/shard_map/ppermute | solution.py:52
  246.9 2.5 shard_map.362
  251.1 4.5 %multiply_subtract_fusion.2 = (f32[256,3072]{1,0:T(8,128)}, f32[256,3072]{1,0:T(8,128)}, f32[256,3072]{1,0:T(8,128)}) fusion(f32[256,3072]{1,0:T(8,128)S(1)} %copy-done.39, bf16[256,3072]{1,0:T(8,128)(2,1)S(1)} %shard_map.361, f32[256,3072]{1,0:T(8,128)S(1)} %copy-done.44, f32[256,3072]{1,0:T(8,128)S(1)} %copy-done.45), kind=kLoop, calls=%fused_computation.10 | loop fusion | flops 12582912 | bytes 20447232 | tf_op jit(solution)/shard_map/sub | solution.py:231
  257.7 4.9 %collective-permute-done.50.refs_1_ = bf16[144,1024]{1,0:T(8,128)(2,1)S(1)} collective-permute-done((bf16[144,1024]{1,0:T(8,128)(2,1)S(1)}, bf16[144,1024]{1,0:T(8,128)(2,1)S(1)}, u32[]{:S(2)}, u32[]{:S(2)}) %collective-permute-start.50) | collective-permute-done | bytes 294944 | tf_op jit(solution)/shard_map/ppermute | solution.py:77
  264.3 2.5 multiply_subtract_fusion.3
  (235 shorter events, 78.5 us)
Async XLA Ops:
  0.7 15.2 %collective-permute-start.1 = (bf16[256,1024]{1,0:T(8,128)(2,1)}, bf16[256,1024]{1,0:T(8,128)(2,1)S(1)}, u32[]{:S(2)}, u32[]{:S(2)}) collective-permute-start(bf16[256,1024]{1,0:T(8,128)(2,1)} %refs_3_.1), channel_id=1, source_target_pairs={{0,16},{8,24},{16,0},{24,8},{1,17},{9,25},{17,1},{25,9},{2,18},{10... | collective-permute-start | bytes 1572872 | tf_op jit(solution)/shard_map/ppermute | solution.py:52
  3.7 13.6 %collective-permute-start = (bf16[256,1024]{1,0:T(8,128)(2,1)}, bf16[256,1024]{1,0:T(8,128)(2,1)S(1)}, u32[]{:S(2)}, u32[]{:S(2)}) collective-permute-start(bf16[256,1024]{1,0:T(8,128)(2,1)} %refs_3_.1), channel_id=1, source_target_pairs={{0,8},{8,0},{16,24},{24,16},{1,9},{9,1},{17,25},{25,17},{2,10},{10... | collective-permute-start | bytes 1572872 | tf_op jit(solution)/shard_map/ppermute | solution.py:52
  19.5 13.5 %collective-permute-start.4 = (bf16[144,1024]{1,0:T(8,128)(2,1)}, bf16[144,1024]{1,0:T(8,128)(2,1)S(1)}, u32[]{:S(2)}, u32[]{:S(2)}) collective-permute-start(bf16[144,1024]{1,0:T(8,128)(2,1)} %get-tuple-element.211), channel_id=1, source_target_pairs={{0,8},{8,0},{16,24},{24,16},{1,9},{9,1},{17,25},{25,17},{2,10},{10... | collective-permute-start | bytes 884744 | tf_op jit(solution)/shard_map/ppermute | solution.py:52
  19.9 21.0 %collective-permute-start.5 = (bf16[144,1024]{1,0:T(8,128)(2,1)}, bf16[144,1024]{1,0:T(8,128)(2,1)S(1)}, u32[]{:S(2)}, u32[]{:S(2)}) collective-permute-start(bf16[144,1024]{1,0:T(8,128)(2,1)} %get-tuple-element.212), channel_id=1, source_target_pairs={{0,16},{8,24},{16,0},{24,8},{1,17},{9,25},{17,1},{25,9},{2,18},{10... | collective-permute-start | bytes 884744 | tf_op jit(solution)/shard_map/ppermute | solution.py:52
  21.5 19.3 %collective-permute-start.6 = (bf16[144,1024]{1,0:T(8,128)(2,1)}, bf16[144,1024]{1,0:T(8,128)(2,1)S(1)}, u32[]{:S(2)}, u32[]{:S(2)}) collective-permute-start(bf16[144,1024]{1,0:T(8,128)(2,1)} %get-tuple-element.213), channel_id=1, source_target_pairs={{0,24},{8,16},{16,8},{24,0},{1,25},{9,17},{17,9},{25,1},{2,26},{10... | collective-permute-start | bytes 884744 | tf_op jit(solution)/shard_map/ppermute | solution.py:52
  26.6 26.1 %collective-permute-start.11 = (bf16[256,1024]{1,0:T(8,128)(2,1)S(1)}, bf16[256,1024]{1,0:T(8,128)(2,1)S(1)}, u32[]{:S(2)}, u32[]{:S(2)}) collective-permute-start(bf16[256,1024]{1,0:T(8,128)(2,1)S(1)} %copy-done.13), channel_id=1, source_target_pairs={{0,16},{8,24},{16,0},{24,8},{1,17},{9,25},{17,1},{25,9},{2,18},{10... | collective-permute-start | bytes 1572872 | tf_op jit(solution)/shard_map/ppermute | solution.py:52
  28.2 24.5 %collective-permute-start.10 = (bf16[256,1024]{1,0:T(8,128)(2,1)S(1)}, bf16[256,1024]{1,0:T(8,128)(2,1)S(1)}, u32[]{:S(2)}, u32[]{:S(2)}) collective-permute-start(bf16[256,1024]{1,0:T(8,128)(2,1)S(1)} %copy-done.13), channel_id=1, source_target_pairs={{0,8},{8,0},{16,24},{24,16},{1,9},{9,1},{17,25},{25,17},{2,10},{10... | collective-permute-start | bytes 1572872 | tf_op jit(solution)/shard_map/ppermute | solution.py:52
  65.0 12.8 %collective-permute-start.14 = (bf16[512,1024]{1,0:T(8,128)(2,1)S(1)}, bf16[512,1024]{1,0:T(8,128)(2,1)S(1)}, u32[]{:S(2)}, u32[]{:S(2)}) collective-permute-start(bf16[512,1024]{1,0:T(8,128)(2,1)S(1)} %get-tuple-element.234), channel_id=1, source_target_pairs={{0,1},{1,0},{2,3},{3,2},{4,5},{5,4},{6,7},{7,6},{8,9},{9,8},{10,11... | collective-permute-start | bytes 3145736 | tf_op jit(solution)/shard_map/ppermute | solution.py:57
  66.6 11.2 %collective-permute-start.16 = (bf16[128,768]{1,0:T(8,128)(2,1)S(1)}, bf16[128,768]{1,0:T(8,128)(2,1)S(1)}, u32[]{:S(2)}, u32[]{:S(2)}) collective-permute-start(bf16[128,768]{1,0:T(8,128)(2,1)S(1)} %copy-done.54), channel_id=1, source_target_pairs={{0,16},{8,24},{16,0},{24,8},{1,17},{9,25},{17,1},{25,9},{2,18},{10... | collective-permute-start | bytes 589832 | tf_op jit(solution)/shard_map/ppermute | solution.py:52
  67.1 10.7 %collective-permute-start.17 = (bf16[128,768]{1,0:T(8,128)(2,1)S(1)}, bf16[128,768]{1,0:T(8,128)(2,1)S(1)}, u32[]{:S(2)}, u32[]{:S(2)}) collective-permute-start(bf16[128,768]{1,0:T(8,128)(2,1)S(1)} %copy-done.53), channel_id=1, source_target_pairs={{0,24},{8,16},{16,8},{24,0},{1,25},{9,17},{17,9},{25,1},{2,26},{10... | collective-permute-start | bytes 589832 | tf_op jit(solution)/shard_map/ppermute | solution.py:52
  81.5 26.2 %collective-permute-start.22 = (bf16[512,1024]{1,0:T(8,128)(2,1)S(1)}, bf16[512,1024]{1,0:T(8,128)(2,1)S(1)}, u32[]{:S(2)}, u32[]{:S(2)}) collective-permute-start(bf16[512,1024]{1,0:T(8,128)(2,1)S(1)} %add.161.refs_0_), channel_id=1, source_target_pairs={{0,2},{1,3},{6,4},{7,5},{8,10},{9,11},{14,12},{15,13},{16,18},{17,... | collective-permute-start | bytes 3145736 | tf_op jit(solution)/shard_map/ppermute | solution.py:77
  85.2 22.6 %collective-permute-start.23 = (bf16[128,1024]{1,0:T(8,128)(2,1)S(1)}, bf16[128,1024]{1,0:T(8,128)(2,1)S(1)}, u32[]{:S(2)}, u32[]{:S(2)}) collective-permute-start(bf16[128,1024]{1,0:T(8,128)(2,1)S(1)} %get-tuple-element.266), channel_id=1, source_target_pairs={{0,8},{8,0},{16,24},{24,16},{1,9},{9,1},{17,25},{25,17},{2,10},{10... | collective-permute-start | bytes 786440 | tf_op jit(solution)/shard_map/ppermute | solution.py:52
  85.8 22.0 %collective-permute-start.24 = (bf16[128,1024]{1,0:T(8,128)(2,1)S(1)}, bf16[128,1024]{1,0:T(8,128)(2,1)S(1)}, u32[]{:S(2)}, u32[]{:S(2)}) collective-permute-start(bf16[128,1024]{1,0:T(8,128)(2,1)S(1)} %get-tuple-element.267), channel_id=1, source_target_pairs={{0,16},{8,24},{16,0},{24,8},{1,17},{9,25},{17,1},{25,9},{2,18},{10... | collective-permute-start | bytes 786440 | tf_op jit(solution)/shard_map/ppermute | solution.py:52
  87.0 20.8 %collective-permute-start.25 = (bf16[128,1024]{1,0:T(8,128)(2,1)S(1)}, bf16[128,1024]{1,0:T(8,128)(2,1)S(1)}, u32[]{:S(2)}, u32[]{:S(2)}) collective-permute-start(bf16[128,1024]{1,0:T(8,128)(2,1)S(1)} %get-tuple-element.268), channel_id=1, source_target_pairs={{0,24},{8,16},{16,8},{24,0},{1,25},{9,17},{17,9},{25,1},{2,26},{10... | collective-permute-start | bytes 786440 | tf_op jit(solution)/shard_map/ppermute | solution.py:52
  111.0 28.4 %collective-permute-start.27 = (bf16[512,1024]{1,0:T(8,128)(2,1)S(1)}, bf16[512,1024]{1,0:T(8,128)(2,1)}, u32[]{:S(2)}, u32[]{:S(2)}) collective-permute-start(bf16[512,1024]{1,0:T(8,128)(2,1)S(1)} %shard_map.352.refs_0_), channel_id=1, source_target_pairs={{2,4},{3,5},{4,2},{5,3},{10,12},{11,13},{12,10},{13,11},{18,20},{1... | collective-permute-start | bytes 3145736 | tf_op jit(solution)/shard_map/ppermute | solution.py:77
  112.6 28.7 %collective-permute-start.28 = (bf16[4,128,1024]{2,1,0:T(8,128)(2,1)S(1)}, bf16[4,128,1024]{2,1,0:T(8,128)(2,1)}, u32[]{:S(2)}, u32[]{:S(2)}) collective-permute-start(bf16[4,128,1024]{2,1,0:T(8,128)(2,1)S(1)} %pad_maximum_fusion.refs_2_), channel_id=1, source_target_pairs={{0,2},{1,3},{6,4},{7,5},{8,10},{9,11},{14,12},{15,13},{16,18},{17,... | collective-permute-start | bytes 3145736 | tf_op jit(solution)/shard_map/ppermute | solution.py:77
  119.9 25.1 %collective-permute-start.29 = (bf16[128,768]{1,0:T(8,128)(2,1)}, bf16[128,768]{1,0:T(8,128)(2,1)S(1)}, u32[]{:S(2)}, u32[]{:S(2)}) collective-permute-start(bf16[128,768]{1,0:T(8,128)(2,1)} %get-tuple-element.285), channel_id=1, source_target_pairs={{0,8},{8,0},{16,24},{24,16},{1,9},{9,1},{17,25},{25,17},{2,10},{10... | collective-permute-start | bytes 589832 | tf_op jit(solution)/shard_map/ppermute | solution.py:52
  120.4 24.6 %collective-permute-start.30 = (bf16[128,768]{1,0:T(8,128)(2,1)}, bf16[128,768]{1,0:T(8,128)(2,1)S(1)}, u32[]{:S(2)}, u32[]{:S(2)}) collective-permute-start(bf16[128,768]{1,0:T(8,128)(2,1)} %get-tuple-element.286), channel_id=1, source_target_pairs={{0,16},{8,24},{16,0},{24,8},{1,17},{9,25},{17,1},{25,9},{2,18},{10... | collective-permute-start | bytes 589832 | tf_op jit(solution)/shard_map/ppermute | solution.py:52
  121.6 23.4 %collective-permute-start.31 = (bf16[128,768]{1,0:T(8,128)(2,1)}, bf16[128,768]{1,0:T(8,128)(2,1)}, u32[]{:S(2)}, u32[]{:S(2)}) collective-permute-start(bf16[128,768]{1,0:T(8,128)(2,1)} %get-tuple-element.287), channel_id=1, source_target_pairs={{0,24},{8,16},{16,8},{24,0},{1,25},{9,17},{17,9},{25,1},{2,26},{10... | collective-permute-start | bytes 589832 | tf_op jit(solution)/shard_map/ppermute | solution.py:52
  146.2 26.4 %collective-permute-start.32 = (bf16[512,1024]{1,0:T(8,128)(2,1)}, bf16[512,1024]{1,0:T(8,128)(2,1)S(1)}, u32[]{:S(2)}, u32[]{:S(2)}) collective-permute-start(bf16[512,1024]{1,0:T(8,128)(2,1)} %copy-done.20), channel_id=1, source_target_pairs={{2,0},{3,1},{4,6},{5,7},{10,8},{11,9},{12,14},{13,15},{18,16},{19,... | collective-permute-start | bytes 3145736 | tf_op jit(solution)/shard_map/ppermute | solution.py:77
  147.5 26.7 %collective-permute-start.33 = (bf16[4,128,1024]{2,1,0:T(8,128)(2,1)}, bf16[4,128,1024]{2,1,0:T(8,128)(2,1)}, u32[]{:S(2)}, u32[]{:S(2)}) collective-permute-start(bf16[4,128,1024]{2,1,0:T(8,128)(2,1)} %copy-done.22), channel_id=1, source_target_pairs={{2,4},{3,5},{4,2},{5,3},{10,12},{11,13},{12,10},{13,11},{18,20},{1... | collective-permute-start | bytes 3145736 | tf_op jit(solution)/shard_map/ppermute | solution.py:77
  149.1 30.5 %collective-permute-start.38 = (bf16[256,2048]{1,0:T(8,128)(2,1)}, bf16[256,2048]{1,0:T(8,128)(2,1)S(1)}, u32[]{:S(2)}, u32[]{:S(2)}) collective-permute-start(bf16[256,2048]{1,0:T(8,128)(2,1)} %get-tuple-element.320), channel_id=1, source_target_pairs={{0,8},{8,0},{16,24},{24,16},{1,9},{9,1},{17,25},{25,17},{2,10},{10... | collective-permute-start | bytes 3145736 | tf_op jit(solution)/shard_map/ppermute | solution.py:52
  149.7 20.7 %collective-permute-start.34 = (bf16[4,128,768]{2,1,0:T(8,128)(2,1)S(1)}, bf16[4,128,768]{2,1,0:T(8,128)(2,1)S(1)}, u32[]{:S(2)}, u32[]{:S(2)}) collective-permute-start(bf16[4,128,768]{2,1,0:T(8,128)(2,1)S(1)} %pad_maximum_fusion.1.refs_4_), channel_id=1, source_target_pairs={{0,2},{1,3},{6,4},{7,5},{8,10},{9,11},{14,12},{15,13},{16,18},{17,... | collective-permute-start | bytes 2359304 | tf_op jit(solution)/shard_map/ppermute | solution.py:77
  155.1 24.5 %collective-permute-start.35 = (f32[16,256]{1,0:T(8,128)S(1)}, f32[16,256]{1,0:T(8,128)S(1)}, u32[]{:S(2)}, u32[]{:S(2)}) collective-permute-start(f32[16,256]{1,0:T(8,128)S(1)} %get-tuple-element.317), channel_id=1, source_target_pairs={{0,8},{8,0},{16,24},{24,16},{1,9},{9,1},{17,25},{25,17},{2,10},{10... | collective-permute-start | bytes 49160 | tf_op jit(solution)/shard_map/ppermute | solution.py:52
  183.0 17.5 %collective-permute-start.43 = (bf16[144,1024]{1,0:T(8,128)(2,1)S(1)}, bf16[144,1024]{1,0:T(8,128)(2,1)S(1)}, u32[]{:S(2)}, u32[]{:S(2)}) collective-permute-start(bf16[144,1024]{1,0:T(8,128)(2,1)S(1)} %fusion.8.refs_4_), channel_id=1, source_target_pairs={{0,2},{1,3},{6,4},{7,5},{8,10},{9,11},{14,12},{15,13},{16,18},{17,... | collective-permute-start | bytes 884744 | tf_op jit(solution)/shard_map/ppermute | solution.py:77
  187.4 13.1 %collective-permute-start.42 = (bf16[4,128,768]{2,1,0:T(8,128)(2,1)S(1)}, bf16[4,128,768]{2,1,0:T(8,128)(2,1)S(1)}, u32[]{:S(2)}, u32[]{:S(2)}) collective-permute-start(bf16[4,128,768]{2,1,0:T(8,128)(2,1)S(1)} %get-tuple-element.340.refs_2_), channel_id=1, source_target_pairs={{2,4},{3,5},{4,2},{5,3},{10,12},{11,13},{12,10},{13,11},{18,20},{1... | collective-permute-start | bytes 2359304 | tf_op jit(solution)/shard_map/ppermute | solution.py:77
  188.2 26.8 %collective-permute-start.41 = (bf16[4,128,1024]{2,1,0:T(8,128)(2,1)S(1)}, bf16[4,128,1024]{2,1,0:T(8,128)(2,1)S(1)}, u32[]{:S(2)}, u32[]{:S(2)}) collective-permute-start(bf16[4,128,1024]{2,1,0:T(8,128)(2,1)S(1)} %get-tuple-element.339.refs_0_), channel_id=1, source_target_pairs={{2,0},{3,1},{4,6},{5,7},{10,8},{11,9},{12,14},{13,15},{18,16},{19,... | collective-permute-start | bytes 3145736 | tf_op jit(solution)/shard_map/ppermute | solution.py:77
  189.7 26.1 %collective-permute-start.44 = (bf16[256,2048]{1,0:T(8,128)(2,1)S(1)}, bf16[256,2048]{1,0:T(8,128)(2,1)S(1)}, u32[]{:S(2)}, u32[]{:S(2)}) collective-permute-start(bf16[256,2048]{1,0:T(8,128)(2,1)S(1)} %copy-done.52), channel_id=1, source_target_pairs={{0,16},{8,24},{16,0},{24,8},{1,17},{9,25},{17,1},{25,9},{2,18},{10... | collective-permute-start | bytes 3145736 | tf_op jit(solution)/shard_map/ppermute | solution.py:52
  218.6 11.7 %collective-permute-start.47 = (bf16[144,1024]{1,0:T(8,128)(2,1)S(1)}, bf16[144,1024]{1,0:T(8,128)(2,1)S(1)}, u32[]{:S(2)}, u32[]{:S(2)}) collective-permute-start(bf16[144,1024]{1,0:T(8,128)(2,1)S(1)} %get-tuple-element.354.refs_2_), channel_id=1, source_target_pairs={{2,4},{3,5},{4,2},{5,3},{10,12},{11,13},{12,10},{13,11},{18,20},{1... | collective-permute-start | bytes 884744 | tf_op jit(solution)/shard_map/ppermute | solution.py:77
  219.3 22.9 %collective-permute-start.46 = (bf16[4,128,768]{2,1,0:T(8,128)(2,1)S(1)}, bf16[4,128,768]{2,1,0:T(8,128)(2,1)S(1)}, u32[]{:S(2)}, u32[]{:S(2)}) collective-permute-start(bf16[4,128,768]{2,1,0:T(8,128)(2,1)S(1)} %get-tuple-element.353.refs_0_), channel_id=1, source_target_pairs={{2,0},{3,1},{4,6},{5,7},{10,8},{11,9},{12,14},{13,15},{18,16},{19,... | collective-permute-start | bytes 2359304 | tf_op jit(solution)/shard_map/ppermute | solution.py:77
  220.6 26.2 %collective-permute-start.48 = (bf16[256,2048]{1,0:T(8,128)(2,1)S(1)}, bf16[256,2048]{1,0:T(8,128)(2,1)S(1)}, u32[]{:S(2)}, u32[]{:S(2)}) collective-permute-start(bf16[256,2048]{1,0:T(8,128)(2,1)S(1)} %copy-done.51), channel_id=1, source_target_pairs={{0,24},{8,16},{16,8},{24,0},{1,25},{9,17},{17,9},{25,1},{2,26},{10... | collective-permute-start | bytes 3145736 | tf_op jit(solution)/shard_map/ppermute | solution.py:52
  249.6 12.9 %collective-permute-start.50 = (bf16[144,1024]{1,0:T(8,128)(2,1)S(1)}, bf16[144,1024]{1,0:T(8,128)(2,1)S(1)}, u32[]{:S(2)}, u32[]{:S(2)}) collective-permute-start(bf16[144,1024]{1,0:T(8,128)(2,1)S(1)} %get-tuple-element.363.refs_0_), channel_id=1, source_target_pairs={{2,0},{3,1},{4,6},{5,7},{10,8},{11,9},{12,14},{13,15},{18,16},{19,... | collective-permute-start | bytes 884744 | tf_op jit(solution)/shard_map/ppermute | solution.py:77
  (76 other events, 1080.8 us)

commit v3 on v2

--- a/solution.py
+++ b/solution.py
@@ -50,6 +50,21 @@
 def shard_swap(value, step):
     size = lax.axis_size("shard")
     return lax.ppermute(value, "shard", [(i, i ^ step) for i in range(size)])
+
+
+def exchange(stay, away):
+    size = lax.axis_size("shard")
+    rows = stay.shape[0] // (size // 2)
+    got = shard_swap(away, 1)
+    pieces = [(got if step % 2 else stay)[step // 2 * rows : (step // 2 + 1) * rows] for step in range(size)]
+    bit = 2
+    while bit < size:
+        sent = [step for step in range(size) if step & bit]
+        got = shard_swap(jnp.concatenate([pieces[step] for step in sent]), bit)
+        for i, step in enumerate(sent):
+            pieces[step] = got[i * rows : (i + 1) * rows]
+        bit *= 2
+    return pieces
 
 
 def core_swap(value):
@@ -131,6 +146,73 @@
     return stages[: half - 1], stages[half - 1 : half], stages[half:]
 
 
+def dp_round(sc, fresh, inner, total, upcoming=None, rows=None):
+    parts = chain_parts()
+    if lax.axis_size("dp") // 2 != 4:
+        moves = [(value, stages) for value, stages in zip((fresh, inner, total), parts, strict=True) if value is not None]
+        moved = iter(advance(*moves))
+        return [None if value is None else next(moved) for value in (fresh, inner, total)]
+    if fresh is None:
+        sent, pairs = total, [(1, 0), (2, 3)]
+    elif total is None:
+        sent, pairs = fresh, [(0, 1), (3, 2)]
+    else:
+        sent, pairs = total, [(0, 1), (1, 0), (2, 3), (3, 2)]
+    edge = place_send(sent, pairs)
+    centre = None if inner is None else place_send(inner, [(1, 2), (2, 1)])
+    arrays, shapes, steps = [], [], []
+
+    def plan(kind, items, shape):
+        steps.append((kind, len(arrays), len(shapes)))
+        arrays.extend(items)
+        shapes.append(shape)
+
+    if fresh is not None:
+        plan("sum", [fresh, edge], fresh)
+    if inner is not None and upcoming is None:
+        plan("sum", [inner, centre], inner)
+    if inner is not None and upcoming is not None:
+        plan("next", [inner, centre, upcoming], max(inner, upcoming, key=lambda item: item.shape[0]))
+    if total is not None:
+        shape = total if rows is None else jax.ShapeDtypeStruct((rows, total.shape[1]), total.dtype)
+        plan("last", [total, edge], shape)
+
+    def body(s_ref, *refs):
+        outs = refs[len(arrays) :]
+        for kind, at, place in steps:
+            value, got, out = refs[at], refs[at + 1], outs[place]
+            size = min(value.shape[0], out.shape[0])
+            if kind == "sum":
+                out[...] = value[...] + got[:size, :]
+                continue
+
+            @pl.when(s_ref[2] == 0)
+            def _(kind=kind, value=value, got=got, out=out, size=size):
+                out[:size, :] = value[:size, :] + got[:size, :] if kind == "next" else value[:size, :]
+
+            @pl.when(s_ref[2] > 0)
+            def _(kind=kind, got=got, out=out, at=at, size=size):
+                if kind == "next":
+                    out[: refs[at + 2].shape[0], :] = refs[at + 2][...]
+                else:
+                    out[...] = got[:size, :]
+
+    moved = iter(on_vmem(body, shapes, sc, arrays))
+    return [None if value is None else next(moved) for value in (fresh, inner, total)]
+
+
+def on_vmem(body, shapes, sc, arrays, limit=8):
+    vmem = pl.BlockSpec(memory_space=pltpu.VMEM)
+    return pl.pallas_call(
+        body,
+        out_shape=[jax.ShapeDtypeStruct(item.shape, item.dtype) for item in shapes],
+        in_specs=[pl.BlockSpec(memory_space=pltpu.SMEM)] + [vmem] * len(arrays),
+        out_specs=[vmem] * len(shapes),
+        compiler_params=pltpu.CompilerParams(vmem_limit_bytes=limit * MIB),
+        cost_estimate=pl.CostEstimate(flops=0, bytes_accessed=int(3.2e6), transcendentals=0),
+    )(sc, *arrays)
+
+
 def gather_rest(block, near):
     groups = lax.axis_size("shard")
     rows = block.shape[0]
@@ -149,15 +231,11 @@
     return pl.BlockSpec(memory_space=pltpu.VMEM)
 
 
-def block_of(shape):
-    return pl.BlockSpec(shape, lambda *_: (0,) * len(shape))
-
-
 def by_row(shape):
     return pl.BlockSpec(shape, lambda i, *_: (i,) + (0,) * (len(shape) - 1))
 
 
-def kernel_call(body, grid, in_specs, outs, scratch=(), time=1.0, limit=20):
+def kernel_call(body, grid, in_specs, outs, scratch=(), time=1.0, limit=12):
     return pl.pallas_call(
         body,
         out_shape=[jax.ShapeDtypeStruct(shape, dtype) for shape, dtype, _ in outs],
@@ -389,19 +467,17 @@
         ((groups, 8, LANES), F32, full((groups, 8, LANES))),
     ]
     return kernel_call(
-        body, (groups,), in_specs, outs, [pltpu.VMEM((rows, width), BF)], 6.5
+        body, (groups,), in_specs, outs, [pltpu.VMEM((rows, width), BF)], 6.5, 20
     )(sc, *flat(xs), own, *mine, *other, vectors, lengths)
 
 
-def grad_of_down(sc, cots, lens, act, slots, scale):
-    groups, n_c = len(cots), len(flat(cots))
+def mask_rows(sc, cots, lens, slots):
+    n_c = len(flat(cots))
     rows, width = cots[0][0].shape
-    ff = act.shape[1]
 
     def body(s_ref, *refs):
         cot_refs = iter(refs[:n_c])
-        lens_ref, act_ref, branch_ref, bias_ref, away_ref, keep_ref = refs[n_c:]
-        core = s_ref[1]
+        lens_ref, branch_ref, bias_ref = refs[n_c:]
         for step, pieces in enumerate(cots):
             _, ends = ends_of(lens_ref, step, slots)
             row = 0
@@ -415,24 +491,35 @@
                 row += size
                 if step == 0:
                     bias_ref[...] = jnp.broadcast_to(jnp.sum(branch, axis=0, keepdims=True), bias_ref.shape)
-        size = ff // 2
+
+    outs = [((len(cots) * rows, width), BF, full(None)), ((8, width), F32, full(None))]
+    in_specs = [full(item.shape) for item in flat(cots) + [lens]]
+    return kernel_call(body, (1,), in_specs, outs, (), 1.0)(sc, *flat(cots), lens)
+
+
+def grad_of_down(sc, branch, act, scale):
+    tok, width = branch.shape
+    size = act.shape[1] // 2
+
+    def body(s_ref, branch_ref, act_ref, away_ref, keep_ref):
+        core = s_ref[1]
         for ref, which in ((away_ref, 1 - core), (keep_ref, core)):
             ref[...] = (dot_lt(act_ref[:, part(which * size, size)], branch_ref[...]) * scale).astype(BF)
 
-    outs = [
-        ((groups * rows, width), BF, full((groups * rows, width))),
-        ((8, width), F32, full((8, width))),
-        ((ff // 2, width), BF, full((ff // 2, width))),
-        ((ff // 2, width), BF, full((ff // 2, width))),
-    ]
-    return kernel_call(
-        body,
-        (1,),
-        [full(item.shape) for item in flat(cots) + [lens, act]],
-        outs,
-        (),
-        3.5,
-    )(sc, *flat(cots), lens, act)
+    outs = [((size, width), BF, full(None))] * 2
+    return kernel_call(body, (1,), [full(branch.shape), full(act.shape)], outs, (), 3.0)(sc, branch, act)
+
+
+def feed_out(sc, act, w_down, groups):
+    tok, ff = act.shape
+    rows = tok // groups
+
+    def body(s_ref, act_ref, wd_ref, out_ref):
+        out_ref[...] = dot(act_ref[...], wd_ref[...]).astype(BF)
+
+    width = w_down.shape[1]
+    outs = [((tok, width), BF, by_row((rows, width)))]
+    return kernel_call(body, (groups,), [by_row((rows, ff)), full(None)], outs, (), 3.0)(sc, act, w_down)[0]
 
 
 def backward_up(sc, branch, slope, w_down, in_mlp, scale, groups):
@@ -561,26 +648,26 @@
         ((8, 3 * wide), F32, full((8, 3 * wide))),
         ((width, 3 * wide), BF, full((width, 3 * wide))),
     ]
-    return kernel_call(body, (groups,), in_specs, outs, (), 11.3)(
+    return kernel_call(body, (groups,), in_specs, outs, (), 0.0)(
         sc, in_attn, branch, cosine, sine, lens, vec, own, *mine, *other, w_out
     )
 
 
-def back_to_tokens(sc, xs, heads, act, d_proj, d_up, stats, vec, w_out, w_down, w_qkv, w_up, bias_up, bias_qkv, bias_out):
+def back_to_tokens(sc, xs, heads, mlp, d_proj, d_up, stats, vec, w_out, w_qkv, w_up, bias_up, bias_qkv, bias_out):
     groups, n_x = len(xs), len(flat(xs))
     rows, width = xs[0][0].shape
     wide = width // groups
-    ff = act.shape[1]
+    ff = d_up.shape[1]
 
     def body(s_ref, *refs):
         x_refs, refs = refs[:n_x], refs[n_x:]
         (
-            heads_ref, act_ref, proj_ref, d_up_ref, stats_ref, vec_ref, wo_ref, wd_ref, wq_ref, wu_ref,
+            heads_ref, mlp_ref, proj_ref, d_up_ref, stats_ref, vec_ref, wo_ref, wq_ref, wu_ref,
             up_ref, qkv_ref, out_ref,
-        ) = refs[:13]
-        own_ref = refs[13]
-        piece_refs = refs[14 : 13 + groups]
-        grad_ref, x_scr = refs[13 + groups :]
+        ) = refs[:12]
+        own_ref = refs[12]
+        piece_refs = refs[13 : 12 + groups]
+        grad_ref, x_scr = refs[12 + groups :]
         me = s_ref[0]
         block = pl.program_id(0)
         load_block(block, xs, x_refs, x_scr)
@@ -595,7 +682,7 @@
             grad_ref[pl.ds(9 + first // width, 1), part(lax.rem(me, width // ff) * ff, ff, LANES)] = up_ref[0:1, :]
 
         normed = (x_scr[...].astype(F32) - stats_ref[:, 0:1]) * stats_ref[:, 1:2]
-        branch_out = dot(heads_ref[...], wo_ref[...]) + dot(act_ref[...], wd_ref[...])
+        branch_out = dot(heads_ref[...], wo_ref[...]) + mlp_ref[...].astype(F32)
         total = None
         for row, left, right in ((0, proj_ref, wq_ref), (2, d_up_ref, wu_ref)):
             d_in = dot_rt(left[...], right[...])
@@ -606,8 +693,8 @@
 
         @pl.when(block == 0)
         def _():
-            own_ref[:, :width] = branch_out
-            own_ref[:, width:] = total
+            own_ref[:, :width] = branch_out.astype(BF)
+            own_ref[:, width:] = total.astype(BF)
 
         for step in range(1, groups):
 
@@ -616,13 +703,13 @@
                 piece_refs[step - 1][:, :width] = branch_out.astype(BF)
                 piece_refs[step - 1][:, width:] = total.astype(BF)
 
-    constant = [vec, w_out, w_down, w_qkv, w_up, bias_up, bias_qkv, bias_out]
+    constant = [vec, w_out, w_qkv, w_up, bias_up, bias_qkv, bias_out]
     in_specs = (
-        [block_of(item.shape) for item in flat(xs)]
-        + [by_row((rows, item.shape[1])) for item in (heads, act, d_proj, d_up, stats)]
-        + [block_of(item.shape) for item in constant]
-    )
-    outs = [((rows, 2 * width), F32, full((rows, 2 * width)))]
+        [full(item.shape) for item in flat(xs)]
+        + [by_row((rows, item.shape[1])) for item in (heads, mlp, d_proj, d_up, stats)]
+        + [full(item.shape) for item in constant]
+    )
+    outs = [((rows, 2 * width), BF, full((rows, 2 * width)))]
     outs += [((rows, 2 * width), BF, full((rows, 2 * width)))] * (groups - 1)
     outs += [((EXTRA, width), F32, full((EXTRA, width)))]
     got = kernel_call(
@@ -631,9 +718,8 @@
         in_specs,
         outs,
         [pltpu.VMEM((rows, width), BF)],
-        9.4,
-        58,
-    )(sc, *flat(xs), heads, act, d_proj, d_up, stats, *constant)
+        0.0,
+    )(sc, *flat(xs), heads, mlp, d_proj, d_up, stats, *constant)
     return got[0], got[1:groups], got[groups]
 
 
@@ -655,11 +741,48 @@
         out_keep[...], out_away[...] = halves(grad, core)
 
     ops = (in_attn, d_proj, heads, branch)
-    out = ((half, width), BF, full((half, width)))
-    qkv = ((groups, half, 3 * wide), BF, full((groups, half, 3 * wide)))
-    return kernel_call(
-        body, (1,), [full(item.shape) for item in ops], [out, out, qkv, qkv], (), 4.0
-    )(sc, *ops)
+    out = ((half, width), BF, full(None))
+    qkv = ((groups, half, 3 * wide), BF, full(None))
+    return kernel_call(body, (1,), [full(None)] * len(ops), [out, out, qkv, qkv], (), 0.0)(sc, *ops)
+
+
+def merge(sc, qkv_keep, qkv_got, vec_grad, scale):
+    groups, half, columns = qkv_keep.shape
+    wide = columns // 3
+    rows = half + EXTRA
+
+    def body(s_ref, keep_ref, got_ref, vec_ref, stay_ref, away_ref):
+        me = s_ref[0]
+        for i in range(groups):
+            ref, at = (away_ref if i % 2 else stay_ref), i // 2 * rows
+            ref[at : at + half, :] = keep_ref[i] + got_ref[i]
+            ref[at + half : at + rows, :] = jnp.zeros((EXTRA, columns), BF)
+            ref[at + half : at + rows, :wide] = (vec_ref[:, part((me ^ i) * wide, wide)] * scale).astype(BF)
+
+    shape = jax.ShapeDtypeStruct((groups // 2 * rows, columns), BF)
+    return on_vmem(body, [shape, shape], sc, [qkv_keep, qkv_got, vec_grad])
+
+
+def join(sc, qkv_rows, out_keep, out_got):
+    groups = len(qkv_rows)
+    half, width = out_keep.shape
+    wide = 2 * half
+    share = width // groups
+
+    def body(s_ref, *refs):
+        rows, (keep_ref, got_ref, out) = refs[:groups], refs[groups:]
+        vec = jnp.zeros((EXTRA, wide), F32)
+        out[groups * half :, :] = jnp.zeros((EXTRA, 3 * wide + share), BF)
+        for i in range(groups):
+            at = slice(i * half, (i + 1) * half)
+            columns = slice(i * share, (i + 1) * share)
+            out[at, : 3 * wide] = rows[i][:half, :]
+            out[at, 3 * wide :] = keep_ref[:, columns] + got_ref[:, columns]
+            vec = vec + rows[i][half:, :wide].astype(F32)
+        out[groups * half :, :wide] = vec.astype(BF)
+
+    shape = jax.ShapeDtypeStruct((groups * half + EXTRA, 3 * wide + share), BF)
+    return on_vmem(body, [shape], sc, [*qkv_rows, out_keep, out_got])[0]
 
 
 def finish(sc, own, got, tokens, cotangent, lens, stats, vec, slots):
@@ -668,8 +791,8 @@
     def body(s_ref, own_ref, *refs):
         got_refs = refs[: len(got)]
         tok_ref, cot_ref, lens_ref, stats_ref, vec_ref, out_ref, grad_ref = refs[len(got) :]
-        branch = own_ref[:, :width]
-        scaled = own_ref[:, width:]
+        branch = own_ref[:, :width].astype(F32)
+        scaled = own_ref[:, width:].astype(F32)
         for ref in got_refs:
             branch = branch + ref[:, :width].astype(F32)
             scaled = scaled + ref[:, width:].astype(F32)
@@ -697,21 +820,49 @@
     )
 
 
-def assemble(shape, arrays, plan):
+def assemble(shapes, arrays, plan):
     def body(*refs):
-        ins, out = refs[: len(arrays)], refs[len(arrays)]
+        ins, outs = refs[: len(arrays)], refs[len(arrays) :]
         me, core = lax.axis_index("shard"), lax.rem(lax.axis_index("dp"), 2)
-        for which, index, row, column, size in plan(me, core):
-            out[part(row, size[0]), part(column, size[1])] = ins[which][index]
-
+        for target, row, column, size, which, index in plan(me, core):
+            outs[target][part(row, size[0]), part(column, size[1])] = ins[which][index]
+
+    vmem = pl.BlockSpec(memory_space=pltpu.VMEM)
     return pl.pallas_call(
         body,
-        out_shape=jax.ShapeDtypeStruct(shape, arrays[0].dtype),
-        in_specs=[pl.BlockSpec(memory_space=pltpu.VMEM)] * len(arrays),
-        out_specs=pl.BlockSpec(memory_space=pltpu.VMEM),
-        compiler_params=pltpu.CompilerParams(vmem_limit_bytes=20 * MIB),
-        cost_estimate=pl.CostEstimate(flops=0, bytes_accessed=0, transcendentals=0),
+        out_shape=[jax.ShapeDtypeStruct(shape, arrays[0].dtype) for shape in shapes],
+        in_specs=[vmem] * len(arrays),
+        out_specs=[vmem] * len(shapes),
+        compiler_params=pltpu.CompilerParams(vmem_limit_bytes=8 * MIB),
+        cost_estimate=pl.CostEstimate(flops=0, bytes_accessed=int(3.2e6), transcendentals=0),
     )(*arrays)
+
+
+def adam_blocks(sc, grads, masters, grid, block, where, fill, time):
+    shape = masters[0].shape
+
+    def body(s_ref, *refs):
+        grad_refs = refs[: len(grads)]
+        w_ref, m_ref, v_ref, g_out, w_out, m_out, v_out = refs[len(grads) :]
+        fill(s_ref, grad_refs, g_out)
+        w_out[...], m_out[...], v_out[...] = adam_terms(
+            w_ref[...], m_ref[...], v_ref[...], g_out[...], DECAY_RATE, LEARN_RATE
+        )
+
+    spec = pl.BlockSpec(block, where)
+    return kernel_call(
+        body, grid, [full(None)] * len(grads) + [spec] * 3, [(shape, F32, spec)] * 4, (), time, 30
+    )(sc, *grads, *masters)
+
+
+def choose(condition, yes, no, out):
+    @pl.when(condition)
+    def _():
+        out[...] = yes().astype(F32)
+
+    @pl.when(jnp.logical_not(condition))
+    def _():
+        out[...] = no().astype(F32)
 
 
 def adam(masters, grad, decay=DECAY_RATE, rate=LEARN_RATE):
@@ -737,11 +888,13 @@
     n_vec = vectors.shape[0]
     slots = lengths.shape[1]
     others = range(1, groups)
-    sc = jnp.stack([me, core]).astype(jnp.int32)
+    places = lax.axis_size("dp") // 2
+    place = lax.axis_index("dp") // 2
+    outer = (place == 0) | (place == places - 1)
+    sc = jnp.stack([me, core, outer]).astype(jnp.int32)
     scale = float(rows * groups * lax.axis_size("dp")) ** (-0.5)
 
     size = ff // 2
-    inward, across, outward = chain_parts()
     fence = lax.optimization_barrier
 
     up_parts, qkv_parts, down_w, out_w = pack(groups, sc, w_up, w_qkv, w_down, w_out, vectors, lengths)
@@ -749,7 +902,7 @@
     near, up_parts = fence((near, up_parts))
     up_mine = [shard_swap(item, step) for item, step in zip(up_parts[1:], others, strict=True)]
     xs = gather_rest(tokens, near)
-    cot_near = [shard_swap(after(cotangent, near), step) for step in (1, 2)]
+    cot_near = [shard_swap(after(cotangent, xs[3]), step) for step in (1, 2)]
     up_other = [core_swap(item) for item in up_mine]
     in_attn, in_mlp, act, slope, stats, up_w, vec, lens = forward_up(
         sc, xs, up_parts[0], up_mine, up_other, vectors, lengths
@@ -757,112 +910,99 @@
     cot_near, act = fence((cot_near, act))
     cots = gather_rest(cotangent, cot_near)
     qkv_mine = [shard_swap(item, step) for item, step in zip(after(qkv_parts[1:], cot_near), others, strict=True)]
-    cosine, sine = tables(sc, after(lens, cot_near), groups, rows, slots)
+    mlp = feed_out(sc, after(act, cot_near), down_w, groups)
+    cosine, sine = tables(sc, after(lens, mlp), groups, rows, slots)
     cots, cosine = fence((cots, cosine))
 
-    branch, bias_out, down_away, down_keep = grad_of_down(sc, cots, lens, act, slots, scale)
-    down_got = core_swap(down_away)
+    branch, bias_out = mask_rows(sc, cots, lens, slots)
     up_away, up_keep, d_up, bias_up = backward_up(sc, branch, slope, down_w, in_mlp, scale, groups)
-    down_got, d_up, up_away, qkv_mine = fence((down_got, d_up, up_away, qkv_mine))
-    down = down_keep + down_got
+    up_away, up_keep, qkv_mine, branch = fence((up_away, up_keep, qkv_mine, branch))
     up_got = core_swap(up_away)
     qkv_other = [core_swap(item) for item in qkv_mine]
-    down, up_got, qkv_other, branch_a = fence((down, up_got, qkv_other, branch))
+    down_away, down_keep = grad_of_down(sc, branch, act, scale)
+    down_away, down_keep, up_got, qkv_other = fence((down_away, down_keep, up_got, qkv_other))
+    down_got = core_swap(down_away)
     up_sums = [up_keep[i] + up_got[i] for i in range(groups)]
-    up_sums, down, branch_a = fence((up_sums, down, branch_a))
-
-    [down] = advance((down, inward))
+    up_sums, down_got = fence((up_sums, down_got))
+    down = down_keep + down_got
+    down, branch_a = fence((down, branch))
+
+    down, _, _ = dp_round(sc, down, None, None)
     up_rows = [up_sums[0]] + [shard_swap(up_sums[step], step) for step in others]
     heads, d_proj, bias_qkv, qkv_w = attention(
         sc, in_attn, branch_a, cosine, sine, lens, vec, qkv_parts[0], qkv_mine, qkv_other, out_w, groups, slots
     )
+    up_rows, d_proj = fence((up_rows, d_proj))
     out_away, out_keep, qkv_away, qkv_keep = grads_of_attention(sc, in_attn, d_proj, heads, branch, scale, groups)
-    down, up_rows, qkv_away, out_away = fence((down, up_rows, qkv_away, out_away))
+    out_away, qkv_away, d_proj = fence((out_away, qkv_away, d_proj))
     qkv_got = core_swap(qkv_away)
-    up = jnp.stack(up_rows)
-    qkv_got, up, down = fence((qkv_got, up, down))
-    qkv_sums = [qkv_keep[i] + qkv_got[i] for i in range(groups)]
-    qkv_sums, up, down, d_proj = fence((qkv_sums, up, down, d_proj))
-
-    down, up = advance((down, across), (up, inward))
-    qkv_rows = [qkv_sums[0]] + [shard_swap(qkv_sums[step], step) for step in others]
+    out_got = core_swap(out_away)
     own, pieces, vec_grad = back_to_tokens(
-        sc, xs, heads, act, d_proj, d_up, stats, vec, out_w, down_w, qkv_w, up_w, bias_up, bias_qkv, bias_out
-    )
-    down, up, qkv_rows, vec_grad, pieces = fence((down, up, qkv_rows, vec_grad, pieces))
-    qkv = jnp.stack(qkv_rows)
-    vec_grad = (vec_grad * scale).reshape(EXTRA, groups, wide)
-    vec_parts = [lax.dynamic_index_in_dim(vec_grad, me ^ step, 1, keepdims=False) for step in range(groups)]
-    down, up, qkv, vec_parts, pieces = fence((down, up, qkv, vec_parts, pieces))
-
-    down, up, qkv = advance((down, outward), (up, across), (qkv, inward))
-    vec_rows = [vec_parts[0]] + [shard_swap(vec_parts[step], step) for step in others]
-    got = [shard_swap(pieces[0], 1)]
-    down, up, qkv, vec_rows, got, pieces = fence((down, up, qkv, vec_rows, got, pieces))
-    vec_sum = jnp.pad(sum(vec_rows).astype(BF), ((0, 0), (0, width - wide)))
-    out_away, out_keep = (jnp.concatenate([item, vec_sum]) for item in (out_away, out_keep))
-    out_got = core_swap(out_away)
+        sc, xs, heads, mlp, d_proj, d_up, stats, vec, out_w, qkv_w, up_w, bias_up, bias_qkv, bias_out
+    )
+    down, up_rows, qkv_got, out_got, vec_grad = fence((down, up_rows, qkv_got, out_got, vec_grad))
+    up = jnp.concatenate(up_rows)
+    stay, away = merge(sc, qkv_keep, qkv_got, vec_grad, scale)
+    up, down, stay, away = fence((up, down, stay, away))
+
+    qkv_rows = exchange(stay, away)
+    rest = join(sc, qkv_rows, out_keep, out_got)
+    up, down, _ = dp_round(sc, up, down, None, rest)
+    down, up, rest, pieces = fence((down, up, rest, pieces))
+
+    rest, up, down = dp_round(sc, rest, up, down, rows=size)
+    got = [shard_swap(item, step) for item, step in zip(pieces[:2], (1, 2), strict=True)]
+    down, up, rest, got, pieces = fence((down, up, rest, got, pieces))
+
     down_other = core_swap(down)
-    out_got, down_other, up, qkv, pieces = fence((out_got, down_other, up, qkv, pieces))
-    out = out_keep + out_got
-    out, down_other, up, qkv, pieces = fence((out, down_other, up, qkv, pieces))
-
-    up, qkv, out = advance((up, outward), (qkv, across), (out, inward))
-    got.append(shard_swap(pieces[1], 2))
-    down_grad = assemble(
-        (ff, width),
-        [down, down_other],
-        lambda me, core: [(side, slice(None), (core ^ side) * size, 0, (size, width)) for side in range(2)],
-    )
-    new_down = adam((w_down, m_down, v_down), down_grad)
-    up, qkv, out, new_down, got, pieces = fence((up, qkv, out, new_down, got, pieces))
+    _, rest, up = dp_round(sc, None, rest, up)
+    got += [shard_swap(item, step) for item, step in zip(pieces[2:], others[2:], strict=True)]
+
+    def fill_down(s_ref, refs, out):
+        step = pl.program_id(0)
+        at = part((step % 2) * (size // 2), size // 2)
+        choose(step // 2 == s_ref[1], lambda: refs[0][at, :], lambda: refs[1][at, :], out)
+
+    new_down = adam_blocks(
+        sc, [down, down_other], (w_down, m_down, v_down),
+        (4,), (size // 2, width), lambda i, s: (i, 0), fill_down, 0.0,
+    )
+    up, rest, new_down, got = fence((up, rest, new_down, got))
+
     up_other = core_swap(up)
-    up_other, qkv, out, pieces = fence((up_other, qkv, out, pieces))
-
-    qkv, out = advance((qkv, outward), (out, across))
-    got += [shard_swap(item, step) for item, step in zip(pieces[2:], others[2:], strict=True)]
-    up_grad = assemble(
-        (wide, hidden),
-        [up, up_other],
-        lambda me, core: [
-            (side, step, (core ^ side) * half, (me ^ step) * ff, (half, ff))
-            for side in range(2)
-            for step in range(groups)
-        ],
-    )
-    new_up = adam((w_up, m_up, v_up), up_grad)
-    qkv, out, new_up, got = fence((qkv, out, new_up, got))
-    qkv_other = core_swap(qkv)
-    qkv_other, out = fence((qkv_other, out))
-
-    [out] = advance((out, outward))
-    qkv_grad = assemble(
-        (wide, 3 * width),
-        [qkv, qkv_other],
-        lambda me, core: [
-            (
-                side,
-                (step, slice(None), slice(p * wide, (p + 1) * wide)),
-                (core ^ side) * half,
-                p * width + (me ^ step) * wide,
-                (half, wide),
-            )
-            for side in range(2)
-            for step in range(groups)
-            for p in range(3)
-        ],
-    )
-    new_qkv = adam((w_qkv, m_qkv, v_qkv), qkv_grad)
+    _, _, rest = dp_round(sc, None, None, rest)
+
+    def fill_up(s_ref, refs, out):
+        at = part((s_ref[0] ^ pl.program_id(1)) * half, half)
+        choose(pl.program_id(0) == s_ref[1], lambda: refs[0][at, :], lambda: refs[1][at, :], out)
+
+    new_up = adam_blocks(
+        sc, [up, up_other], (w_up, m_up, v_up),
+        (2, groups), (half, ff), lambda i, j, s: (i, j), fill_up, 0.0,
+    )
     output, input_grad = finish(sc, own, got, tokens, cotangent, lens, stats, vec, slots)
-    out, new_qkv, output, input_grad = fence((out, new_qkv, output, input_grad))
-    out_other = core_swap(out)
-    out_grad = jnp.where(
-        (jnp.arange(2) == core)[:, None, None], out[None, :half], out_other[None, :half]
-    ).reshape(wide, width)
-    vec_total = out[half : half + n_vec, :wide]
+    rest, new_up, output, input_grad = fence((rest, new_up, output, input_grad))
+    rest_other = core_swap(rest)
+
+    def rest_plan(me, core):
+        plan = []
+        for side in range(2):
+            row = (core ^ side) * half
+            for step in range(groups):
+                at = slice(step * half, (step + 1) * half)
+                for p in range(3):
+                    columns = slice(p * wide, (p + 1) * wide)
+                    plan.append((0, row, p * width + (me ^ step) * wide, (half, wide), side, (at, columns)))
+                columns = slice(3 * wide, 4 * wide)
+                plan.append((1, row, step * wide, (half, wide), side, (at, columns)))
+        return plan
+
+    qkv_grad, out_grad = assemble([(wide, 3 * width), (wide, width)], [rest, rest_other], rest_plan)
+    vec_rows = slice(groups * half, groups * half + n_vec)
+    vec_total = rest[vec_rows, :wide].astype(F32) + rest_other[vec_rows, :wide].astype(F32)
 
     news = (
-        new_qkv,
+        adam((w_qkv, m_qkv, v_qkv), qkv_grad),
         adam((w_out, m_out, v_out), out_grad),
         new_up,
         new_down,

time: 268 us -> 234 us (0.87)
  other arithmetic: 32.5 us -> 9.85 us
  starting transfers between devices: 62.7 us -> 45.3 us
  local copies, waits for them, and re-layouts: 12 us -> 1.33 us
  Pallas kernels: 66.7 us -> 77 us
  waiting for transfers between devices: 91.3 us -> 99 us
    pallas_call x12 -> x15, Pallas kernels: 24.2 us -> 43.2 us  [the longest x2 14.9 us: adam_blocks(): kernel_call(body, grid, [full(None)] * len(grads) + [spec] * 3, [(shape,...]
    ppermute x12 -> x8, starting transfers between devices: 31 us -> 15.1 us  [place_send(): lax.ppermute(value, 'dp', [(2 * a + core, 2 * b + core) for a, b in pairs...]
    sub x5 -> x3, other arithmetic: 21.2 us -> 8.57 us  [adam_terms(): return (weight - rate * (step_size + decay * weight), first_new, second_new)]
    unnamed x112 -> x52, local copies, waits for them, and re-layouts: 11.7 us -> 1.17 us
    pallas_call x1, Pallas kernels: 16 us -> 7.22 us  [back_to_tokens(): kernel_call(body, (groups,), in_specs, outs, [pltpu.VMEM((rows, width), B...]
    convert_element_type x4 -> x0, other arithmetic: 8.12 us -> none  [the longest x3 7.24 us: adam(): grad = grad.astype(F32)]
    ppermute x12 -> x8, waiting for transfers between devices: 48.9 us -> 55 us  [place_send(): lax.ppermute(value, 'dp', [(2 * a + core, 2 * b + core) for a, b in pairs...]
    ppermute x26 -> x22, waiting for transfers between devices: 31.5 us -> 37.2 us  [shard_swap(): return lax.ppermute(value, 'shard', [(i, i ^ step) for i in range(size)])]
  transfers between devices with their start and end apart: 52 -> 43, of which waited for: 26 -> 18; matrix products, arithmetic and copies ran while one was open for 11% -> 1% of each run, Pallas kernels for 24% -> 32%
where the time goes in v3:
time: 234 us
  waiting for transfers between devices  99 us (42%)
  Pallas kernels  77 us (33%)
  starting transfers between devices  45.3 us (19%)
  other arithmetic  9.85 us (4%)
    ppermute x8, waiting for transfers between devices, place_send(): lax.ppermute(value, 'dp', [(2 * a + core, 2 * b + core) for a, b in pairs...  55 us
    ppermute x22, waiting for transfers between devices, shard_swap(): return lax.ppermute(value, 'shard', [(i, i ^ step) for i in range(size)])  37.2 us
    ppermute x22, starting transfers between devices, shard_swap(): return lax.ppermute(value, 'shard', [(i, i ^ step) for i in range(size)])  27.7 us
    ppermute x8, starting transfers between devices, place_send(): lax.ppermute(value, 'dp', [(2 * a + core, 2 * b + core) for a, b in pairs...  15.1 us
    pallas_call x2, Pallas kernels, adam_blocks(): kernel_call(body, grid, [full(None)] * len(grads) + [spec] * 3, [(shape,...  14.9 us
    pallas_call x1, Pallas kernels, attention(): kernel_call(body, (groups,), in_specs, outs, (), 0.0)  11.4 us
    sub x3, other arithmetic, adam_terms(): return (weight - rate * (step_size + decay * weight), first_new, second_new)  8.57 us
    pallas_call x1, Pallas kernels, pack(): kernel_call(body, (1,), in_specs, outs, scratch, 7.0, 60)  7.78 us
  transfers between devices with their start and end apart: 43, of which 18 were waited for; matrix products, arithmetic and copies ran while one was open for 1% of the time, Pallas kernels for 32%

profile of v3, /device:TPU:0, one launch (start us, length us, event | category | flops | bytes accessed | tf_op | source)
XLA Modules:
  0.0 233.8 jit_solution(11405015670076269449)
XLA Ops:
  0.7 3.0 %collective-permute-start = (bf16[256,1024]{1,0:T(8,128)(2,1)}, bf16[256,1024]{1,0:T(8,128)(2,1)S(1)}, u32[]{:S(2)}, u32[]{:S(2)}) collective-permute-start(bf16[256,1024]{1,0:T(8,128)(2,1)} %refs_3_.5), channel_id=1, source_target_pairs={{0,8},{8,0},{16,24},{24,16},{1,9},{9,1},{17,25},{25,17},{2,10},{10... | collective-permute-start | bytes 1572872 | tf_op jit(solution)/shard_map/ppermute | solution.py:52
  5.8 7.8 %shard_map.345 = (bf16[256,1024]{1,0:T(8,128)(2,1)}, bf16[256,768]{1,0:T(8,128)(2,1)}, bf16[144,1024]{1,0:T(8,128)(2,1)}, bf16[128,768]{1,0:T(8,128)(2,1)}, bf16...) custom-call(s32[3]{0:T(128)} %pad_add_fusion.s_ref, ...), custom_call_target="tpu_custom_call" | custom-call | bytes 22400000 | tf_op jit(solution)/shard_map/pallas_call | solution.py:378
  13.6 2.2 collective-permute-done.refs_1_
  17.3 1.6 collective-permute-start.2
  19.8 2.6 %collective-permute-start.8 = (bf16[144,1024]{1,0:T(8,128)(2,1)}, bf16[144,1024]{1,0:T(8,128)(2,1)S(1)}, u32[]{:S(2)}, u32[]{:S(2)}) collective-permute-start(bf16[144,1024]{1,0:T(8,128)(2,1)} %get-tuple-element.182), channel_id=1, source_target_pairs={{0,24},{8,16},{16,8},{24,0},{1,25},{9,17},{17,9},{25,1},{2,26},{10... | collective-permute-start | bytes 884744 | tf_op jit(solution)/shard_map/ppermute | solution.py:52
  23.0 8.3 %collective-permute-done.2.refs_3_ = bf16[128,1024]{1,0:T(8,128)(2,1)S(1)} collective-permute-done((bf16[128,1024]{1,0:T(8,128)(2,1)S(1)}, bf16[128,1024]{1,0:T(8,128)(2,1)S(1)}, u32[]{:S(2)}, u32[]{:S(2)}) %collective-permute-start.2) | collective-permute-done | bytes 262176 | tf_op jit(solution)/shard_map/ppermute | solution.py:52
  31.7 1.7 collective-permute-start.5
  33.4 5.9 %collective-permute-done.7.refs_7_ = bf16[144,1024]{1,0:T(8,128)(2,1)S(1)} collective-permute-done((bf16[144,1024]{1,0:T(8,128)(2,1)}, bf16[144,1024]{1,0:T(8,128)(2,1)S(1)}, u32[]{:S(2)}, u32[]{:S(2)}) %collective-permute-start.7) | collective-permute-done | bytes 294944 | tf_op jit(solution)/shard_map/ppermute | solution.py:52
  43.5 6.5 %shard_map.346 = (bf16[1024,1024]{1,0:T(8,128)(2,1)S(1)}, bf16[1024,1024]{1,0:T(8,128)(2,1)S(1)}, bf16[1024,1024]{1,0:T(8,128)(2,1)S(1)}, f32[1024,1024]{1,0:T(8...) custom-call(s32[3]{0:T(128)S(1)} %copy-done.12, ...), custom_call_target="tpu_custom_call" | custom-call | bytes 20800000 | tf_op jit(solution)/shard_map/pallas_call | solution.py:469
  55.0 3.4 %shard_map.347.refs_6_ = bf16[1024,1024]{1,0:T(8,128)(2,1)S(1)} custom-call(s32[3]{0:T(128)S(1)} %copy-done.12, bf16[1024,1024]{1,0:T(8,128)(2,1)S(1)} %get-tuple-element.188.act_ref, bf16[1024,1024]{1,0:T(8,128)(2,1)S(1)} %copy-done.2), custom_call_target="tpu_custom_call" | custom-call | bytes 9600000 | tf_op jit(solution)/shard_map/pallas_call | solution.py:522
  58.5 3.1 %shard_map.348 = (f32[1024,128]{1,0:T(8,128)S(1)}, f32[1024,128]{1,0:T(8,128)S(1)}) custom-call(s32[3]{0:T(128)S(1)} %copy-done.12, f32[4,8,128]{2,1,0:T(8,128)S(1)} %get-tuple-element.190.lens_ref.refs_5_.refs_4_), custom_call_target="tpu_custom_call" | custom-call | bytes 9600000 | tf_op jit(solution)/shard_map/pallas_call | solution.py:398
  62.7 6.8 %shard_map.350 = (bf16[4,128,1024]{2,1,0:T(8,128)(2,1)S(1)}, bf16[4,128,1024]{2,1,0:T(8,128)(2,1)S(1)}, bf16[1024,1024]{1,0:T(8,128)(2,1)S(1)}, f32[8,1024]{1,0:T(8,128)S(1)}) custom-call(s32[3]{0:T(128)S(1)} %copy-done.12, bf16[1024,1024]{1,0:T(8,128)(2,1)S(1)} %get-tuple-element.226.branch_ref.refs_1_, f32[1024,1024]{1,0:T(8,128)S(1)} %get-tuple-element.198.slope_ref, ...), custom_call_target="tpu_custom_call" | custom-call | bytes 21760000 | tf_op jit(solution)/shard_map/pallas_call | solution.py:559
  70.5 2.9 %shard_map.351 = (bf16[512,1024]{1,0:T(8,128)(2,1)S(1)}, bf16[512,1024]{1,0:T(8,128)(2,1)S(1)}) custom-call(s32[3]{0:T(128)S(1)} %copy-done.12, bf16[1024,1024]{1,0:T(8,128)(2,1)S(1)} %get-tuple-element.226.branch_ref.refs_1_, bf16[1024,1024]{1,0:T(8,128)(2,1)S(1)} %get-tuple-element.188.act_ref), custom_call_target="tpu_custom_call" | custom-call | bytes 9600000 | tf_op jit(solution)/shard_map/pallas_call | solution.py:510
  73.9 2.4 %collective-permute-done.21 = bf16[512,1024]{1,0:T(8,128)(2,1)S(1)} collective-permute-done((bf16[512,1024]{1,0:T(8,128)(2,1)S(1)}, bf16[512,1024]{1,0:T(8,128)(2,1)S(1)}, u32[]{:S(2)}, u32[]{:S(2)}) %collective-permute-start.21) | collective-permute-done | bytes 1048608 | tf_op jit(solution)/shard_map/ppermute | solution.py:72
  80.2 3.7 %collective-permute-start.22 = (bf16[512,1024]{1,0:T(8,128)(2,1)S(1)}, bf16[512,1024]{1,0:T(8,128)(2,1)S(1)}, u32[]{:S(2)}, u32[]{:S(2)}) collective-permute-start(bf16[512,1024]{1,0:T(8,128)(2,1)S(1)} %add.89.refs_0_), channel_id=1, source_target_pairs={{0,2},{1,3},{6,4},{7,5},{8,10},{9,11},{14,12},{15,13},{16,18},{17,... | collective-permute-start | bytes 3145736 | tf_op jit(solution)/shard_map/ppermute | solution.py:92
  83.9 11.4 %shard_map.353 = (bf16[1024,256]{1,0:T(8,128)(2,1)S(1)}, bf16[1024,768]{1,0:T(8,128)(2,1)S(1)}, f32[8,768]{1,0:T(8,128)S(1)}, bf16[1024,768]{1,0:T(8,128)(2,1)S(1)}) custom-call(s32[3]{0:T(128)S(1)} %copy-done.12, bf16[1024,1024]{1,0:T(8,128)(2,1)S(1)} %get-tuple-element.225.refs_0_.a_ref, bf16[1024,1024]{1,0:T(8,128)(2,1)S(1)} %get-tuple-element.226.branch_ref.refs_1_, ...), custom_call_target="tpu_custom_call" | custom-call | tf_op jit(solution)/shard_map/pallas_call | solution.py:651
  95.4 4.0 %shard_map.354 = (bf16[128,1024]{1,0:T(8,128)(2,1)S(1)}, bf16[128,1024]{1,0:T(8,128)(2,1)S(1)}, bf16[4,128,768]{2,1,0:T(8,128)(2,1)S(1)}, bf16[4,128,768]{2,1,0:T(8,128)(2,1)S(1)}) custom-call(s32[3]{0:T(128)S(1)} %copy-done.12, bf16[1024,1024]{1,0:T(8,128)(2,1)S(1)} %get-tuple-element.225.refs_0_.a_ref, ...), custom_call_target="tpu_custom_call" | custom-call | tf_op jit(solution)/shard_map/pallas_call | solution.py:746
  100.0 7.2 %shard_map.355 = (bf16[256,2048]{1,0:T(8,128)(2,1)S(1)}, bf16[256,2048]{1,0:T(8,128)(2,1)S(1)}, bf16[256,2048]{1,0:T(8,128)(2,1)S(1)}, bf16[256,2048]{1,0:T(8,128)(2,1)S(1)}, f32[16,1024]{1,0:T(8,128)S(1)}) custom-call(s32[3]{0:T(128)S(1)} %copy-done.12, bf16[256,1024]{1,0:T(8,128)(2,1)S(1)} %copy-done.3, ...), custom_call_target="tpu_custom_call" | custom-call | tf_op jit(solution)/shard_map/pallas_call | solution.py:715
  110.2 2.8 %collective-permute-start.28 = (bf16[512,1024]{1,0:T(8,128)(2,1)S(1)}, bf16[512,1024]{1,0:T(8,128)(2,1)S(1)}, u32[]{:S(2)}, u32[]{:S(2)}) collective-permute-start(bf16[512,1024]{1,0:T(8,128)(2,1)S(1)} %pad_maximum_fusion.refs_0_), channel_id=1, source_target_pairs={{0,2},{1,3},{6,4},{7,5},{8,10},{9,11},{14,12},{15,13},{16,18},{17,... | collective-permute-start | bytes 3145736 | tf_op jit(solution)/shard_map/ppermute | solution.py:92
  113.7 7.1 %collective-permute-done.30 = bf16[288,768]{1,0:T(8,128)(2,1)S(1)} collective-permute-done((bf16[288,768]{1,0:T(8,128)(2,1)S(1)}, bf16[288,768]{1,0:T(8,128)(2,1)S(1)}, u32[]{:S(2)}, u32[]{:S(2)}) %collective-permute-start.30) | collective-permute-done | bytes 442400 | tf_op jit(solution)/shard_map/ppermute | solution.py:52
  122.3 10.0 %collective-permute-done.31 = bf16[288,768]{1,0:T(8,128)(2,1)S(1)} collective-permute-done((bf16[288,768]{1,0:T(8,128)(2,1)S(1)}, bf16[288,768]{1,0:T(8,128)(2,1)S(1)}, u32[]{:S(2)}, u32[]{:S(2)}) %collective-permute-start.31) | collective-permute-done | bytes 442400 | tf_op jit(solution)/shard_map/ppermute | solution.py:52
  134.9 3.6 %collective-permute-start.32 = (bf16[528,1024]{1,0:T(8,128)(2,1)S(1)}, bf16[528,1024]{1,0:T(8,128)(2,1)S(1)}, u32[]{:S(2)}, u32[]{:S(2)}) collective-permute-start(bf16[528,1024]{1,0:T(8,128)(2,1)S(1)} %get-tuple-element.277.refs_4_), channel_id=1, source_target_pairs={{0,2},{1,3},{2,0},{3,1},{4,6},{5,7},{6,4},{7,5},{8,10},{9,11},{10,... | collective-permute-start | bytes 3244040 | tf_op jit(solution)/shard_map/ppermute | solution.py:92
  141.1 18.8 %collective-permute-done.32.refs_1_.refs_5_ = bf16[528,1024]{1,0:T(8,128)(2,1)S(1)} collective-permute-done((bf16[528,1024]{1,0:T(8,128)(2,1)S(1)}, bf16[528,1024]{1,0:T(8,128)(2,1)S(1)}, u32[]{:S(2)}, u32[]{:S(2)}) %collective-permute-start.32) | collective-permute-done | bytes 1081376 | tf_op jit(solution)/shard_map/ppermute | solution.py:92
  163.8 2.3 collective-permute-start.39
  166.2 6.9 %shard_map.361 = (f32[1024,1024]{1,0:T(8,128)}, f32[1024,1024]{1,0:T(8,128)}, f32[1024,1024]{1,0:T(8,128)}, f32[1024,1024]{1,0:T(8,128)}) custom-call(s32[3]{0:T(128)S(1)} %copy-done.12, bf16[512,1024]{1,0:T(8,128)(2,1)S(1)} %get-tuple-element.289.refs_0_, bf16[512,1024]{1,0:T(8,128)(2,1)S(1)} %collective-permute-done.38.refs_1_, f32[1024,1024]{1,0:T(8,128)S(1)} %copy-done, ...), custom_call_target="tpu_custom_call" | custom-call | tf_op jit(solution)/shard_map/pallas_call | solution.py:853
  173.1 19.5 %collective-permute-done.37.refs_3_ = bf16[512,1024]{1,0:T(8,128)(2,1)S(1)} collective-permute-done((bf16[512,1024]{1,0:T(8,128)(2,1)S(1)}, bf16[512,1024]{1,0:T(8,128)(2,1)S(1)}, u32[]{:S(2)}, u32[]{:S(2)}) %collective-permute-start.37) | collective-permute-done | bytes 1048608 | tf_op jit(solution)/shard_map/ppermute | solution.py:92
  195.0 2.5 %shard_map.364 = (bf16[256,1024]{1,0:T(8,128)(2,1)}, bf16[256,1024]{1,0:T(8,128)(2,1)}) custom-call(s32[3]{0:T(128)S(1)} %copy-done.12, bf16[256,2048]{1,0:T(8,128)(2,1)S(1)} %get-tuple-element.303.own_ref, bf16[256,2048]{1,0:T(8,128)(2,1)S(1)} %collective-permute-done.34.refs_0_, bf16[256,2048]{1,0:T(8,128)(2,1)S(1)} %collective-permute-done.35.refs_1_, ...), custom_call_target="tpu_custom_call" | custom-call | bytes 7680000 | tf_op jit(solution)/shard_map/pallas_call | solution.py:818
  197.7 8.0 %shard_map.363 = (f32[256,4096]{1,0:T(8,128)}, f32[256,4096]{1,0:T(8,128)}, f32[256,4096]{1,0:T(8,128)}, f32[256,4096]{1,0:T(8,128)}) custom-call(s32[3]{0:T(128)S(1)} %copy-done.12, bf16[512,1024]{1,0:T(8,128)(2,1)S(1)} %get-tuple-element.298.refs_0_, bf16[512,1024]{1,0:T(8,128)(2,1)S(1)} %collective-permute-done.41.refs_1_, f32[256,4096]{1,0:T(8,128)S(1)} %copy-done.1, ...), custom_call_target="tpu_custom_call" | custom-call | tf_op jit(solution)/shard_map/pallas_call | solution.py:853
  205.7 15.5 %collective-permute-done.40.refs_1_ = bf16[528,1024]{1,0:T(8,128)(2,1)S(1)} collective-permute-done((bf16[528,1024]{1,0:T(8,128)(2,1)S(1)}, bf16[528,1024]{1,0:T(8,128)(2,1)S(1)}, u32[]{:S(2)}, u32[]{:S(2)}) %collective-permute-start.40) | collective-permute-done | bytes 1081376 | tf_op jit(solution)/shard_map/ppermute | solution.py:92
  222.2 2.7 %collective-permute-done.42.refs_1_ = bf16[528,1024]{1,0:T(8,128)(2,1)S(1)} collective-permute-done((bf16[528,1024]{1,0:T(8,128)(2,1)S(1)}, bf16[528,1024]{1,0:T(8,128)(2,1)S(1)}, u32[]{:S(2)}, u32[]{:S(2)}) %collective-permute-start.42) | collective-permute-done | bytes 1081376 | tf_op jit(solution)/shard_map/ppermute | solution.py:72
  225.2 5.6 %multiply_subtract_fusion = (f32[256,3072]{1,0:T(8,128)}, f32[256,3072]{1,0:T(8,128)}, f32[256,3072]{1,0:T(8,128)}, f32[256,3072]{1,0:T(8,128)}) fusion(f32[256,3072]{1,0:T(8,128)S(1)} %copy-done.15, f32[256,3072]{1,0:T(8,128)S(1)} %copy-done.17, f32[256,3072]{1,0:T(8,128)S(1)} %copy-done.18, bf16[256,3072]{1,0:T(8,128)(2,1)S(1)} %get-tuple-element.312), kind=kLoop, calls=%fused_computation.2 | loop fusion | flops 12582912 | bytes 23592960 | tf_op jit(solution)/shard_map/sub | solution.py:309
  230.8 2.3 multiply_subtract_fusion.1
  (142 shorter events, 40.3 us)
Async XLA Ops:
  0.7 15.1 %collective-permute-start = (bf16[256,1024]{1,0:T(8,128)(2,1)}, bf16[256,1024]{1,0:T(8,128)(2,1)S(1)}, u32[]{:S(2)}, u32[]{:S(2)}) collective-permute-start(bf16[256,1024]{1,0:T(8,128)(2,1)} %refs_3_.5), channel_id=1, source_target_pairs={{0,8},{8,0},{16,24},{24,16},{1,9},{9,1},{17,25},{25,17},{2,10},{10... | collective-permute-start | bytes 1572872 | tf_op jit(solution)/shard_map/ppermute | solution.py:52
  3.7 13.6 %collective-permute-start.1 = (bf16[256,1024]{1,0:T(8,128)(2,1)}, bf16[256,1024]{1,0:T(8,128)(2,1)S(1)}, u32[]{:S(2)}, u32[]{:S(2)}) collective-permute-start(bf16[256,1024]{1,0:T(8,128)(2,1)} %refs_3_.5), channel_id=1, source_target_pairs={{0,16},{8,24},{16,0},{24,8},{1,17},{9,25},{17,1},{25,9},{2,18},{10... | collective-permute-start | bytes 1572872 | tf_op jit(solution)/shard_map/ppermute | solution.py:52
  17.3 14.0 %collective-permute-start.2 = (bf16[128,1024]{1,0:T(8,128)(2,1)S(1)}, bf16[128,1024]{1,0:T(8,128)(2,1)S(1)}, u32[]{:S(2)}, u32[]{:S(2)}) collective-permute-start(bf16[128,1024]{1,0:T(8,128)(2,1)S(1)} %slice.60), channel_id=1, source_target_pairs={{0,16},{8,24},{16,0},{24,8},{1,17},{9,25},{17,1},{25,9},{2,18},{10... | collective-permute-start | bytes 786440 | tf_op jit(solution)/shard_map/ppermute | solution.py:52
  18.9 12.4 %collective-permute-start.3 = (bf16[128,1024]{1,0:T(8,128)(2,1)S(1)}, bf16[128,1024]{1,0:T(8,128)(2,1)S(1)}, u32[]{:S(2)}, u32[]{:S(2)}) collective-permute-start(bf16[128,1024]{1,0:T(8,128)(2,1)S(1)} %slice.61), channel_id=1, source_target_pairs={{0,8},{8,0},{16,24},{24,16},{1,9},{9,1},{17,25},{25,17},{2,10},{10... | collective-permute-start | bytes 786440 | tf_op jit(solution)/shard_map/ppermute | solution.py:52
  19.5 19.7 %collective-permute-start.7 = (bf16[144,1024]{1,0:T(8,128)(2,1)}, bf16[144,1024]{1,0:T(8,128)(2,1)S(1)}, u32[]{:S(2)}, u32[]{:S(2)}) collective-permute-start(bf16[144,1024]{1,0:T(8,128)(2,1)} %get-tuple-element.181), channel_id=1, source_target_pairs={{0,16},{8,24},{16,0},{24,8},{1,17},{9,25},{17,1},{25,9},{2,18},{10... | collective-permute-start | bytes 884744 | tf_op jit(solution)/shard_map/ppermute | solution.py:52
  19.8 19.4 %collective-permute-start.8 = (bf16[144,1024]{1,0:T(8,128)(2,1)}, bf16[144,1024]{1,0:T(8,128)(2,1)S(1)}, u32[]{:S(2)}, u32[]{:S(2)}) collective-permute-start(bf16[144,1024]{1,0:T(8,128)(2,1)} %get-tuple-element.182), channel_id=1, source_target_pairs={{0,24},{8,16},{16,8},{24,0},{1,25},{9,17},{17,9},{25,1},{2,26},{10... | collective-permute-start | bytes 884744 | tf_op jit(solution)/shard_map/ppermute | solution.py:52
  22.4 18.4 %collective-permute-start.6 = (bf16[144,1024]{1,0:T(8,128)(2,1)}, bf16[144,1024]{1,0:T(8,128)(2,1)S(1)}, u32[]{:S(2)}, u32[]{:S(2)}) collective-permute-start(bf16[144,1024]{1,0:T(8,128)(2,1)} %get-tuple-element.180), channel_id=1, source_target_pairs={{0,8},{8,0},{16,24},{24,16},{1,9},{9,1},{17,25},{25,17},{2,10},{10... | collective-permute-start | bytes 884744 | tf_op jit(solution)/shard_map/ppermute | solution.py:52
  31.3 18.8 %collective-permute-start.4 = (bf16[256,1024]{1,0:T(8,128)(2,1)S(1)}, bf16[256,1024]{1,0:T(8,128)(2,1)S(1)}, u32[]{:S(2)}, u32[]{:S(2)}) collective-permute-start(bf16[256,1024]{1,0:T(8,128)(2,1)S(1)} %copy-done.8), channel_id=1, source_target_pairs={{0,8},{8,0},{16,24},{24,16},{1,9},{9,1},{17,25},{25,17},{2,10},{10... | collective-permute-start | bytes 1572872 | tf_op jit(solution)/shard_map/ppermute | solution.py:52
  31.7 18.4 %collective-permute-start.5 = (bf16[256,1024]{1,0:T(8,128)(2,1)S(1)}, bf16[256,1024]{1,0:T(8,128)(2,1)S(1)}, u32[]{:S(2)}, u32[]{:S(2)}) collective-permute-start(bf16[256,1024]{1,0:T(8,128)(2,1)S(1)} %copy-done.8), channel_id=1, source_target_pairs={{0,16},{8,24},{16,0},{24,8},{1,17},{9,25},{17,1},{25,9},{2,18},{10... | collective-permute-start | bytes 1572872 | tf_op jit(solution)/shard_map/ppermute | solution.py:52
  50.1 11.4 %collective-permute-start.12 = (bf16[128,1024]{1,0:T(8,128)(2,1)S(1)}, bf16[128,1024]{1,0:T(8,128)(2,1)S(1)}, u32[]{:S(2)}, u32[]{:S(2)}) collective-permute-start(bf16[128,1024]{1,0:T(8,128)(2,1)S(1)} %slice.62), channel_id=1, source_target_pairs={{0,16},{8,24},{16,0},{24,8},{1,17},{9,25},{17,1},{25,9},{2,18},{10... | collective-permute-start | bytes 786440 | tf_op jit(solution)/shard_map/ppermute | solution.py:52
  50.9 10.6 %collective-permute-start.13 = (bf16[128,1024]{1,0:T(8,128)(2,1)S(1)}, bf16[128,1024]{1,0:T(8,128)(2,1)S(1)}, u32[]{:S(2)}, u32[]{:S(2)}) collective-permute-start(bf16[128,1024]{1,0:T(8,128)(2,1)S(1)} %slice.63), channel_id=1, source_target_pairs={{0,8},{8,0},{16,24},{24,16},{1,9},{9,1},{17,25},{25,17},{2,10},{10... | collective-permute-start | bytes 786440 | tf_op jit(solution)/shard_map/ppermute | solution.py:52
  51.5 17.9 %collective-permute-start.14 = (bf16[128,768]{1,0:T(8,128)(2,1)S(1)}, bf16[128,768]{1,0:T(8,128)(2,1)S(1)}, u32[]{:S(2)}, u32[]{:S(2)}) collective-permute-start(bf16[128,768]{1,0:T(8,128)(2,1)S(1)} %copy-done.25), channel_id=1, source_target_pairs={{0,8},{8,0},{16,24},{24,16},{1,9},{9,1},{17,25},{25,17},{2,10},{10... | collective-permute-start | bytes 589832 | tf_op jit(solution)/shard_map/ppermute | solution.py:52
  53.0 16.4 %collective-permute-start.15 = (bf16[128,768]{1,0:T(8,128)(2,1)S(1)}, bf16[128,768]{1,0:T(8,128)(2,1)S(1)}, u32[]{:S(2)}, u32[]{:S(2)}) collective-permute-start(bf16[128,768]{1,0:T(8,128)(2,1)S(1)} %copy-done.24), channel_id=1, source_target_pairs={{0,16},{8,24},{16,0},{24,8},{1,17},{9,25},{17,1},{25,9},{2,18},{10... | collective-permute-start | bytes 589832 | tf_op jit(solution)/shard_map/ppermute | solution.py:52
  54.3 15.1 %collective-permute-start.16 = (bf16[128,768]{1,0:T(8,128)(2,1)S(1)}, bf16[128,768]{1,0:T(8,128)(2,1)S(1)}, u32[]{:S(2)}, u32[]{:S(2)}) collective-permute-start(bf16[128,768]{1,0:T(8,128)(2,1)S(1)} %copy-done.23), channel_id=1, source_target_pairs={{0,24},{8,16},{16,8},{24,0},{1,25},{9,17},{17,9},{25,1},{2,26},{10... | collective-permute-start | bytes 589832 | tf_op jit(solution)/shard_map/ppermute | solution.py:52
  69.5 4.1 %collective-permute-start.17 = (bf16[4,128,1024]{2,1,0:T(8,128)(2,1)S(1)}, bf16[4,128,1024]{2,1,0:T(8,128)(2,1)S(1)}, u32[]{:S(2)}, u32[]{:S(2)}) collective-permute-start(bf16[4,128,1024]{2,1,0:T(8,128)(2,1)S(1)} %get-tuple-element.211), channel_id=1, source_target_pairs={{0,1},{1,0},{2,3},{3,2},{4,5},{5,4},{6,7},{7,6},{8,9},{9,8},{10,11... | collective-permute-start | bytes 3145736 | tf_op jit(solution)/shard_map/ppermute | solution.py:72
  76.3 19.1 %collective-permute-start.23 = (bf16[128,1024]{1,0:T(8,128)(2,1)S(1)}, bf16[128,1024]{1,0:T(8,128)(2,1)S(1)}, u32[]{:S(2)}, u32[]{:S(2)}) collective-permute-start(bf16[128,1024]{1,0:T(8,128)(2,1)S(1)} %get-tuple-element.222), channel_id=1, source_target_pairs={{0,8},{8,0},{16,24},{24,16},{1,9},{9,1},{17,25},{25,17},{2,10},{10... | collective-permute-start | bytes 786440 | tf_op jit(solution)/shard_map/ppermute | solution.py:52
  77.8 17.6 %collective-permute-start.24 = (bf16[128,1024]{1,0:T(8,128)(2,1)S(1)}, bf16[128,1024]{1,0:T(8,128)(2,1)S(1)}, u32[]{:S(2)}, u32[]{:S(2)}) collective-permute-start(bf16[128,1024]{1,0:T(8,128)(2,1)S(1)} %get-tuple-element.223), channel_id=1, source_target_pairs={{0,16},{8,24},{16,0},{24,8},{1,17},{9,25},{17,1},{25,9},{2,18},{10... | collective-permute-start | bytes 786440 | tf_op jit(solution)/shard_map/ppermute | solution.py:52
  79.1 16.3 %collective-permute-start.25 = (bf16[128,1024]{1,0:T(8,128)(2,1)S(1)}, bf16[128,1024]{1,0:T(8,128)(2,1)S(1)}, u32[]{:S(2)}, u32[]{:S(2)}) collective-permute-start(bf16[128,1024]{1,0:T(8,128)(2,1)S(1)} %get-tuple-element.224), channel_id=1, source_target_pairs={{0,24},{8,16},{16,8},{24,0},{1,25},{9,17},{17,9},{25,1},{2,26},{10... | collective-permute-start | bytes 786440 | tf_op jit(solution)/shard_map/ppermute | solution.py:52
  80.2 27.0 %collective-permute-start.22 = (bf16[512,1024]{1,0:T(8,128)(2,1)S(1)}, bf16[512,1024]{1,0:T(8,128)(2,1)S(1)}, u32[]{:S(2)}, u32[]{:S(2)}) collective-permute-start(bf16[512,1024]{1,0:T(8,128)(2,1)S(1)} %add.89.refs_0_), channel_id=1, source_target_pairs={{0,2},{1,3},{6,4},{7,5},{8,10},{9,11},{14,12},{15,13},{16,18},{17,... | collective-permute-start | bytes 3145736 | tf_op jit(solution)/shard_map/ppermute | solution.py:92
  99.4 8.5 %collective-permute-start.26 = (bf16[4,128,768]{2,1,0:T(8,128)(2,1)S(1)}, bf16[4,128,768]{2,1,0:T(8,128)(2,1)S(1)}, u32[]{:S(2)}, u32[]{:S(2)}) collective-permute-start(bf16[4,128,768]{2,1,0:T(8,128)(2,1)S(1)} %get-tuple-element.244), channel_id=1, source_target_pairs={{0,1},{1,0},{2,3},{3,2},{4,5},{5,4},{6,7},{7,6},{8,9},{9,8},{10,11... | collective-permute-start | bytes 2359304 | tf_op jit(solution)/shard_map/ppermute | solution.py:72
  99.5 8.4 %collective-permute-start.27 = (bf16[128,1024]{1,0:T(8,128)(2,1)S(1)}, bf16[128,1024]{1,0:T(8,128)(2,1)S(1)}, u32[]{:S(2)}, u32[]{:S(2)}) collective-permute-start(bf16[128,1024]{1,0:T(8,128)(2,1)S(1)} %get-tuple-element.245), channel_id=1, source_target_pairs={{0,1},{1,0},{2,3},{3,2},{4,5},{5,4},{6,7},{7,6},{8,9},{9,8},{10,11... | collective-permute-start | bytes 786440 | tf_op jit(solution)/shard_map/ppermute | solution.py:72
  108.6 12.2 %collective-permute-start.30 = (bf16[288,768]{1,0:T(8,128)(2,1)S(1)}, bf16[288,768]{1,0:T(8,128)(2,1)S(1)}, u32[]{:S(2)}, u32[]{:S(2)}) collective-permute-start(bf16[288,768]{1,0:T(8,128)(2,1)S(1)} %get-tuple-element.268), channel_id=1, source_target_pairs={{0,8},{8,0},{16,24},{24,16},{1,9},{9,1},{17,25},{25,17},{2,10},{10... | collective-permute-start | bytes 1327112 | tf_op jit(solution)/shard_map/ppermute | solution.py:52
  110.2 23.9 %collective-permute-start.28 = (bf16[512,1024]{1,0:T(8,128)(2,1)S(1)}, bf16[512,1024]{1,0:T(8,128)(2,1)S(1)}, u32[]{:S(2)}, u32[]{:S(2)}) collective-permute-start(bf16[512,1024]{1,0:T(8,128)(2,1)S(1)} %pad_maximum_fusion.refs_0_), channel_id=1, source_target_pairs={{0,2},{1,3},{6,4},{7,5},{8,10},{9,11},{14,12},{15,13},{16,18},{17,... | collective-permute-start | bytes 3145736 | tf_op jit(solution)/shard_map/ppermute | solution.py:92
  113.0 21.2 %collective-permute-start.29 = (bf16[512,1024]{1,0:T(8,128)(2,1)S(1)}, bf16[512,1024]{1,0:T(8,128)(2,1)S(1)}, u32[]{:S(2)}, u32[]{:S(2)}) collective-permute-start(bf16[512,1024]{1,0:T(8,128)(2,1)S(1)} %shard_map.352.refs_2_), channel_id=1, source_target_pairs={{2,4},{3,5},{4,2},{5,3},{10,12},{11,13},{12,10},{13,11},{18,20},{1... | collective-permute-start | bytes 3145736 | tf_op jit(solution)/shard_map/ppermute | solution.py:92
  120.9 11.4 %collective-permute-start.31 = (bf16[288,768]{1,0:T(8,128)(2,1)S(1)}, bf16[288,768]{1,0:T(8,128)(2,1)S(1)}, u32[]{:S(2)}, u32[]{:S(2)}) collective-permute-start(bf16[288,768]{1,0:T(8,128)(2,1)S(1)} %pad_maximum_fusion.1), channel_id=1, source_target_pairs={{0,16},{8,24},{16,0},{24,8},{1,17},{9,25},{17,1},{25,9},{2,18},{10... | collective-permute-start | bytes 1327112 | tf_op jit(solution)/shard_map/ppermute | solution.py:52
  134.9 25.0 %collective-permute-start.32 = (bf16[528,1024]{1,0:T(8,128)(2,1)S(1)}, bf16[528,1024]{1,0:T(8,128)(2,1)S(1)}, u32[]{:S(2)}, u32[]{:S(2)}) collective-permute-start(bf16[528,1024]{1,0:T(8,128)(2,1)S(1)} %get-tuple-element.277.refs_4_), channel_id=1, source_target_pairs={{0,2},{1,3},{2,0},{3,1},{4,6},{5,7},{6,4},{7,5},{8,10},{9,11},{10,... | collective-permute-start | bytes 3244040 | tf_op jit(solution)/shard_map/ppermute | solution.py:92
  139.2 22.3 %collective-permute-start.34 = (bf16[256,2048]{1,0:T(8,128)(2,1)S(1)}, bf16[256,2048]{1,0:T(8,128)(2,1)S(1)}, u32[]{:S(2)}, u32[]{:S(2)}) collective-permute-start(bf16[256,2048]{1,0:T(8,128)(2,1)S(1)} %get-tuple-element.282), channel_id=1, source_target_pairs={{0,8},{8,0},{16,24},{24,16},{1,9},{9,1},{17,25},{25,17},{2,10},{10... | collective-permute-start | bytes 3145736 | tf_op jit(solution)/shard_map/ppermute | solution.py:52
  139.8 21.9 %collective-permute-start.35 = (bf16[256,2048]{1,0:T(8,128)(2,1)S(1)}, bf16[256,2048]{1,0:T(8,128)(2,1)S(1)}, u32[]{:S(2)}, u32[]{:S(2)}) collective-permute-start(bf16[256,2048]{1,0:T(8,128)(2,1)S(1)} %get-tuple-element.283), channel_id=1, source_target_pairs={{0,16},{8,24},{16,0},{24,8},{1,17},{9,25},{17,1},{25,9},{2,18},{10... | collective-permute-start | bytes 3145736 | tf_op jit(solution)/shard_map/ppermute | solution.py:52
  161.7 30.9 %collective-permute-start.36 = (bf16[528,1024]{1,0:T(8,128)(2,1)S(1)}, bf16[528,1024]{1,0:T(8,128)(2,1)S(1)}, u32[]{:S(2)}, u32[]{:S(2)}) collective-permute-start(bf16[528,1024]{1,0:T(8,128)(2,1)S(1)} %get-tuple-element.285.refs_0_), channel_id=1, source_target_pairs={{2,4},{3,5},{4,2},{5,3},{10,12},{11,13},{12,10},{13,11},{18,20},{1... | collective-permute-start | bytes 3244040 | tf_op jit(solution)/shard_map/ppermute | solution.py:92
  162.5 30.1 %collective-permute-start.37 = (bf16[512,1024]{1,0:T(8,128)(2,1)S(1)}, bf16[512,1024]{1,0:T(8,128)(2,1)S(1)}, u32[]{:S(2)}, u32[]{:S(2)}) collective-permute-start(bf16[512,1024]{1,0:T(8,128)(2,1)S(1)} %get-tuple-element.286.refs_2_), channel_id=1, source_target_pairs={{2,0},{3,1},{4,6},{5,7},{10,8},{11,9},{12,14},{13,15},{18,16},{19,... | collective-permute-start | bytes 3145736 | tf_op jit(solution)/shard_map/ppermute | solution.py:92
  163.8 29.5 %collective-permute-start.39 = (bf16[256,2048]{1,0:T(8,128)(2,1)S(1)}, bf16[256,2048]{1,0:T(8,128)(2,1)S(1)}, u32[]{:S(2)}, u32[]{:S(2)}) collective-permute-start(bf16[256,2048]{1,0:T(8,128)(2,1)S(1)} %get-tuple-element.296), channel_id=1, source_target_pairs={{0,24},{8,16},{16,8},{24,0},{1,25},{9,17},{17,9},{25,1},{2,26},{10... | collective-permute-start | bytes 3145736 | tf_op jit(solution)/shard_map/ppermute | solution.py:52
  193.4 27.8 %collective-permute-start.40 = (bf16[528,1024]{1,0:T(8,128)(2,1)S(1)}, bf16[528,1024]{1,0:T(8,128)(2,1)S(1)}, u32[]{:S(2)}, u32[]{:S(2)}) collective-permute-start(bf16[528,1024]{1,0:T(8,128)(2,1)S(1)} %get-tuple-element.297.refs_0_), channel_id=1, source_target_pairs={{2,0},{3,1},{4,6},{5,7},{10,8},{11,9},{12,14},{13,15},{18,16},{19,... | collective-permute-start | bytes 3244040 | tf_op jit(solution)/shard_map/ppermute | solution.py:92
  (37 other events, 524.6 us)

commit v4 on v3

--- a/solution.py
+++ b/solution.py
@@ -311,7 +311,7 @@
 
 def pack(groups, sc, w_up, w_qkv, w_down, w_out, vectors, lengths):
     wide, hidden = w_up.shape
-    half, ff = wide // 2, hidden // groups
+    half, quarter, ff = wide // 2, wide // 4, hidden // groups
     n_vec, slots = vectors.shape[0], lengths.shape[1]
 
     def body(s_ref, up_hbm, qkv_hbm, down_hbm, out_hbm, vec_ref, len_ref, *refs):
@@ -324,11 +324,14 @@
         ]
         copies = []
         for step in range(groups):
+            size = wide if step == 0 else quarter
+            rows = pl.ds(0, wide) if step == 0 else part((2 * s_ref[3] + core) * quarter, quarter)
+            owner = me ^ step
+            at = pl.ds(0 if step == 0 else wide + (step - 1) * quarter, size)
+            mine = [pltpu.make_async_copy(up_hbm.at[rows, part(owner * ff, ff)], up_scr.at[at], sems.at[step, 0])]
             size = wide if step == 0 else half
             rows = pl.ds(0, wide) if step == 0 else part(core * half, half)
-            owner = me ^ step
             at = pl.ds(0 if step == 0 else wide + (step - 1) * half, size)
-            mine = [pltpu.make_async_copy(up_hbm.at[rows, part(owner * ff, ff)], up_scr.at[at], sems.at[step, 0])]
             for p in range(3):
                 mine.append(
                     pltpu.make_async_copy(
@@ -352,11 +355,12 @@
                 up_out[...] = up_scr[:wide].astype(BF)
                 qkv_out[...] = qkv_scr[:wide].astype(BF)
                 continue
+            at = wide + (step - 1) * quarter
+            up_out[:quarter, :] = up_scr[at : at + quarter].astype(BF)
+            up_out[quarter:, :] = jnp.zeros((EXTRA, ff), BF)
+            up_out[quarter : quarter + n_vec, :wide] = vec_ref[...].astype(BF)
+            up_out[quarter + n_vec : quarter + n_vec + 1, :slots] = len_ref[...].astype(F32).astype(BF)
             at = wide + (step - 1) * half
-            up_out[:half, :] = up_scr[at : at + half].astype(BF)
-            up_out[half:, :] = jnp.zeros((EXTRA, ff), BF)
-            up_out[half : half + n_vec, :wide] = vec_ref[...].astype(BF)
-            up_out[half + n_vec : half + n_vec + 1, :slots] = len_ref[...].astype(F32).astype(BF)
             qkv_out[...] = qkv_scr[at : at + half].astype(BF)
         for copy in rest:
             copy.wait()
@@ -367,12 +371,11 @@
     outs = []
     for step in range(groups):
         size = wide if step == 0 else half
-        extra = 0 if step == 0 else EXTRA
-        outs.append(((size + extra, ff), BF, full(None)))
+        outs.append(((wide if step == 0 else quarter + EXTRA, ff), BF, full(None)))
         outs.append(((size, 3 * wide), BF, full(None)))
     outs += [(w_down.shape, BF, full(None)), (w_out.shape, BF, full(None))]
     rows = wide + (groups - 1) * half
-    scratch = [pltpu.VMEM((rows, ff), F32), pltpu.VMEM((rows, 3 * wide), F32)]
+    scratch = [pltpu.VMEM((wide + (groups - 1) * quarter, ff), F32), pltpu.VMEM((rows, 3 * wide), F32)]
     scratch += [pltpu.VMEM(w_down.shape, F32), pltpu.VMEM(w_out.shape, F32)]
     scratch += [pltpu.SemaphoreType.DMA((groups, 4)), pltpu.SemaphoreType.DMA((2,))]
     got = kernel_call(body, (1,), in_specs, outs, scratch, 7.0, 60)(sc, w_up, w_qkv, w_down, w_out, vectors, lengths)
@@ -381,28 +384,34 @@
 
 def tables(sc, lens, groups, rows, slots):
     def body(s_ref, lens_ref, cos_ref, sin_ref):
-        block = pl.program_id(0)
-        lengths, ends = ends_of(lens_ref, block, slots)
+        lane = lax.broadcasted_iota(jnp.int32, (8, LANES), 1) % HD
+        pair = (lane % (ROT // 2)).astype(F32)
+        freq = jnp.where(lane < ROT, jnp.exp(-pair * (2.0 * math.log(10000.0) / ROT)), 0.0)[0:1, :]
         index = index_of((rows, LANES), 0)
-        start = jnp.zeros((rows, LANES), F32)
-        for length, end in zip(lengths, ends, strict=True):
-            start = start + jnp.where(jnp.broadcast_to(end, index.shape) <= index, length, 0.0)
-        lane = lax.broadcasted_iota(jnp.int32, (rows, LANES), 1) % HD
-        pair = (lane % (ROT // 2)).astype(F32)
-        freq = jnp.where(lane < ROT, jnp.exp(-pair * (2.0 * math.log(10000.0) / ROT)), 0.0)
-        angle = (index - start) * freq
-        cos_ref[...] = jnp.cos(angle)
-        sin_ref[...] = jnp.sin(angle)
-
-    out = ((groups * rows, LANES), F32, by_row((rows, LANES)))
-    return kernel_call(body, (groups,), [full(lens.shape)], [out, out], (), 3.0)(sc, lens)
+        angle = index * freq
+        cos_index, sin_index = jnp.cos(angle), jnp.sin(angle)
+        for block in range(groups):
+            lengths, ends = ends_of(lens_ref, block, slots)
+            cos_start = jnp.ones((rows, LANES), F32)
+            sin_start = jnp.zeros((rows, LANES), F32)
+            for length, end in zip(lengths, ends, strict=True):
+                turn = jnp.broadcast_to(end, (8, LANES)) * jnp.broadcast_to(freq, (8, LANES))
+                inside = jnp.broadcast_to(end, index.shape) <= index
+                cos_start = jnp.where(inside, jnp.cos(turn)[0:1, :], cos_start)
+                sin_start = jnp.where(inside, jnp.sin(turn)[0:1, :], sin_start)
+            at = slice(block * rows, (block + 1) * rows)
+            cos_ref[at, :] = cos_index * cos_start + sin_index * sin_start
+            sin_ref[at, :] = sin_index * cos_start - cos_index * sin_start
+
+    out = ((groups * rows, LANES), F32, full(None))
+    return kernel_call(body, (1,), [full(lens.shape)], [out, out], (), 1.5)(sc, lens)
 
 
 def forward_up(sc, xs, own, mine, other, vectors, lengths):
     groups, n_x = len(xs), len(flat(xs))
     rows, width = xs[0][0].shape
     wide, ff = own.shape
-    half = wide // 2
+    quarter = wide // 4
     n_vec, slots = vectors.shape[0], lengths.shape[1]
     tok = groups * rows
 
@@ -410,10 +419,10 @@
         x_refs, refs = refs[:n_x], refs[n_x:]
         own_ref = refs[0]
         mine_refs = refs[1:groups]
-        other_refs = refs[groups : 2 * groups - 1]
-        vec_in, len_in = refs[2 * groups - 1 : 2 * groups + 1]
-        attn_ref, mlp_ref, act_ref, slope_ref, stats_ref, w_ref, vec_ref, lens_ref, x_scr = refs[2 * groups + 1 :]
-        me, core = s_ref[0], s_ref[1]
+        other_refs = refs[groups : groups + 3]
+        vec_in, len_in = refs[groups + 3 : groups + 5]
+        attn_ref, mlp_ref, act_ref, slope_ref, stats_ref, w_ref, vec_ref, lens_ref, x_scr = refs[groups + 5 :]
+        me, core, side = s_ref[0], s_ref[1], s_ref[3]
         block = pl.program_id(0)
 
         @pl.when(block == 0)
@@ -425,11 +434,14 @@
             lens_ref[0, 0:1, 0:slots] = len_in[...].astype(F32)
             for step in range(1, groups):
                 at = (me ^ step) * wide
-                w_ref[part(at + core * half, half), :] = mine_refs[step - 1][:half, :]
-                w_ref[part(at + (1 - core) * half, half), :] = other_refs[step - 1][:half, :]
-                vec_ref[0:n_vec, part(at, wide)] = mine_refs[step - 1][half : half + n_vec, :wide].astype(F32)
+                w_ref[part(at + (2 * side + core) * quarter, quarter), :] = mine_refs[step - 1][:quarter, :]
+                for ref, which in zip(
+                    other_refs, (2 * (1 - side) + core, 2 * side + 1 - core, 2 * (1 - side) + 1 - core), strict=True
+                ):
+                    w_ref[part(at + which * quarter, quarter), :] = ref[(step - 1) * quarter : step * quarter, :]
+                vec_ref[0:n_vec, part(at, wide)] = mine_refs[step - 1][quarter : quarter + n_vec, :wide].astype(F32)
                 lens_ref[step, 0:1, 0:slots] = mine_refs[step - 1][
-                    half + n_vec : half + n_vec + 1, :slots
+                    quarter + n_vec : quarter + n_vec + 1, :slots
                 ].astype(F32)
 
         load_block(block, xs, x_refs, x_scr)
@@ -449,11 +461,10 @@
         act_ref[...] = act.astype(BF)
         slope_ref[...] = slope
 
-    piece = (half + EXTRA, ff)
     in_specs = (
         [full(item.shape) for item in flat(xs)]
         + [full(own.shape)]
-        + [full(piece)] * (2 * (groups - 1))
+        + [full(None)] * (groups + 2)
         + [full(vectors.shape), full(lengths.shape)]
     )
     outs = [
@@ -746,56 +757,63 @@
     return kernel_call(body, (1,), [full(None)] * len(ops), [out, out, qkv, qkv], (), 0.0)(sc, *ops)
 
 
-def merge(sc, qkv_keep, qkv_got, vec_grad, scale):
+def merge(sc, qkv_keep, qkv_got):
     groups, half, columns = qkv_keep.shape
-    wide = columns // 3
-    rows = half + EXTRA
-
-    def body(s_ref, keep_ref, got_ref, vec_ref, stay_ref, away_ref):
-        me = s_ref[0]
+
+    def body(s_ref, keep_ref, got_ref, stay_ref, away_ref):
         for i in range(groups):
-            ref, at = (away_ref if i % 2 else stay_ref), i // 2 * rows
+            ref, at = (away_ref if i % 2 else stay_ref), i // 2 * half
             ref[at : at + half, :] = keep_ref[i] + got_ref[i]
-            ref[at + half : at + rows, :] = jnp.zeros((EXTRA, columns), BF)
-            ref[at + half : at + rows, :wide] = (vec_ref[:, part((me ^ i) * wide, wide)] * scale).astype(BF)
-
-    shape = jax.ShapeDtypeStruct((groups // 2 * rows, columns), BF)
-    return on_vmem(body, [shape, shape], sc, [qkv_keep, qkv_got, vec_grad])
-
-
-def join(sc, qkv_rows, out_keep, out_got):
+
+    shape = jax.ShapeDtypeStruct((groups // 2 * half, columns), BF)
+    return on_vmem(body, [shape, shape], sc, [qkv_keep, qkv_got])
+
+
+def join(sc, qkv_rows, out_keep, out_got, vec_sum):
     groups = len(qkv_rows)
     half, width = out_keep.shape
     wide = 2 * half
     share = width // groups
 
     def body(s_ref, *refs):
-        rows, (keep_ref, got_ref, out) = refs[:groups], refs[groups:]
-        vec = jnp.zeros((EXTRA, wide), F32)
+        rows, (keep_ref, got_ref, vec_ref, out) = refs[:groups], refs[groups:]
         out[groups * half :, :] = jnp.zeros((EXTRA, 3 * wide + share), BF)
         for i in range(groups):
             at = slice(i * half, (i + 1) * half)
             columns = slice(i * share, (i + 1) * share)
-            out[at, : 3 * wide] = rows[i][:half, :]
+            out[at, : 3 * wide] = rows[i][...]
             out[at, 3 * wide :] = keep_ref[:, columns] + got_ref[:, columns]
-            vec = vec + rows[i][half:, :wide].astype(F32)
-        out[groups * half :, :wide] = vec.astype(BF)
+        out[groups * half :, :wide] = vec_ref[:, part(s_ref[0] * wide, wide)].astype(BF)
 
     shape = jax.ShapeDtypeStruct((groups * half + EXTRA, 3 * wide + share), BF)
-    return on_vmem(body, [shape], sc, [*qkv_rows, out_keep, out_got])[0]
-
-
-def finish(sc, own, got, tokens, cotangent, lens, stats, vec, slots):
+    return on_vmem(body, [shape], sc, [*qkv_rows, out_keep, out_got, vec_sum])[0]
+
+
+def sum_along(value, axis):
+    size = lax.axis_size(axis)
+    bit = 1
+    while bit < size:
+        value = value + lax.ppermute(value, axis, [(i, i ^ bit) for i in range(size)])
+        bit *= 2
+    return value
+
+
+def finish(sc, own, got, left, right, tokens, cotangent, lens, stats, vec, slots):
     rows, width = tokens.shape
 
     def body(s_ref, own_ref, *refs):
-        got_refs = refs[: len(got)]
-        tok_ref, cot_ref, lens_ref, stats_ref, vec_ref, out_ref, grad_ref = refs[len(got) :]
+        count = len(got) + 2 * len(left)
+        got_refs, left_refs, right_refs = refs[: len(got)], refs[len(got) : len(got) + len(left)], refs[len(got) + len(left) : count]
+        tok_ref, cot_ref, lens_ref, stats_ref, vec_ref, out_ref, grad_ref = refs[count:]
         branch = own_ref[:, :width].astype(F32)
         scaled = own_ref[:, width:].astype(F32)
         for ref in got_refs:
             branch = branch + ref[:, :width].astype(F32)
             scaled = scaled + ref[:, width:].astype(F32)
+        for ref in left_refs:
+            branch = branch + ref[...].astype(F32)
+        for ref in right_refs:
+            scaled = scaled + ref[...].astype(F32)
         size = branch.shape[0]
         _, ends = ends_of(lens_ref, 0, slots)
         index = index_of((size, 1), 0) + (pl.program_id(0) * size).astype(F32)
@@ -812,11 +830,11 @@
         grad_ref[...] = (cot_ref[...].astype(F32) + d_tokens).astype(BF)
 
     size = rows // 2
-    in_specs = [by_row((size, 2 * width))] * (1 + len(got)) + [by_row((size, width))] * 2
+    in_specs = [by_row((size, 2 * width))] * (1 + len(got)) + [by_row((size, width))] * (2 * len(left) + 2)
     in_specs += [full(lens.shape), by_row((size, LANES)), full(vec.shape)]
     out = ((rows, width), BF, by_row((size, width)))
     return kernel_call(body, (2,), in_specs, [out, out], (), 2.4)(
-        sc, own, *got, tokens, cotangent, lens, stats, vec
+        sc, own, *got, *left, *right, tokens, cotangent, lens, stats, vec
     )
 
 
@@ -888,10 +906,11 @@
     n_vec = vectors.shape[0]
     slots = lengths.shape[1]
     others = range(1, groups)
+    quarter = wide // 4
     places = lax.axis_size("dp") // 2
     place = lax.axis_index("dp") // 2
     outer = (place == 0) | (place == places - 1)
-    sc = jnp.stack([me, core, outer]).astype(jnp.int32)
+    sc = jnp.stack([me, core, outer, place % 2]).astype(jnp.int32)
     scale = float(rows * groups * lax.axis_size("dp")) ** (-0.5)
 
     size = ff // 2
@@ -903,16 +922,16 @@
     up_mine = [shard_swap(item, step) for item, step in zip(up_parts[1:], others, strict=True)]
     xs = gather_rest(tokens, near)
     cot_near = [shard_swap(after(cotangent, xs[3]), step) for step in (1, 2)]
-    up_other = [core_swap(item) for item in up_mine]
+    up_stack = jnp.concatenate([item[:quarter] for item in up_mine])
+    up_side = place_send(up_stack, [(i, i ^ 1) for i in range(places)])
+    up_other = [up_side, core_swap(up_stack), core_swap(up_side)]
     in_attn, in_mlp, act, slope, stats, up_w, vec, lens = forward_up(
         sc, xs, up_parts[0], up_mine, up_other, vectors, lengths
     )
     cot_near, act = fence((cot_near, act))
     cots = gather_rest(cotangent, cot_near)
     qkv_mine = [shard_swap(item, step) for item, step in zip(after(qkv_parts[1:], cot_near), others, strict=True)]
-    mlp = feed_out(sc, after(act, cot_near), down_w, groups)
-    cosine, sine = tables(sc, after(lens, mlp), groups, rows, slots)
-    cots, cosine = fence((cots, cosine))
+    cots, act = fence((cots, act))
 
     branch, bias_out = mask_rows(sc, cots, lens, slots)
     up_away, up_keep, d_up, bias_up = backward_up(sc, branch, slope, down_w, in_mlp, scale, groups)
@@ -922,31 +941,33 @@
     down_away, down_keep = grad_of_down(sc, branch, act, scale)
     down_away, down_keep, up_got, qkv_other = fence((down_away, down_keep, up_got, qkv_other))
     down_got = core_swap(down_away)
+    cosine, sine = tables(sc, after(lens, down_away), groups, rows, slots)
+    down = down_keep + down_got
+    down, branch_a, up_got, cosine = fence((down, branch, up_got, cosine))
+
+    down, _, _ = dp_round(sc, down, None, None)
     up_sums = [up_keep[i] + up_got[i] for i in range(groups)]
-    up_sums, down_got = fence((up_sums, down_got))
-    down = down_keep + down_got
-    down, branch_a = fence((down, branch))
-
-    down, _, _ = dp_round(sc, down, None, None)
+    up_sums, branch_a = fence((up_sums, branch_a))
     up_rows = [up_sums[0]] + [shard_swap(up_sums[step], step) for step in others]
     heads, d_proj, bias_qkv, qkv_w = attention(
         sc, in_attn, branch_a, cosine, sine, lens, vec, qkv_parts[0], qkv_mine, qkv_other, out_w, groups, slots
     )
-    up_rows, d_proj = fence((up_rows, d_proj))
     out_away, out_keep, qkv_away, qkv_keep = grads_of_attention(sc, in_attn, d_proj, heads, branch, scale, groups)
-    out_away, qkv_away, d_proj = fence((out_away, qkv_away, d_proj))
+    up_rows, out_away, qkv_away = fence((up_rows, out_away, qkv_away))
     qkv_got = core_swap(qkv_away)
     out_got = core_swap(out_away)
+    mlp = feed_out(sc, after(act, out_away), down_w, groups)
+    down, up_rows, qkv_got, out_got, d_proj, mlp = fence((down, up_rows, qkv_got, out_got, d_proj, mlp))
+    up = jnp.concatenate(up_rows)
+    stay, away = merge(sc, qkv_keep, qkv_got)
+    up, down, stay, away, d_proj = fence((up, down, stay, away, d_proj))
+
+    qkv_rows = exchange(stay, away)
     own, pieces, vec_grad = back_to_tokens(
         sc, xs, heads, mlp, d_proj, d_up, stats, vec, out_w, qkv_w, up_w, bias_up, bias_qkv, bias_out
     )
-    down, up_rows, qkv_got, out_got, vec_grad = fence((down, up_rows, qkv_got, out_got, vec_grad))
-    up = jnp.concatenate(up_rows)
-    stay, away = merge(sc, qkv_keep, qkv_got, vec_grad, scale)
-    up, down, stay, away = fence((up, down, stay, away))
-
-    qkv_rows = exchange(stay, away)
-    rest = join(sc, qkv_rows, out_keep, out_got)
+    vec_sum = sum_along(vec_grad * scale, "shard")
+    rest = join(sc, qkv_rows, out_keep, out_got, vec_sum)
     up, down, _ = dp_round(sc, up, down, None, rest)
     down, up, rest, pieces = fence((down, up, rest, pieces))
 
@@ -956,7 +977,7 @@
 
     down_other = core_swap(down)
     _, rest, up = dp_round(sc, None, rest, up)
-    got += [shard_swap(item, step) for item, step in zip(pieces[2:], others[2:], strict=True)]
+    left = [shard_swap(item[:, :width], step) for item, step in zip(pieces[2:], others[2:], strict=True)]
 
     def fill_down(s_ref, refs, out):
         step = pl.program_id(0)
@@ -967,7 +988,8 @@
         sc, [down, down_other], (w_down, m_down, v_down),
         (4,), (size // 2, width), lambda i, s: (i, 0), fill_down, 0.0,
     )
-    up, rest, new_down, got = fence((up, rest, new_down, got))
+    up, rest, new_down, left, pieces = fence((up, rest, new_down, left, pieces))
+    right = [shard_swap(item[:, width:], step) for item, step in zip(pieces[2:], others[2:], strict=True)]
 
     up_other = core_swap(up)
     _, _, rest = dp_round(sc, None, None, rest)
@@ -980,7 +1002,9 @@
         sc, [up, up_other], (w_up, m_up, v_up),
         (2, groups), (half, ff), lambda i, j, s: (i, j), fill_up, 0.0,
     )
-    output, input_grad = finish(sc, own, got, tokens, cotangent, lens, stats, vec, slots)
+    output, input_grad = finish(
+        sc, own, got, left, after(right, new_up), tokens, cotangent, lens, stats, vec, slots
+    )
     rest, new_up, output, input_grad = fence((rest, new_up, output, input_grad))
     rest_other = core_swap(rest)
 

time: 234 us -> 228 us (0.974)
  waiting for transfers between devices: 99 us -> 86.5 us
  starting transfers between devices: 45.3 us -> 52.3 us
    ppermute x22 -> x23, waiting for transfers between devices: 37.2 us -> 22.1 us  [shard_swap(): return lax.ppermute(value, 'shard', [(i, i ^ step) for i in range(size)])]
    ppermute x0 -> x2, waiting for transfers between devices: none -> 6.93 us  [sum_along(): lax.ppermute(value, axis, [(i, i ^ bit) for i in range(size)])]
    ppermute x8 -> x9, waiting for transfers between devices: 55 us -> 51.3 us  [place_send(): lax.ppermute(value, 'dp', [(2 * a + core, 2 * b + core) for a, b in pairs...]
    ppermute x8 -> x9, starting transfers between devices: 15.1 us -> 18.6 us  [place_send(): lax.ppermute(value, 'dp', [(2 * a + core, 2 * b + core) for a, b in pairs...]
    ppermute x22 -> x23, starting transfers between devices: 27.7 us -> 29.5 us  [shard_swap(): return lax.ppermute(value, 'shard', [(i, i ^ step) for i in range(size)])]
    ppermute x13 -> x12, waiting for transfers between devices: 6.86 us -> 6.24 us  [core_swap(): return lax.ppermute(value, 'dp', [(i, i ^ 1) for i in range(size)])]
  transfers between devices with their start and end apart: 43 -> 46, of which waited for: 18 -> 24; matrix products, arithmetic and copies ran while one was open for 1% -> 0% of each run, Pallas kernels for 32% -> 32%
where the time goes in v4:
time: 228 us
  waiting for transfers between devices  86.5 us (38%)
  Pallas kernels  76.2 us (33%)
  starting transfers between devices  52.3 us (23%)
  other arithmetic  9.85 us (4%)
    ppermute x9, waiting for transfers between devices, place_send(): lax.ppermute(value, 'dp', [(2 * a + core, 2 * b + core) for a, b in pairs...  51.3 us
    ppermute x23, starting transfers between devices, shard_swap(): return lax.ppermute(value, 'shard', [(i, i ^ step) for i in range(size)])  29.5 us
    ppermute x23, waiting for transfers between devices, shard_swap(): return lax.ppermute(value, 'shard', [(i, i ^ step) for i in range(size)])  22.1 us
    ppermute x9, starting transfers between devices, place_send(): lax.ppermute(value, 'dp', [(2 * a + core, 2 * b + core) for a, b in pairs...  18.6 us
    pallas_call x2, Pallas kernels, adam_blocks(): kernel_call(body, grid, [full(None)] * len(grads) + [spec] * 3, [(shape,...  15.9 us
    pallas_call x1, Pallas kernels, attention(): kernel_call(body, (groups,), in_specs, outs, (), 0.0)  11.4 us
    sub x3, other arithmetic, adam_terms(): return (weight - rate * (step_size + decay * weight), first_new, second_new)  8.57 us
    pallas_call x1, Pallas kernels, pack(): kernel_call(body, (1,), in_specs, outs, scratch, 7.0, 60)  7.46 us
  transfers between devices with their start and end apart: 46, of which 24 were waited for; matrix products, arithmetic and copies ran while one was open for 0% of the time, Pallas kernels for 32%

profile of v4, /device:TPU:0, one launch (start us, length us, event | category | flops | bytes accessed | tf_op | source)
XLA Modules:
  0.0 227.6 jit_solution(1368117406489640075)
XLA Ops:
  0.7 3.0 %collective-permute-start = (bf16[256,1024]{1,0:T(8,128)(2,1)}, bf16[256,1024]{1,0:T(8,128)(2,1)S(1)}, u32[]{:S(2)}, u32[]{:S(2)}) collective-permute-start(bf16[256,1024]{1,0:T(8,128)(2,1)} %refs_4_.5), channel_id=1, source_target_pairs={{0,8},{8,0},{16,24},{24,16},{1,9},{9,1},{17,25},{25,17},{2,10},{10... | collective-permute-start | bytes 1572872 | tf_op jit(solution)/shard_map/ppermute | solution.py:52
  5.8 7.5 %shard_map.345 = (bf16[256,1024]{1,0:T(8,128)(2,1)}, bf16[256,768]{1,0:T(8,128)(2,1)}, bf16[80,1024]{1,0:T(8,128)(2,1)}, bf16[128,768]{1,0:T(8,128)(2,1)}, bf16[...) custom-call(s32[4]{0:T(128)} %pad_add_fusion.s_ref, ...), custom_call_target="tpu_custom_call" | custom-call | bytes 22400000 | tf_op jit(solution)/shard_map/pallas_call | solution.py:381
  13.3 2.5 %collective-permute-done.refs_1_ = bf16[256,1024]{1,0:T(8,128)(2,1)S(1)} collective-permute-done((bf16[256,1024]{1,0:T(8,128)(2,1)}, bf16[256,1024]{1,0:T(8,128)(2,1)S(1)}, u32[]{:S(2)}, u32[]{:S(2)}) %collective-permute-start) | collective-permute-done | bytes 524320 | tf_op jit(solution)/shard_map/ppermute | solution.py:52
  17.6 1.7 collective-permute-start.7
  24.6 3.2 %collective-permute-done.7.refs_7_ = bf16[80,1024]{1,0:T(8,128)(2,1)S(1)} collective-permute-done((bf16[80,1024]{1,0:T(8,128)(2,1)}, bf16[80,1024]{1,0:T(8,128)(2,1)S(1)}, u32[]{:S(2)}, u32[]{:S(2)}) %collective-permute-start.7) | collective-permute-done | bytes 163872 | tf_op jit(solution)/shard_map/ppermute | solution.py:52
  34.6 2.4 %collective-permute-done.9.refs_9_ = bf16[192,1024]{1,0:T(8,128)(2,1)S(1)} collective-permute-done((bf16[192,1024]{1,0:T(8,128)(2,1)S(1)}, bf16[192,1024]{1,0:T(8,128)(2,1)S(1)}, u32[]{:S(2)}, u32[]{:S(2)}) %collective-permute-start.9) | collective-permute-done | bytes 393248 | tf_op jit(solution)/shard_map/ppermute | solution.py:92
  37.0 1.7 collective-permute-done.11.refs_11_
  39.8 6.5 %shard_map.346 = (bf16[1024,1024]{1,0:T(8,128)(2,1)S(1)}, bf16[1024,1024]{1,0:T(8,128)(2,1)S(1)}, bf16[1024,1024]{1,0:T(8,128)(2,1)S(1)}, f32[1024,1024]{1,0:T(8...) custom-call(s32[4]{0:T(128)S(1)} %copy-done.12, ...), custom_call_target="tpu_custom_call" | custom-call | bytes 20800000 | tf_op jit(solution)/shard_map/pallas_call | solution.py:480
  51.9 3.7 %collective-permute-done.12.refs_3_ = bf16[128,1024]{1,0:T(8,128)(2,1)S(1)} collective-permute-done((bf16[128,1024]{1,0:T(8,128)(2,1)S(1)}, bf16[128,1024]{1,0:T(8,128)(2,1)S(1)}, u32[]{:S(2)}, u32[]{:S(2)}) %collective-permute-start.12) | collective-permute-done | bytes 262176 | tf_op jit(solution)/shard_map/ppermute | solution.py:52
  57.3 6.8 %shard_map.348 = (bf16[4,128,1024]{2,1,0:T(8,128)(2,1)S(1)}, bf16[4,128,1024]{2,1,0:T(8,128)(2,1)S(1)}, bf16[1024,1024]{1,0:T(8,128)(2,1)S(1)}, f32[8,1024]{1,0:T(8,128)S(1)}) custom-call(s32[4]{0:T(128)S(1)} %copy-done.12, bf16[1024,1024]{1,0:T(8,128)(2,1)S(1)} %get-tuple-element.229.branch_ref.refs_1_, f32[1024,1024]{1,0:T(8,128)S(1)} %get-tuple-element.196.slope_ref, ...), custom_call_target="tpu_custom_call" | custom-call | bytes 21760000 | tf_op jit(solution)/shard_map/pallas_call | solution.py:570
  65.5 2.9 %shard_map.349 = (bf16[512,1024]{1,0:T(8,128)(2,1)S(1)}, bf16[512,1024]{1,0:T(8,128)(2,1)S(1)}) custom-call(s32[4]{0:T(128)S(1)} %copy-done.12, bf16[1024,1024]{1,0:T(8,128)(2,1)S(1)} %get-tuple-element.229.branch_ref.refs_1_, bf16[1024,1024]{1,0:T(8,128)(2,1)S(1)} %get-tuple-element.248.act_ref), custom_call_target="tpu_custom_call" | custom-call | bytes 9600000 | tf_op jit(solution)/shard_map/pallas_call | solution.py:521
  68.5 1.8 shard_map.350
  75.3 3.7 %collective-permute-start.22 = (bf16[512,1024]{1,0:T(8,128)(2,1)S(1)}, bf16[512,1024]{1,0:T(8,128)(2,1)S(1)}, u32[]{:S(2)}, u32[]{:S(2)}) collective-permute-start(bf16[512,1024]{1,0:T(8,128)(2,1)S(1)} %add.91.refs_0_), channel_id=1, source_target_pairs={{0,2},{1,3},{6,4},{7,5},{8,10},{9,11},{14,12},{15,13},{16,18},{17,... | collective-permute-start | bytes 3145736 | tf_op jit(solution)/shard_map/ppermute | solution.py:92
  79.0 11.4 %shard_map.352 = (bf16[1024,256]{1,0:T(8,128)(2,1)S(1)}, bf16[1024,768]{1,0:T(8,128)(2,1)S(1)}, f32[8,768]{1,0:T(8,128)S(1)}, bf16[1024,768]{1,0:T(8,128)(2,1)S(1)}) custom-call(s32[4]{0:T(128)S(1)} %copy-done.12, bf16[1024,1024]{1,0:T(8,128)(2,1)S(1)} %get-tuple-element.228.refs_0_.a_ref, bf16[1024,1024]{1,0:T(8,128)(2,1)S(1)} %get-tuple-element.229.branch_ref.refs_1_, ...), custom_call_target="tpu_custom_call" | custom-call | tf_op jit(solution)/shard_map/pallas_call | solution.py:662
  90.5 4.0 %shard_map.353 = (bf16[128,1024]{1,0:T(8,128)(2,1)S(1)}, bf16[128,1024]{1,0:T(8,128)(2,1)S(1)}, bf16[4,128,768]{2,1,0:T(8,128)(2,1)S(1)}, bf16[4,128,768]{2,1,0:T(8,128)(2,1)S(1)}) custom-call(s32[4]{0:T(128)S(1)} %copy-done.12, bf16[1024,1024]{1,0:T(8,128)(2,1)S(1)} %get-tuple-element.228.refs_0_.a_ref, ...), custom_call_target="tpu_custom_call" | custom-call | tf_op jit(solution)/shard_map/pallas_call | solution.py:757
  95.1 3.4 %shard_map.354.refs_6_ = bf16[1024,1024]{1,0:T(8,128)(2,1)S(1)} custom-call(s32[4]{0:T(128)S(1)} %copy-done.12, bf16[1024,1024]{1,0:T(8,128)(2,1)S(1)} %get-tuple-element.248.act_ref, bf16[1024,1024]{1,0:T(8,128)(2,1)S(1)} %copy-done.2), custom_call_target="tpu_custom_call" | custom-call | bytes 9600000 | tf_op jit(solution)/shard_map/pallas_call | solution.py:533
  98.5 2.1 collective-permute-done.22.refs_1_
  103.2 4.4 %collective-permute-start.28 = (bf16[512,1024]{1,0:T(8,128)(2,1)S(1)}, bf16[512,1024]{1,0:T(8,128)(2,1)S(1)}, u32[]{:S(2)}, u32[]{:S(2)}) collective-permute-start(bf16[512,1024]{1,0:T(8,128)(2,1)S(1)} %pad_maximum_fusion.refs_0_), channel_id=1, source_target_pairs={{0,2},{1,3},{6,4},{7,5},{8,10},{9,11},{14,12},{15,13},{16,18},{17,... | collective-permute-start | bytes 3145736 | tf_op jit(solution)/shard_map/ppermute | solution.py:92
  108.4 7.3 %shard_map.356 = (bf16[256,2048]{1,0:T(8,128)(2,1)S(1)}, bf16[256,2048]{1,0:T(8,128)(2,1)S(1)}, bf16[256,2048]{1,0:T(8,128)(2,1)S(1)}, bf16[256,2048]{1,0:T(8,128)(2,1)S(1)}, f32[16,1024]{1,0:T(8,128)S(1)}) custom-call(s32[4]{0:T(128)S(1)} %copy-done.12, bf16[256,1024]{1,0:T(8,128)(2,1)S(1)} %copy-done.3, ...), custom_call_target="tpu_custom_call" | custom-call | tf_op jit(solution)/shard_map/pallas_call | solution.py:726
  118.0 3.1 %collective-permute-done.32 = f32[16,1024]{1,0:T(8,128)S(1)} collective-permute-done((f32[16,1024]{1,0:T(8,128)S(1)}, f32[16,1024]{1,0:T(8,128)S(1)}, u32[]{:S(2)}, u32[]{:S(2)}) %collective-permute-start.32) | collective-permute-done | bytes 65568 | tf_op jit(solution)/shard_map/ppermute | solution.py:796
  122.3 3.8 %collective-permute-done.33 = f32[16,1024]{1,0:T(8,128)S(1)} collective-permute-done((f32[16,1024]{1,0:T(8,128)S(1)}, f32[16,1024]{1,0:T(8,128)S(1)}, u32[]{:S(2)}, u32[]{:S(2)}) %collective-permute-start.33) | collective-permute-done | bytes 65568 | tf_op jit(solution)/shard_map/ppermute | solution.py:796
  129.0 3.9 %collective-permute-start.34 = (bf16[528,1024]{1,0:T(8,128)(2,1)S(1)}, bf16[528,1024]{1,0:T(8,128)(2,1)S(1)}, u32[]{:S(2)}, u32[]{:S(2)}) collective-permute-start(bf16[528,1024]{1,0:T(8,128)(2,1)S(1)} %get-tuple-element.281.refs_4_), channel_id=1, source_target_pairs={{0,2},{1,3},{2,0},{3,1},{4,6},{5,7},{6,4},{7,5},{8,10},{9,11},{10,... | collective-permute-start | bytes 3244040 | tf_op jit(solution)/shard_map/ppermute | solution.py:92
  135.8 18.3 %collective-permute-done.34.refs_1_.refs_5_ = bf16[528,1024]{1,0:T(8,128)(2,1)S(1)} collective-permute-done((bf16[528,1024]{1,0:T(8,128)(2,1)S(1)}, bf16[528,1024]{1,0:T(8,128)(2,1)S(1)}, u32[]{:S(2)}, u32[]{:S(2)}) %collective-permute-start.34) | collective-permute-done | bytes 1081376 | tf_op jit(solution)/shard_map/ppermute | solution.py:92
  160.1 7.9 %shard_map.361 = (f32[1024,1024]{1,0:T(8,128)}, f32[1024,1024]{1,0:T(8,128)}, f32[1024,1024]{1,0:T(8,128)}, f32[1024,1024]{1,0:T(8,128)}) custom-call(s32[4]{0:T(128)S(1)} %copy-done.12, bf16[512,1024]{1,0:T(8,128)(2,1)S(1)} %get-tuple-element.293.refs_0_, bf16[512,1024]{1,0:T(8,128)(2,1)S(1)} %collective-permute-done.40.refs_1_, f32[1024,1024]{1,0:T(8,128)S(1)} %copy-done, ...), custom_call_target="tpu_custom_call" | custom-call | tf_op jit(solution)/shard_map/pallas_call | solution.py:871
  168.0 18.9 %collective-permute-done.39.refs_3_ = bf16[512,1024]{1,0:T(8,128)(2,1)S(1)} collective-permute-done((bf16[512,1024]{1,0:T(8,128)(2,1)S(1)}, bf16[512,1024]{1,0:T(8,128)(2,1)S(1)}, u32[]{:S(2)}, u32[]{:S(2)}) %collective-permute-start.39) | collective-permute-done | bytes 1048608 | tf_op jit(solution)/shard_map/ppermute | solution.py:92
  192.0 8.0 %shard_map.363 = (f32[256,4096]{1,0:T(8,128)}, f32[256,4096]{1,0:T(8,128)}, f32[256,4096]{1,0:T(8,128)}, f32[256,4096]{1,0:T(8,128)}) custom-call(s32[4]{0:T(128)S(1)} %copy-done.12, bf16[512,1024]{1,0:T(8,128)(2,1)S(1)} %get-tuple-element.300.refs_0_, bf16[512,1024]{1,0:T(8,128)(2,1)S(1)} %collective-permute-done.43.refs_1_, f32[256,4096]{1,0:T(8,128)S(1)} %copy-done.1, ...), custom_call_target="tpu_custom_call" | custom-call | tf_op jit(solution)/shard_map/pallas_call | solution.py:871
  200.0 4.7 %collective-permute-done.44.refs_3_ = bf16[256,1024]{1,0:T(8,128)(2,1)S(1)} collective-permute-done((bf16[256,1024]{1,0:T(8,128)(2,1)S(1)}, bf16[256,1024]{1,0:T(8,128)(2,1)S(1)}, u32[]{:S(2)}, u32[]{:S(2)}) %collective-permute-start.44) | collective-permute-done | bytes 524320 | tf_op jit(solution)/shard_map/ppermute | solution.py:52
  204.7 2.5 %shard_map.364 = (bf16[256,1024]{1,0:T(8,128)(2,1)}, bf16[256,1024]{1,0:T(8,128)(2,1)}) custom-call(s32[4]{0:T(128)S(1)} %copy-done.12, bf16[256,2048]{1,0:T(8,128)(2,1)S(1)} %get-tuple-element.305.own_ref, bf16[256,2048]{1,0:T(8,128)(2,1)S(1)} %collective-permute-done.36.refs_0_, bf16[256,2048]{1,0:T(8,128)(2,1)S(1)} %collective-permute-done.37.refs_1_, ...), custom_call_target="tpu_custom_call" | custom-call | bytes 7680000 | tf_op jit(solution)/shard_map/pallas_call | solution.py:836
  207.1 8.1 %collective-permute-done.42.refs_1_ = bf16[528,1024]{1,0:T(8,128)(2,1)S(1)} collective-permute-done((bf16[528,1024]{1,0:T(8,128)(2,1)S(1)}, bf16[528,1024]{1,0:T(8,128)(2,1)S(1)}, u32[]{:S(2)}, u32[]{:S(2)}) %collective-permute-start.42) | collective-permute-done | bytes 1081376 | tf_op jit(solution)/shard_map/ppermute | solution.py:92
  216.0 2.7 %collective-permute-done.45.refs_1_ = bf16[528,1024]{1,0:T(8,128)(2,1)S(1)} collective-permute-done((bf16[528,1024]{1,0:T(8,128)(2,1)S(1)}, bf16[528,1024]{1,0:T(8,128)(2,1)S(1)}, u32[]{:S(2)}, u32[]{:S(2)}) %collective-permute-start.45) | collective-permute-done | bytes 1081376 | tf_op jit(solution)/shard_map/ppermute | solution.py:72
  219.0 5.6 %multiply_subtract_fusion = (f32[256,3072]{1,0:T(8,128)}, f32[256,3072]{1,0:T(8,128)}, f32[256,3072]{1,0:T(8,128)}, f32[256,3072]{1,0:T(8,128)}) fusion(f32[256,3072]{1,0:T(8,128)S(1)} %copy-done.15, f32[256,3072]{1,0:T(8,128)S(1)} %copy-done.17, f32[256,3072]{1,0:T(8,128)S(1)} %copy-done.18, bf16[256,3072]{1,0:T(8,128)(2,1)S(1)} %get-tuple-element.316), kind=kLoop, calls=%fused_computation.2 | loop fusion | flops 12582912 | bytes 23592960 | tf_op jit(solution)/shard_map/sub | solution.py:309
  224.7 2.3 %multiply_subtract_fusion.1 = (f32[256,1024]{1,0:T(8,128)}, f32[256,1024]{1,0:T(8,128)}, f32[256,1024]{1,0:T(8,128)}, f32[256,1024]{1,0:T(8,128)}) fusion(f32[256,1024]{1,0:T(8,128)S(1)} %copy-done.16, f32[256,1024]{1,0:T(8,128)S(1)} %copy-done.19, f32[256,1024]{1,0:T(8,128)S(1)} %copy-done.20, bf16[256,1024]{1,0:T(8,128)(2,1)S(1)} %get-tuple-element.317), kind=kLoop, calls=%fused_computation.7 | loop fusion | flops 4194304 | bytes 7864320 | tf_op jit(solution)/shard_map/sub | solution.py:309
  (157 shorter events, 56.4 us)
Async XLA Ops:
  0.7 15.1 %collective-permute-start = (bf16[256,1024]{1,0:T(8,128)(2,1)}, bf16[256,1024]{1,0:T(8,128)(2,1)S(1)}, u32[]{:S(2)}, u32[]{:S(2)}) collective-permute-start(bf16[256,1024]{1,0:T(8,128)(2,1)} %refs_4_.5), channel_id=1, source_target_pairs={{0,8},{8,0},{16,24},{24,16},{1,9},{9,1},{17,25},{25,17},{2,10},{10... | collective-permute-start | bytes 1572872 | tf_op jit(solution)/shard_map/ppermute | solution.py:52
  3.7 13.6 %collective-permute-start.1 = (bf16[256,1024]{1,0:T(8,128)(2,1)}, bf16[256,1024]{1,0:T(8,128)(2,1)S(1)}, u32[]{:S(2)}, u32[]{:S(2)}) collective-permute-start(bf16[256,1024]{1,0:T(8,128)(2,1)} %refs_4_.5), channel_id=1, source_target_pairs={{0,16},{8,24},{16,0},{24,8},{1,17},{9,25},{17,1},{25,9},{2,18},{10... | collective-permute-start | bytes 1572872 | tf_op jit(solution)/shard_map/ppermute | solution.py:52
  17.3 7.3 %collective-permute-start.6 = (bf16[80,1024]{1,0:T(8,128)(2,1)}, bf16[80,1024]{1,0:T(8,128)(2,1)S(1)}, u32[]{:S(2)}, u32[]{:S(2)}) collective-permute-start(bf16[80,1024]{1,0:T(8,128)(2,1)} %get-tuple-element.182), channel_id=1, source_target_pairs={{0,8},{8,0},{16,24},{24,16},{1,9},{9,1},{17,25},{25,17},{2,10},{10... | collective-permute-start | bytes 491528 | tf_op jit(solution)/shard_map/ppermute | solution.py:52
  17.6 10.2 %collective-permute-start.7 = (bf16[80,1024]{1,0:T(8,128)(2,1)}, bf16[80,1024]{1,0:T(8,128)(2,1)S(1)}, u32[]{:S(2)}, u32[]{:S(2)}) collective-permute-start(bf16[80,1024]{1,0:T(8,128)(2,1)} %get-tuple-element.183), channel_id=1, source_target_pairs={{0,16},{8,24},{16,0},{24,8},{1,17},{9,25},{17,1},{25,9},{2,18},{10... | collective-permute-start | bytes 491528 | tf_op jit(solution)/shard_map/ppermute | solution.py:52
  19.3 9.8 %collective-permute-start.8 = (bf16[80,1024]{1,0:T(8,128)(2,1)}, bf16[80,1024]{1,0:T(8,128)(2,1)S(1)}, u32[]{:S(2)}, u32[]{:S(2)}) collective-permute-start(bf16[80,1024]{1,0:T(8,128)(2,1)} %get-tuple-element.184), channel_id=1, source_target_pairs={{0,24},{8,16},{16,8},{24,0},{1,25},{9,17},{17,9},{25,1},{2,26},{10... | collective-permute-start | bytes 491528 | tf_op jit(solution)/shard_map/ppermute | solution.py:52
  20.8 11.3 %collective-permute-start.2 = (bf16[128,1024]{1,0:T(8,128)(2,1)S(1)}, bf16[128,1024]{1,0:T(8,128)(2,1)S(1)}, u32[]{:S(2)}, u32[]{:S(2)}) collective-permute-start(bf16[128,1024]{1,0:T(8,128)(2,1)S(1)} %slice.75), channel_id=1, source_target_pairs={{0,16},{8,24},{16,0},{24,8},{1,17},{9,25},{17,1},{25,9},{2,18},{10... | collective-permute-start | bytes 786440 | tf_op jit(solution)/shard_map/ppermute | solution.py:52
  22.4 9.7 %collective-permute-start.3 = (bf16[128,1024]{1,0:T(8,128)(2,1)S(1)}, bf16[128,1024]{1,0:T(8,128)(2,1)S(1)}, u32[]{:S(2)}, u32[]{:S(2)}) collective-permute-start(bf16[128,1024]{1,0:T(8,128)(2,1)S(1)} %slice.76), channel_id=1, source_target_pairs={{0,8},{8,0},{16,24},{24,16},{1,9},{9,1},{17,25},{25,17},{2,10},{10... | collective-permute-start | bytes 786440 | tf_op jit(solution)/shard_map/ppermute | solution.py:52
  29.1 7.8 %collective-permute-start.9 = (bf16[192,1024]{1,0:T(8,128)(2,1)S(1)}, bf16[192,1024]{1,0:T(8,128)(2,1)S(1)}, u32[]{:S(2)}, u32[]{:S(2)}) collective-permute-start(bf16[192,1024]{1,0:T(8,128)(2,1)S(1)} %pad_maximum_fusion.1), channel_id=1, source_target_pairs={{0,2},{1,3},{2,0},{3,1},{4,6},{5,7},{6,4},{7,5},{8,10},{9,11},{10,... | collective-permute-start | bytes 1179656 | tf_op jit(solution)/shard_map/ppermute | solution.py:92
  32.1 14.2 %collective-permute-start.4 = (bf16[256,1024]{1,0:T(8,128)(2,1)S(1)}, bf16[256,1024]{1,0:T(8,128)(2,1)S(1)}, u32[]{:S(2)}, u32[]{:S(2)}) collective-permute-start(bf16[256,1024]{1,0:T(8,128)(2,1)S(1)} %copy-done.8), channel_id=1, source_target_pairs={{0,8},{8,0},{16,24},{24,16},{1,9},{9,1},{17,25},{25,17},{2,10},{10... | collective-permute-start | bytes 1572872 | tf_op jit(solution)/shard_map/ppermute | solution.py:52
  33.1 13.2 %collective-permute-start.5 = (bf16[256,1024]{1,0:T(8,128)(2,1)S(1)}, bf16[256,1024]{1,0:T(8,128)(2,1)S(1)}, u32[]{:S(2)}, u32[]{:S(2)}) collective-permute-start(bf16[256,1024]{1,0:T(8,128)(2,1)S(1)} %copy-done.8), channel_id=1, source_target_pairs={{0,16},{8,24},{16,0},{24,8},{1,17},{9,25},{17,1},{25,9},{2,18},{10... | collective-permute-start | bytes 1572872 | tf_op jit(solution)/shard_map/ppermute | solution.py:52
  46.4 9.2 %collective-permute-start.12 = (bf16[128,1024]{1,0:T(8,128)(2,1)S(1)}, bf16[128,1024]{1,0:T(8,128)(2,1)S(1)}, u32[]{:S(2)}, u32[]{:S(2)}) collective-permute-start(bf16[128,1024]{1,0:T(8,128)(2,1)S(1)} %slice.80), channel_id=1, source_target_pairs={{0,16},{8,24},{16,0},{24,8},{1,17},{9,25},{17,1},{25,9},{2,18},{10... | collective-permute-start | bytes 786440 | tf_op jit(solution)/shard_map/ppermute | solution.py:52
  47.0 9.3 %collective-permute-start.13 = (bf16[128,1024]{1,0:T(8,128)(2,1)S(1)}, bf16[128,1024]{1,0:T(8,128)(2,1)S(1)}, u32[]{:S(2)}, u32[]{:S(2)}) collective-permute-start(bf16[128,1024]{1,0:T(8,128)(2,1)S(1)} %slice.81), channel_id=1, source_target_pairs={{0,8},{8,0},{16,24},{24,16},{1,9},{9,1},{17,25},{25,17},{2,10},{10... | collective-permute-start | bytes 786440 | tf_op jit(solution)/shard_map/ppermute | solution.py:52
  48.4 15.6 %collective-permute-start.14 = (bf16[128,768]{1,0:T(8,128)(2,1)S(1)}, bf16[128,768]{1,0:T(8,128)(2,1)S(1)}, u32[]{:S(2)}, u32[]{:S(2)}) collective-permute-start(bf16[128,768]{1,0:T(8,128)(2,1)S(1)} %copy-done.25), channel_id=1, source_target_pairs={{0,8},{8,0},{16,24},{24,16},{1,9},{9,1},{17,25},{25,17},{2,10},{10... | collective-permute-start | bytes 589832 | tf_op jit(solution)/shard_map/ppermute | solution.py:52
  49.0 15.0 %collective-permute-start.15 = (bf16[128,768]{1,0:T(8,128)(2,1)S(1)}, bf16[128,768]{1,0:T(8,128)(2,1)S(1)}, u32[]{:S(2)}, u32[]{:S(2)}) collective-permute-start(bf16[128,768]{1,0:T(8,128)(2,1)S(1)} %copy-done.24), channel_id=1, source_target_pairs={{0,16},{8,24},{16,0},{24,8},{1,17},{9,25},{17,1},{25,9},{2,18},{10... | collective-permute-start | bytes 589832 | tf_op jit(solution)/shard_map/ppermute | solution.py:52
  50.6 13.9 %collective-permute-start.16 = (bf16[128,768]{1,0:T(8,128)(2,1)S(1)}, bf16[128,768]{1,0:T(8,128)(2,1)S(1)}, u32[]{:S(2)}, u32[]{:S(2)}) collective-permute-start(bf16[128,768]{1,0:T(8,128)(2,1)S(1)} %copy-done.23), channel_id=1, source_target_pairs={{0,24},{8,16},{16,8},{24,0},{1,25},{9,17},{17,9},{25,1},{2,26},{10... | collective-permute-start | bytes 589832 | tf_op jit(solution)/shard_map/ppermute | solution.py:52
  71.7 22.7 %collective-permute-start.23 = (bf16[128,1024]{1,0:T(8,128)(2,1)S(1)}, bf16[128,1024]{1,0:T(8,128)(2,1)S(1)}, u32[]{:S(2)}, u32[]{:S(2)}) collective-permute-start(bf16[128,1024]{1,0:T(8,128)(2,1)S(1)} %get-tuple-element.225), channel_id=1, source_target_pairs={{0,8},{8,0},{16,24},{24,16},{1,9},{9,1},{17,25},{25,17},{2,10},{10... | collective-permute-start | bytes 786440 | tf_op jit(solution)/shard_map/ppermute | solution.py:52
  72.9 21.5 %collective-permute-start.24 = (bf16[128,1024]{1,0:T(8,128)(2,1)S(1)}, bf16[128,1024]{1,0:T(8,128)(2,1)S(1)}, u32[]{:S(2)}, u32[]{:S(2)}) collective-permute-start(bf16[128,1024]{1,0:T(8,128)(2,1)S(1)} %get-tuple-element.226), channel_id=1, source_target_pairs={{0,16},{8,24},{16,0},{24,8},{1,17},{9,25},{17,1},{25,9},{2,18},{10... | collective-permute-start | bytes 786440 | tf_op jit(solution)/shard_map/ppermute | solution.py:52
  73.9 20.5 %collective-permute-start.25 = (bf16[128,1024]{1,0:T(8,128)(2,1)S(1)}, bf16[128,1024]{1,0:T(8,128)(2,1)S(1)}, u32[]{:S(2)}, u32[]{:S(2)}) collective-permute-start(bf16[128,1024]{1,0:T(8,128)(2,1)S(1)} %get-tuple-element.227), channel_id=1, source_target_pairs={{0,24},{8,16},{16,8},{24,0},{1,25},{9,17},{17,9},{25,1},{2,26},{10... | collective-permute-start | bytes 786440 | tf_op jit(solution)/shard_map/ppermute | solution.py:52
  75.3 25.3 %collective-permute-start.22 = (bf16[512,1024]{1,0:T(8,128)(2,1)S(1)}, bf16[512,1024]{1,0:T(8,128)(2,1)S(1)}, u32[]{:S(2)}, u32[]{:S(2)}) collective-permute-start(bf16[512,1024]{1,0:T(8,128)(2,1)S(1)} %add.91.refs_0_), channel_id=1, source_target_pairs={{0,2},{1,3},{6,4},{7,5},{8,10},{9,11},{14,12},{15,13},{16,18},{17,... | collective-permute-start | bytes 3145736 | tf_op jit(solution)/shard_map/ppermute | solution.py:92
  94.5 6.8 %collective-permute-start.26 = (bf16[4,128,768]{2,1,0:T(8,128)(2,1)S(1)}, bf16[4,128,768]{2,1,0:T(8,128)(2,1)S(1)}, u32[]{:S(2)}, u32[]{:S(2)}) collective-permute-start(bf16[4,128,768]{2,1,0:T(8,128)(2,1)S(1)} %get-tuple-element.246), channel_id=1, source_target_pairs={{0,1},{1,0},{2,3},{3,2},{4,5},{5,4},{6,7},{7,6},{8,9},{9,8},{10,11... | collective-permute-start | bytes 2359304 | tf_op jit(solution)/shard_map/ppermute | solution.py:72
  102.0 13.7 %collective-permute-start.30 = (bf16[256,768]{1,0:T(8,128)(2,1)S(1)}, bf16[256,768]{1,0:T(8,128)(2,1)S(1)}, u32[]{:S(2)}, u32[]{:S(2)}) collective-permute-start(bf16[256,768]{1,0:T(8,128)(2,1)S(1)} %get-tuple-element.262), channel_id=1, source_target_pairs={{0,8},{8,0},{16,24},{24,16},{1,9},{9,1},{17,25},{25,17},{2,10},{10... | collective-permute-start | bytes 1179656 | tf_op jit(solution)/shard_map/ppermute | solution.py:52
  103.2 25.0 %collective-permute-start.28 = (bf16[512,1024]{1,0:T(8,128)(2,1)S(1)}, bf16[512,1024]{1,0:T(8,128)(2,1)S(1)}, u32[]{:S(2)}, u32[]{:S(2)}) collective-permute-start(bf16[512,1024]{1,0:T(8,128)(2,1)S(1)} %pad_maximum_fusion.refs_0_), channel_id=1, source_target_pairs={{0,2},{1,3},{6,4},{7,5},{8,10},{9,11},{14,12},{15,13},{16,18},{17,... | collective-permute-start | bytes 3145736 | tf_op jit(solution)/shard_map/ppermute | solution.py:92
  107.6 20.6 %collective-permute-start.29 = (bf16[512,1024]{1,0:T(8,128)(2,1)S(1)}, bf16[512,1024]{1,0:T(8,128)(2,1)S(1)}, u32[]{:S(2)}, u32[]{:S(2)}) collective-permute-start(bf16[512,1024]{1,0:T(8,128)(2,1)S(1)} %shard_map.351.refs_2_), channel_id=1, source_target_pairs={{2,4},{3,5},{4,2},{5,3},{10,12},{11,13},{12,10},{13,11},{18,20},{1... | collective-permute-start | bytes 3145736 | tf_op jit(solution)/shard_map/ppermute | solution.py:92
  115.8 10.3 %collective-permute-start.31 = (bf16[256,768]{1,0:T(8,128)(2,1)S(1)}, bf16[256,768]{1,0:T(8,128)(2,1)S(1)}, u32[]{:S(2)}, u32[]{:S(2)}) collective-permute-start(bf16[256,768]{1,0:T(8,128)(2,1)S(1)} %pad_maximum_fusion.2), channel_id=1, source_target_pairs={{0,16},{8,24},{16,0},{24,8},{1,17},{9,25},{17,1},{25,9},{2,18},{10... | collective-permute-start | bytes 1179656 | tf_op jit(solution)/shard_map/ppermute | solution.py:52
  129.0 25.1 %collective-permute-start.34 = (bf16[528,1024]{1,0:T(8,128)(2,1)S(1)}, bf16[528,1024]{1,0:T(8,128)(2,1)S(1)}, u32[]{:S(2)}, u32[]{:S(2)}) collective-permute-start(bf16[528,1024]{1,0:T(8,128)(2,1)S(1)} %get-tuple-element.281.refs_4_), channel_id=1, source_target_pairs={{0,2},{1,3},{2,0},{3,1},{4,6},{5,7},{6,4},{7,5},{8,10},{9,11},{10,... | collective-permute-start | bytes 3244040 | tf_op jit(solution)/shard_map/ppermute | solution.py:92
  133.6 22.0 %collective-permute-start.36 = (bf16[256,2048]{1,0:T(8,128)(2,1)S(1)}, bf16[256,2048]{1,0:T(8,128)(2,1)S(1)}, u32[]{:S(2)}, u32[]{:S(2)}) collective-permute-start(bf16[256,2048]{1,0:T(8,128)(2,1)S(1)} %get-tuple-element.286), channel_id=1, source_target_pairs={{0,8},{8,0},{16,24},{24,16},{1,9},{9,1},{17,25},{25,17},{2,10},{10... | collective-permute-start | bytes 3145736 | tf_op jit(solution)/shard_map/ppermute | solution.py:52
  134.6 21.7 %collective-permute-start.37 = (bf16[256,2048]{1,0:T(8,128)(2,1)S(1)}, bf16[256,2048]{1,0:T(8,128)(2,1)S(1)}, u32[]{:S(2)}, u32[]{:S(2)}) collective-permute-start(bf16[256,2048]{1,0:T(8,128)(2,1)S(1)} %get-tuple-element.287), channel_id=1, source_target_pairs={{0,16},{8,24},{16,0},{24,8},{1,17},{9,25},{17,1},{25,9},{2,18},{10... | collective-permute-start | bytes 3145736 | tf_op jit(solution)/shard_map/ppermute | solution.py:52
  156.3 30.7 %collective-permute-start.38 = (bf16[528,1024]{1,0:T(8,128)(2,1)S(1)}, bf16[528,1024]{1,0:T(8,128)(2,1)S(1)}, u32[]{:S(2)}, u32[]{:S(2)}) collective-permute-start(bf16[528,1024]{1,0:T(8,128)(2,1)S(1)} %get-tuple-element.289.refs_0_), channel_id=1, source_target_pairs={{2,4},{3,5},{4,2},{5,3},{10,12},{11,13},{12,10},{13,11},{18,20},{1... | collective-permute-start | bytes 3244040 | tf_op jit(solution)/shard_map/ppermute | solution.py:92
  157.1 29.9 %collective-permute-start.39 = (bf16[512,1024]{1,0:T(8,128)(2,1)S(1)}, bf16[512,1024]{1,0:T(8,128)(2,1)S(1)}, u32[]{:S(2)}, u32[]{:S(2)}) collective-permute-start(bf16[512,1024]{1,0:T(8,128)(2,1)S(1)} %get-tuple-element.290.refs_2_), channel_id=1, source_target_pairs={{2,0},{3,1},{4,6},{5,7},{10,8},{11,9},{12,14},{13,15},{18,16},{19,... | collective-permute-start | bytes 3145736 | tf_op jit(solution)/shard_map/ppermute | solution.py:92
  158.4 29.3 %collective-permute-start.41 = (bf16[256,1024]{1,0:T(8,128)(2,1)S(1)}, bf16[256,1024]{1,0:T(8,128)(2,1)S(1)}, u32[]{:S(2)}, u32[]{:S(2)}) collective-permute-start(bf16[256,1024]{1,0:T(8,128)(2,1)S(1)} %slice.96), channel_id=1, source_target_pairs={{0,24},{8,16},{16,8},{24,0},{1,25},{9,17},{17,9},{25,1},{2,26},{10... | collective-permute-start | bytes 1572872 | tf_op jit(solution)/shard_map/ppermute | solution.py:52
  187.7 27.6 %collective-permute-start.42 = (bf16[528,1024]{1,0:T(8,128)(2,1)S(1)}, bf16[528,1024]{1,0:T(8,128)(2,1)S(1)}, u32[]{:S(2)}, u32[]{:S(2)}) collective-permute-start(bf16[528,1024]{1,0:T(8,128)(2,1)S(1)} %get-tuple-element.299.refs_0_), channel_id=1, source_target_pairs={{2,0},{3,1},{4,6},{5,7},{10,8},{11,9},{12,14},{13,15},{18,16},{19,... | collective-permute-start | bytes 3244040 | tf_op jit(solution)/shard_map/ppermute | solution.py:92
  189.4 15.3 %collective-permute-start.44 = (bf16[256,1024]{1,0:T(8,128)(2,1)S(1)}, bf16[256,1024]{1,0:T(8,128)(2,1)S(1)}, u32[]{:S(2)}, u32[]{:S(2)}) collective-permute-start(bf16[256,1024]{1,0:T(8,128)(2,1)S(1)} %slice.97), channel_id=1, source_target_pairs={{0,24},{8,16},{16,8},{24,0},{1,25},{9,17},{17,9},{25,1},{2,26},{10... | collective-permute-start | bytes 1572872 | tf_op jit(solution)/shard_map/ppermute | solution.py:52
  (40 other events, 562.9 us)

commit v5 on v4

--- a/solution.py
+++ b/solution.py
@@ -482,32 +482,6 @@
     )(sc, *flat(xs), own, *mine, *other, vectors, lengths)
 
 
-def mask_rows(sc, cots, lens, slots):
-    n_c = len(flat(cots))
-    rows, width = cots[0][0].shape
-
-    def body(s_ref, *refs):
-        cot_refs = iter(refs[:n_c])
-        lens_ref, branch_ref, bias_ref = refs[n_c:]
-        for step, pieces in enumerate(cots):
-            _, ends = ends_of(lens_ref, step, slots)
-            row = 0
-            for piece in pieces:
-                size = piece.shape[0]
-                index = index_of((size, 1), 0) + float(row)
-                valid = jnp.where(index < jnp.broadcast_to(ends[-1], (size, 1)), 1.0, 0.0)
-                branch = next(cot_refs)[...].astype(F32) * valid
-                at = step * rows + row
-                branch_ref[at : at + size, :] = branch.astype(BF)
-                row += size
-                if step == 0:
-                    bias_ref[...] = jnp.broadcast_to(jnp.sum(branch, axis=0, keepdims=True), bias_ref.shape)
-
-    outs = [((len(cots) * rows, width), BF, full(None)), ((8, width), F32, full(None))]
-    in_specs = [full(item.shape) for item in flat(cots) + [lens]]
-    return kernel_call(body, (1,), in_specs, outs, (), 1.0)(sc, *flat(cots), lens)
-
-
 def grad_of_down(sc, branch, act, scale):
     tok, width = branch.shape
     size = act.shape[1] // 2
@@ -533,13 +507,16 @@
     return kernel_call(body, (groups,), [by_row((rows, ff)), full(None)], outs, (), 3.0)(sc, act, w_down)[0]
 
 
-def backward_up(sc, branch, slope, w_down, in_mlp, scale, groups):
-    tok, width = branch.shape
-    rows = tok // groups
+def backward_up(sc, cots, lens, slots, slope, w_down, in_mlp, scale):
+    groups, n_c = len(cots), len(flat(cots))
+    rows, width = cots[0][0].shape
+    tok = groups * rows
     ff = slope.shape[1]
     half = width // groups // 2
 
-    def body(s_ref, branch_ref, slope_ref, wd_ref, mlp_ref, away_ref, keep_ref, up_ref, bias_ref):
+    def body(s_ref, *refs):
+        cot_refs, refs = refs[:n_c], refs[n_c:]
+        lens_ref, slope_ref, wd_ref, mlp_ref, branch_ref, sum_ref, away_ref, keep_ref, up_ref, bias_ref, scratch = refs
         me, core = s_ref[0], s_ref[1]
         block = pl.program_id(0)
 
@@ -547,7 +524,20 @@
         def _():
             bias_ref[...] = jnp.zeros_like(bias_ref)
 
-        d_up = dot_rt(branch_ref[...], wd_ref[...]) * slope_ref[...]
+        load_block(block, cots, cot_refs, scratch)
+        total = jnp.zeros((1, 1), F32)
+        for slot in range(slots):
+            total = total + lens_ref[block, 0:1, slot : slot + 1]
+        valid = jnp.where(index_of((rows, 1), 0) < jnp.broadcast_to(total, (rows, 1)), 1.0, 0.0)
+        branch_f = scratch[...].astype(F32) * valid
+        branch = branch_f.astype(BF)
+        branch_ref[...] = branch
+
+        @pl.when(block == 0)
+        def _():
+            sum_ref[...] = jnp.broadcast_to(jnp.sum(branch_f, axis=0, keepdims=True), sum_ref.shape)
+
+        d_up = dot_rt(branch, wd_ref[...]) * slope_ref[...]
         bias_ref[0:1, :] += jnp.sum(d_up, axis=0, keepdims=True)
         up_ref[part(block * rows, rows), :] = d_up.astype(BF)
 
@@ -560,15 +550,17 @@
 
             lax.fori_loop(0, groups, piece, 0)
 
-    in_specs = [by_row((rows, width)), by_row((rows, ff)), full(w_down.shape), full(in_mlp.shape)]
+    in_specs = [full(None)] * (n_c + 1) + [by_row((rows, ff)), full(w_down.shape), full(in_mlp.shape)]
     outs = [
+        ((tok, width), BF, by_row((rows, width))),
+        ((8, width), F32, full(None)),
         ((groups, half, ff), BF, full((groups, half, ff))),
         ((groups, half, ff), BF, full((groups, half, ff))),
         ((tok, ff), BF, full((tok, ff))),
         ((8, ff), F32, full((8, ff))),
     ]
-    return kernel_call(body, (groups,), in_specs, outs, (), 6.8)(
-        sc, branch, slope, w_down, in_mlp
+    return kernel_call(body, (groups,), in_specs, outs, [pltpu.VMEM((rows, width), BF)], 6.8)(
+        sc, *flat(cots), lens, slope, w_down, in_mlp
     )
 
 
@@ -918,8 +910,8 @@
 
     up_parts, qkv_parts, down_w, out_w = pack(groups, sc, w_up, w_qkv, w_down, w_out, vectors, lengths)
     near = [shard_swap(tokens, step) for step in (1, 2)]
-    near, up_parts = fence((near, up_parts))
     up_mine = [shard_swap(item, step) for item, step in zip(up_parts[1:], others, strict=True)]
+    near, up_mine[0], qkv_parts = fence((near, up_mine[0], qkv_parts))
     xs = gather_rest(tokens, near)
     cot_near = [shard_swap(after(cotangent, xs[3]), step) for step in (1, 2)]
     up_stack = jnp.concatenate([item[:quarter] for item in up_mine])
@@ -933,8 +925,9 @@
     qkv_mine = [shard_swap(item, step) for item, step in zip(after(qkv_parts[1:], cot_near), others, strict=True)]
     cots, act = fence((cots, act))
 
-    branch, bias_out = mask_rows(sc, cots, lens, slots)
-    up_away, up_keep, d_up, bias_up = backward_up(sc, branch, slope, down_w, in_mlp, scale, groups)
+    branch, bias_out, up_away, up_keep, d_up, bias_up = backward_up(
+        sc, cots, lens, slots, slope, down_w, in_mlp, scale
+    )
     up_away, up_keep, qkv_mine, branch = fence((up_away, up_keep, qkv_mine, branch))
     up_got = core_swap(up_away)
     qkv_other = [core_swap(item) for item in qkv_mine]
@@ -958,7 +951,7 @@
     out_got = core_swap(out_away)
     mlp = feed_out(sc, after(act, out_away), down_w, groups)
     down, up_rows, qkv_got, out_got, d_proj, mlp = fence((down, up_rows, qkv_got, out_got, d_proj, mlp))
-    up = jnp.concatenate(up_rows)
+    up = jnp.concatenate(up_rows + [jnp.zeros((EXTRA, ff), BF)])
     stay, away = merge(sc, qkv_keep, qkv_got)
     up, down, stay, away, d_proj = fence((up, down, stay, away, d_proj))
 

time: 228 us -> 226 us (level)
    ppermute x9, waiting for transfers between devices: 51.3 us -> 48.5 us  [place_send(): lax.ppermute(value, 'dp', [(2 * a + core, 2 * b + core) for a, b in pairs...]
    pallas_call x2 -> x1, Pallas kernels: 7.83 us -> 8.07 us  [backward_up(): kernel_call(body, (groups,), in_specs, outs, [pltpu.VMEM((rows, width), B...]
  transfers between devices with their start and end apart: 46 -> 46, of which waited for: 24 -> 20; matrix products, arithmetic and copies ran while one was open for 0% -> 0% of each run, Pallas kernels for 32% -> 33%
where the time goes in v5:
time: 226 us; the launch traced here: 225 us
  waiting for transfers between devices  84.3 us (37%)
  Pallas kernels  76.4 us (34%)
  starting transfers between devices  50.8 us (22%)
  other arithmetic  9.75 us (4%)
  local copies, waits for them, and re-layouts  2.49 us (1%)
    ppermute x9, waiting for transfers between devices, place_send(): lax.ppermute(value, 'dp', [(2 * a + core, 2 * b + core) for a, b in pairs...  48.5 us
    ppermute x23, starting transfers between devices, shard_swap(): return lax.ppermute(value, 'shard', [(i, i ^ step) for i in range(size)])  29.7 us
    ppermute x23, waiting for transfers between devices, shard_swap(): return lax.ppermute(value, 'shard', [(i, i ^ step) for i in range(size)])  23 us
    ppermute x9, starting transfers between devices, place_send(): lax.ppermute(value, 'dp', [(2 * a + core, 2 * b + core) for a, b in pairs...  17.9 us
    pallas_call x2, Pallas kernels, adam_blocks(): kernel_call(body, grid, [full(None)] * len(grads) + [spec] * 3, [(shape,...  15.9 us
    pallas_call x1, Pallas kernels, attention(): kernel_call(body, (groups,), in_specs, outs, (), 0.0)  11.4 us
    sub x3, other arithmetic, adam_terms(): return (weight - rate * (step_size + decay * weight), first_new, second_new)  8.57 us
    pallas_call x1, Pallas kernels, backward_up(): kernel_call(body, (groups,), in_specs, outs, [pltpu.VMEM((rows, width), B...  8.07 us
  transfers between devices with their start and end apart: 46, of which 20 were waited for; matrix products, arithmetic and copies ran while one was open for 0% of the time, Pallas kernels for 33%

profile of v5, /device:TPU:0, one launch (start us, length us, event | category | flops | bytes accessed | tf_op | source)
XLA Modules:
  0.0 225.2 jit_solution(4245028642840056817)
XLA Ops:
  0.7 3.0 %collective-permute-start = (bf16[256,1024]{1,0:T(8,128)(2,1)}, bf16[256,1024]{1,0:T(8,128)(2,1)S(1)}, u32[]{:S(2)}, u32[]{:S(2)}) collective-permute-start(bf16[256,1024]{1,0:T(8,128)(2,1)} %refs_4_.5), channel_id=1, source_target_pairs={{0,8},{8,0},{16,24},{24,16},{1,9},{9,1},{17,25},{25,17},{2,10},{10... | collective-permute-start | bytes 1572872 | tf_op jit(solution)/shard_map/ppermute | solution.py:52
  5.8 7.5 %shard_map.345 = (bf16[256,1024]{1,0:T(8,128)(2,1)}, bf16[256,768]{1,0:T(8,128)(2,1)}, bf16[80,1024]{1,0:T(8,128)(2,1)}, bf16[128,768]{1,0:T(8,128)(2,1)}, bf16[...) custom-call(s32[4]{0:T(128)} %pad_add_fusion.s_ref, ...), custom_call_target="tpu_custom_call" | custom-call | bytes 22400000 | tf_op jit(solution)/shard_map/pallas_call | solution.py:381
  16.8 7.5 %collective-permute-done.7.refs_7_ = bf16[80,1024]{1,0:T(8,128)(2,1)S(1)} collective-permute-done((bf16[80,1024]{1,0:T(8,128)(2,1)}, bf16[80,1024]{1,0:T(8,128)(2,1)S(1)}, u32[]{:S(2)}, u32[]{:S(2)}) %collective-permute-start.7) | collective-permute-done | bytes 163872 | tf_op jit(solution)/shard_map/ppermute | solution.py:52
  28.3 3.0 %collective-permute-done.3.refs_3_ = bf16[128,1024]{1,0:T(8,128)(2,1)S(1)} collective-permute-done((bf16[128,1024]{1,0:T(8,128)(2,1)S(1)}, bf16[128,1024]{1,0:T(8,128)(2,1)S(1)}, u32[]{:S(2)}, u32[]{:S(2)}) %collective-permute-start.3) | collective-permute-done | bytes 262176 | tf_op jit(solution)/shard_map/ppermute | solution.py:52
  33.9 2.0 collective-permute-done.9.refs_9_
  38.7 6.6 %shard_map.346 = (bf16[1024,1024]{1,0:T(8,128)(2,1)S(1)}, bf16[1024,1024]{1,0:T(8,128)(2,1)S(1)}, bf16[1024,1024]{1,0:T(8,128)(2,1)S(1)}, f32[1024,1024]{1,0:T(8...) custom-call(s32[4]{0:T(128)S(1)} %copy-done.14, ...), custom_call_target="tpu_custom_call" | custom-call | bytes 20800000 | tf_op jit(solution)/shard_map/pallas_call | solution.py:480
  50.9 3.6 %collective-permute-done.12.refs_3_ = bf16[128,1024]{1,0:T(8,128)(2,1)S(1)} collective-permute-done((bf16[128,1024]{1,0:T(8,128)(2,1)S(1)}, bf16[128,1024]{1,0:T(8,128)(2,1)S(1)}, u32[]{:S(2)}, u32[]{:S(2)}) %collective-permute-start.12) | collective-permute-done | bytes 262176 | tf_op jit(solution)/shard_map/ppermute | solution.py:52
  55.3 8.1 %shard_map.347 = (bf16[1024,1024]{1,0:T(8,128)(2,1)S(1)}, f32[8,1024]{1,0:T(8,128)S(1)}, bf16[4,128,1024]{2,1,0:T(8,128)(2,1)S(1)}, bf16[4,128,1024]{2,1,0:T(8,1...) custom-call(s32[4]{0:T(128)S(1)} %copy-done.14, bf16[256,1024]{1,0:T(8,128)(2,1)S(1)} %copy-done.9, ...), custom_call_target="tpu_custom_call" | custom-call | bytes 21760000 | tf_op jit(solution)/shard_map/pallas_call | solution.py:562
  64.4 2.9 %shard_map.348 = (bf16[512,1024]{1,0:T(8,128)(2,1)S(1)}, bf16[512,1024]{1,0:T(8,128)(2,1)S(1)}) custom-call(s32[4]{0:T(128)S(1)} %copy-done.14, bf16[1024,1024]{1,0:T(8,128)(2,1)S(1)} %get-tuple-element.231.branch_ref.refs_1_, bf16[1024,1024]{1,0:T(8,128)(2,1)S(1)} %get-tuple-element.250.act_ref), custom_call_target="tpu_custom_call" | custom-call | bytes 9600000 | tf_op jit(solution)/shard_map/pallas_call | solution.py:495
  67.6 1.8 shard_map.349
  74.2 3.7 %collective-permute-start.22 = (bf16[512,1024]{1,0:T(8,128)(2,1)S(1)}, bf16[512,1024]{1,0:T(8,128)(2,1)S(1)}, u32[]{:S(2)}, u32[]{:S(2)}) collective-permute-start(bf16[512,1024]{1,0:T(8,128)(2,1)S(1)} %add.91.refs_0_), channel_id=1, source_target_pairs={{0,2},{1,3},{6,4},{7,5},{8,10},{9,11},{14,12},{15,13},{16,18},{17,... | collective-permute-start | bytes 3145736 | tf_op jit(solution)/shard_map/ppermute | solution.py:92
  77.9 11.4 %shard_map.351 = (bf16[1024,256]{1,0:T(8,128)(2,1)S(1)}, bf16[1024,768]{1,0:T(8,128)(2,1)S(1)}, f32[8,768]{1,0:T(8,128)S(1)}, bf16[1024,768]{1,0:T(8,128)(2,1)S(1)}) custom-call(s32[4]{0:T(128)S(1)} %copy-done.14, bf16[1024,1024]{1,0:T(8,128)(2,1)S(1)} %get-tuple-element.230.refs_0_.a_ref, bf16[1024,1024]{1,0:T(8,128)(2,1)S(1)} %get-tuple-element.231.branch_ref.refs_1_, ...), custom_call_target="tpu_custom_call" | custom-call | tf_op jit(solution)/shard_map/pallas_call | solution.py:654
  89.3 4.0 %shard_map.352 = (bf16[128,1024]{1,0:T(8,128)(2,1)S(1)}, bf16[128,1024]{1,0:T(8,128)(2,1)S(1)}, bf16[4,128,768]{2,1,0:T(8,128)(2,1)S(1)}, bf16[4,128,768]{2,1,0:T(8,128)(2,1)S(1)}) custom-call(s32[4]{0:T(128)S(1)} %copy-done.14, bf16[1024,1024]{1,0:T(8,128)(2,1)S(1)} %get-tuple-element.230.refs_0_.a_ref, ...), custom_call_target="tpu_custom_call" | custom-call | tf_op jit(solution)/shard_map/pallas_call | solution.py:749
  93.9 3.4 %shard_map.353.refs_6_ = bf16[1024,1024]{1,0:T(8,128)(2,1)S(1)} custom-call(s32[4]{0:T(128)S(1)} %copy-done.14, bf16[1024,1024]{1,0:T(8,128)(2,1)S(1)} %get-tuple-element.250.act_ref, bf16[1024,1024]{1,0:T(8,128)(2,1)S(1)} %copy-done.2), custom_call_target="tpu_custom_call" | custom-call | bytes 9600000 | tf_op jit(solution)/shard_map/pallas_call | solution.py:507
  97.3 2.2 collective-permute-done.22.refs_1_
  102.5 4.4 %collective-permute-start.28 = (bf16[528,1024]{1,0:T(8,128)(2,1)S(1)}, bf16[528,1024]{1,0:T(8,128)(2,1)S(1)}, u32[]{:S(2)}, u32[]{:S(2)}) collective-permute-start(bf16[528,1024]{1,0:T(8,128)(2,1)S(1)} %broadcast_dynamic-update-slice_fusion.refs_0_), channel_id=1, source_target_pairs={{0,2},{1,3},{6,4},{7,5},{8,10},{9,11},{14,12},{15,13},{16,18},{17,... | collective-permute-start | bytes 3244040 | tf_op jit(solution)/shard_map/ppermute | solution.py:92
  107.6 7.2 %shard_map.355 = (bf16[256,2048]{1,0:T(8,128)(2,1)S(1)}, bf16[256,2048]{1,0:T(8,128)(2,1)S(1)}, bf16[256,2048]{1,0:T(8,128)(2,1)S(1)}, bf16[256,2048]{1,0:T(8,128)(2,1)S(1)}, f32[16,1024]{1,0:T(8,128)S(1)}) custom-call(s32[4]{0:T(128)S(1)} %copy-done.14, bf16[256,1024]{1,0:T(8,128)(2,1)S(1)} %copy-done.3, ...), custom_call_target="tpu_custom_call" | custom-call | tf_op jit(solution)/shard_map/pallas_call | solution.py:718
  117.2 3.7 %collective-permute-done.32 = f32[16,1024]{1,0:T(8,128)S(1)} collective-permute-done((f32[16,1024]{1,0:T(8,128)S(1)}, f32[16,1024]{1,0:T(8,128)S(1)}, u32[]{:S(2)}, u32[]{:S(2)}) %collective-permute-start.32) | collective-permute-done | bytes 65568 | tf_op jit(solution)/shard_map/ppermute | solution.py:788
  121.5 3.8 %collective-permute-done.33 = f32[16,1024]{1,0:T(8,128)S(1)} collective-permute-done((f32[16,1024]{1,0:T(8,128)S(1)}, f32[16,1024]{1,0:T(8,128)S(1)}, u32[]{:S(2)}, u32[]{:S(2)}) %collective-permute-start.33) | collective-permute-done | bytes 65568 | tf_op jit(solution)/shard_map/ppermute | solution.py:788
  126.0 2.2 collective-permute-done.28.refs_1_
  128.9 3.2 %collective-permute-start.34 = (bf16[528,1024]{1,0:T(8,128)(2,1)S(1)}, bf16[528,1024]{1,0:T(8,128)(2,1)S(1)}, u32[]{:S(2)}, u32[]{:S(2)}) collective-permute-start(bf16[528,1024]{1,0:T(8,128)(2,1)S(1)} %get-tuple-element.283.refs_4_), channel_id=1, source_target_pairs={{0,2},{1,3},{2,0},{3,1},{4,6},{5,7},{6,4},{7,5},{8,10},{9,11},{10,... | collective-permute-start | bytes 3244040 | tf_op jit(solution)/shard_map/ppermute | solution.py:92
  135.0 18.4 %collective-permute-done.34.refs_1_.refs_5_ = bf16[528,1024]{1,0:T(8,128)(2,1)S(1)} collective-permute-done((bf16[528,1024]{1,0:T(8,128)(2,1)S(1)}, bf16[528,1024]{1,0:T(8,128)(2,1)S(1)}, u32[]{:S(2)}, u32[]{:S(2)}) %collective-permute-start.34) | collective-permute-done | bytes 1081376 | tf_op jit(solution)/shard_map/ppermute | solution.py:92
  158.3 2.4 %collective-permute-start.41 = (bf16[256,1024]{1,0:T(8,128)(2,1)S(1)}, bf16[256,1024]{1,0:T(8,128)(2,1)S(1)}, u32[]{:S(2)}, u32[]{:S(2)}) collective-permute-start(bf16[256,1024]{1,0:T(8,128)(2,1)S(1)} %slice.96), channel_id=1, source_target_pairs={{0,24},{8,16},{16,8},{24,0},{1,25},{9,17},{17,9},{25,1},{2,26},{10... | collective-permute-start | bytes 1572872 | tf_op jit(solution)/shard_map/ppermute | solution.py:52
  160.9 7.9 %shard_map.360 = (f32[1024,1024]{1,0:T(8,128)}, f32[1024,1024]{1,0:T(8,128)}, f32[1024,1024]{1,0:T(8,128)}, f32[1024,1024]{1,0:T(8,128)}) custom-call(s32[4]{0:T(128)S(1)} %copy-done.14, bf16[512,1024]{1,0:T(8,128)(2,1)S(1)} %get-tuple-element.295.refs_0_, bf16[512,1024]{1,0:T(8,128)(2,1)S(1)} %collective-permute-done.40.refs_1_, f32[1024,1024]{1,0:T(8,128)S(1)} %copy-done, ...), custom_call_target="tpu_custom_call" | custom-call | tf_op jit(solution)/shard_map/pallas_call | solution.py:863
  168.9 15.0 %collective-permute-done.39.refs_3_ = bf16[528,1024]{1,0:T(8,128)(2,1)S(1)} collective-permute-done((bf16[528,1024]{1,0:T(8,128)(2,1)S(1)}, bf16[528,1024]{1,0:T(8,128)(2,1)S(1)}, u32[]{:S(2)}, u32[]{:S(2)}) %collective-permute-start.39) | collective-permute-done | bytes 1081376 | tf_op jit(solution)/shard_map/ppermute | solution.py:92
  187.8 8.0 %shard_map.362 = (f32[256,4096]{1,0:T(8,128)}, f32[256,4096]{1,0:T(8,128)}, f32[256,4096]{1,0:T(8,128)}, f32[256,4096]{1,0:T(8,128)}) custom-call(s32[4]{0:T(128)S(1)} %copy-done.14, bf16[528,1024]{1,0:T(8,128)(2,1)S(1)} %get-tuple-element.302.refs_0_, bf16[528,1024]{1,0:T(8,128)(2,1)S(1)} %collective-permute-done.43.refs_1_, f32[256,4096]{1,0:T(8,128)S(1)} %copy-done.1, ...), custom_call_target="tpu_custom_call" | custom-call | tf_op jit(solution)/shard_map/pallas_call | solution.py:863
  195.8 5.7 %collective-permute-done.44.refs_3_ = bf16[256,1024]{1,0:T(8,128)(2,1)S(1)} collective-permute-done((bf16[256,1024]{1,0:T(8,128)(2,1)S(1)}, bf16[256,1024]{1,0:T(8,128)(2,1)S(1)}, u32[]{:S(2)}, u32[]{:S(2)}) %collective-permute-start.44) | collective-permute-done | bytes 524320 | tf_op jit(solution)/shard_map/ppermute | solution.py:52
  201.6 2.5 %shard_map.363 = (bf16[256,1024]{1,0:T(8,128)(2,1)}, bf16[256,1024]{1,0:T(8,128)(2,1)}) custom-call(s32[4]{0:T(128)S(1)} %copy-done.14, bf16[256,2048]{1,0:T(8,128)(2,1)S(1)} %get-tuple-element.307.own_ref, bf16[256,2048]{1,0:T(8,128)(2,1)S(1)} %collective-permute-done.36.refs_0_, bf16[256,2048]{1,0:T(8,128)(2,1)S(1)} %copy-done.11, ...), custom_call_target="tpu_custom_call" | custom-call | bytes 7680000 | tf_op jit(solution)/shard_map/pallas_call | solution.py:828
  204.0 8.8 %collective-permute-done.42.refs_1_ = bf16[528,1024]{1,0:T(8,128)(2,1)S(1)} collective-permute-done((bf16[528,1024]{1,0:T(8,128)(2,1)S(1)}, bf16[528,1024]{1,0:T(8,128)(2,1)S(1)}, u32[]{:S(2)}, u32[]{:S(2)}) %collective-permute-start.42) | collective-permute-done | bytes 1081376 | tf_op jit(solution)/shard_map/ppermute | solution.py:92
  213.5 2.7 %collective-permute-done.45.refs_1_ = bf16[528,1024]{1,0:T(8,128)(2,1)S(1)} collective-permute-done((bf16[528,1024]{1,0:T(8,128)(2,1)S(1)}, bf16[528,1024]{1,0:T(8,128)(2,1)S(1)}, u32[]{:S(2)}, u32[]{:S(2)}) %collective-permute-start.45) | collective-permute-done | bytes 1081376 | tf_op jit(solution)/shard_map/ppermute | solution.py:72
  216.6 5.6 %multiply_subtract_fusion = (f32[256,3072]{1,0:T(8,128)}, f32[256,3072]{1,0:T(8,128)}, f32[256,3072]{1,0:T(8,128)}, f32[256,3072]{1,0:T(8,128)}) fusion(f32[256,3072]{1,0:T(8,128)S(1)} %copy-done.17, f32[256,3072]{1,0:T(8,128)S(1)} %copy-done.19, f32[256,3072]{1,0:T(8,128)S(1)} %copy-done.20, bf16[256,3072]{1,0:T(8,128)(2,1)S(1)} %get-tuple-element.318), kind=kLoop, calls=%fused_computation.2 | loop fusion | flops 12582912 | bytes 23592960 | tf_op jit(solution)/shard_map/sub | solution.py:309
  222.2 2.3 %multiply_subtract_fusion.1 = (f32[256,1024]{1,0:T(8,128)}, f32[256,1024]{1,0:T(8,128)}, f32[256,1024]{1,0:T(8,128)}, f32[256,1024]{1,0:T(8,128)}) fusion(f32[256,1024]{1,0:T(8,128)S(1)} %copy-done.18, f32[256,1024]{1,0:T(8,128)S(1)} %copy-done.21, f32[256,1024]{1,0:T(8,128)S(1)} %copy-done.22, bf16[256,1024]{1,0:T(8,128)(2,1)S(1)} %get-tuple-element.319), kind=kLoop, calls=%fused_computation.6 | loop fusion | flops 4194304 | bytes 7864320 | tf_op jit(solution)/shard_map/sub | solution.py:309
  (164 shorter events, 49.4 us)
Async XLA Ops:
  0.7 23.7 %collective-permute-start = (bf16[256,1024]{1,0:T(8,128)(2,1)}, bf16[256,1024]{1,0:T(8,128)(2,1)S(1)}, u32[]{:S(2)}, u32[]{:S(2)}) collective-permute-start(bf16[256,1024]{1,0:T(8,128)(2,1)} %refs_4_.5), channel_id=1, source_target_pairs={{0,8},{8,0},{16,24},{24,16},{1,9},{9,1},{17,25},{25,17},{2,10},{10... | collective-permute-start | bytes 1572872 | tf_op jit(solution)/shard_map/ppermute | solution.py:52
  3.7 20.7 %collective-permute-start.1 = (bf16[256,1024]{1,0:T(8,128)(2,1)}, bf16[256,1024]{1,0:T(8,128)(2,1)S(1)}, u32[]{:S(2)}, u32[]{:S(2)}) collective-permute-start(bf16[256,1024]{1,0:T(8,128)(2,1)} %refs_4_.5), channel_id=1, source_target_pairs={{0,16},{8,24},{16,0},{24,8},{1,17},{9,25},{17,1},{25,9},{2,18},{10... | collective-permute-start | bytes 1572872 | tf_op jit(solution)/shard_map/ppermute | solution.py:52
  13.3 11.0 %collective-permute-start.7 = (bf16[80,1024]{1,0:T(8,128)(2,1)}, bf16[80,1024]{1,0:T(8,128)(2,1)S(1)}, u32[]{:S(2)}, u32[]{:S(2)}) collective-permute-start(bf16[80,1024]{1,0:T(8,128)(2,1)} %get-tuple-element.185), channel_id=1, source_target_pairs={{0,16},{8,24},{16,0},{24,8},{1,17},{9,25},{17,1},{25,9},{2,18},{10... | collective-permute-start | bytes 491528 | tf_op jit(solution)/shard_map/ppermute | solution.py:52
  13.8 10.5 %collective-permute-start.8 = (bf16[80,1024]{1,0:T(8,128)(2,1)}, bf16[80,1024]{1,0:T(8,128)(2,1)S(1)}, u32[]{:S(2)}, u32[]{:S(2)}) collective-permute-start(bf16[80,1024]{1,0:T(8,128)(2,1)} %get-tuple-element.186), channel_id=1, source_target_pairs={{0,24},{8,16},{16,8},{24,0},{1,25},{9,17},{17,9},{25,1},{2,26},{10... | collective-permute-start | bytes 491528 | tf_op jit(solution)/shard_map/ppermute | solution.py:52
  15.3 9.0 %collective-permute-start.2 = (bf16[80,1024]{1,0:T(8,128)(2,1)}, bf16[80,1024]{1,0:T(8,128)(2,1)S(1)}, u32[]{:S(2)}, u32[]{:S(2)}) collective-permute-start(bf16[80,1024]{1,0:T(8,128)(2,1)} %get-tuple-element.175), channel_id=1, source_target_pairs={{0,8},{8,0},{16,24},{24,16},{1,9},{9,1},{17,25},{25,17},{2,10},{10... | collective-permute-start | bytes 491528 | tf_op jit(solution)/shard_map/ppermute | solution.py:52
  24.4 6.9 %collective-permute-start.3 = (bf16[128,1024]{1,0:T(8,128)(2,1)S(1)}, bf16[128,1024]{1,0:T(8,128)(2,1)S(1)}, u32[]{:S(2)}, u32[]{:S(2)}) collective-permute-start(bf16[128,1024]{1,0:T(8,128)(2,1)S(1)} %slice.75), channel_id=1, source_target_pairs={{0,16},{8,24},{16,0},{24,8},{1,17},{9,25},{17,1},{25,9},{2,18},{10... | collective-permute-start | bytes 786440 | tf_op jit(solution)/shard_map/ppermute | solution.py:52
  26.7 9.2 %collective-permute-start.9 = (bf16[192,1024]{1,0:T(8,128)(2,1)S(1)}, bf16[192,1024]{1,0:T(8,128)(2,1)S(1)}, u32[]{:S(2)}, u32[]{:S(2)}) collective-permute-start(bf16[192,1024]{1,0:T(8,128)(2,1)S(1)} %pad_maximum_fusion), channel_id=1, source_target_pairs={{0,2},{1,3},{2,0},{3,1},{4,6},{5,7},{6,4},{7,5},{8,10},{9,11},{10,... | collective-permute-start | bytes 1179656 | tf_op jit(solution)/shard_map/ppermute | solution.py:92
  32.7 12.5 %collective-permute-start.5 = (bf16[256,1024]{1,0:T(8,128)(2,1)S(1)}, bf16[256,1024]{1,0:T(8,128)(2,1)S(1)}, u32[]{:S(2)}, u32[]{:S(2)}) collective-permute-start(bf16[256,1024]{1,0:T(8,128)(2,1)S(1)} %copy-done.9), channel_id=1, source_target_pairs={{0,8},{8,0},{16,24},{24,16},{1,9},{9,1},{17,25},{25,17},{2,10},{10... | collective-permute-start | bytes 1572872 | tf_op jit(solution)/shard_map/ppermute | solution.py:52
  33.2 12.0 %collective-permute-start.6 = (bf16[256,1024]{1,0:T(8,128)(2,1)S(1)}, bf16[256,1024]{1,0:T(8,128)(2,1)S(1)}, u32[]{:S(2)}, u32[]{:S(2)}) collective-permute-start(bf16[256,1024]{1,0:T(8,128)(2,1)S(1)} %copy-done.9), channel_id=1, source_target_pairs={{0,16},{8,24},{16,0},{24,8},{1,17},{9,25},{17,1},{25,9},{2,18},{10... | collective-permute-start | bytes 1572872 | tf_op jit(solution)/shard_map/ppermute | solution.py:52
  45.3 9.2 %collective-permute-start.12 = (bf16[128,1024]{1,0:T(8,128)(2,1)S(1)}, bf16[128,1024]{1,0:T(8,128)(2,1)S(1)}, u32[]{:S(2)}, u32[]{:S(2)}) collective-permute-start(bf16[128,1024]{1,0:T(8,128)(2,1)S(1)} %slice.80), channel_id=1, source_target_pairs={{0,16},{8,24},{16,0},{24,8},{1,17},{9,25},{17,1},{25,9},{2,18},{10... | collective-permute-start | bytes 786440 | tf_op jit(solution)/shard_map/ppermute | solution.py:52
  46.0 9.3 %collective-permute-start.13 = (bf16[128,1024]{1,0:T(8,128)(2,1)S(1)}, bf16[128,1024]{1,0:T(8,128)(2,1)S(1)}, u32[]{:S(2)}, u32[]{:S(2)}) collective-permute-start(bf16[128,1024]{1,0:T(8,128)(2,1)S(1)} %slice.81), channel_id=1, source_target_pairs={{0,8},{8,0},{16,24},{24,16},{1,9},{9,1},{17,25},{25,17},{2,10},{10... | collective-permute-start | bytes 786440 | tf_op jit(solution)/shard_map/ppermute | solution.py:52
  47.4 15.9 %collective-permute-start.14 = (bf16[128,768]{1,0:T(8,128)(2,1)S(1)}, bf16[128,768]{1,0:T(8,128)(2,1)S(1)}, u32[]{:S(2)}, u32[]{:S(2)}) collective-permute-start(bf16[128,768]{1,0:T(8,128)(2,1)S(1)} %copy-done.27), channel_id=1, source_target_pairs={{0,8},{8,0},{16,24},{24,16},{1,9},{9,1},{17,25},{25,17},{2,10},{10... | collective-permute-start | bytes 589832 | tf_op jit(solution)/shard_map/ppermute | solution.py:52
  48.1 15.3 %collective-permute-start.15 = (bf16[128,768]{1,0:T(8,128)(2,1)S(1)}, bf16[128,768]{1,0:T(8,128)(2,1)S(1)}, u32[]{:S(2)}, u32[]{:S(2)}) collective-permute-start(bf16[128,768]{1,0:T(8,128)(2,1)S(1)} %copy-done.26), channel_id=1, source_target_pairs={{0,16},{8,24},{16,0},{24,8},{1,17},{9,25},{17,1},{25,9},{2,18},{10... | collective-permute-start | bytes 589832 | tf_op jit(solution)/shard_map/ppermute | solution.py:52
  49.5 13.9 %collective-permute-start.16 = (bf16[128,768]{1,0:T(8,128)(2,1)S(1)}, bf16[128,768]{1,0:T(8,128)(2,1)S(1)}, u32[]{:S(2)}, u32[]{:S(2)}) collective-permute-start(bf16[128,768]{1,0:T(8,128)(2,1)S(1)} %copy-done.25), channel_id=1, source_target_pairs={{0,24},{8,16},{16,8},{24,0},{1,25},{9,17},{17,9},{25,1},{2,26},{10... | collective-permute-start | bytes 589832 | tf_op jit(solution)/shard_map/ppermute | solution.py:52
  70.7 22.6 %collective-permute-start.23 = (bf16[128,1024]{1,0:T(8,128)(2,1)S(1)}, bf16[128,1024]{1,0:T(8,128)(2,1)S(1)}, u32[]{:S(2)}, u32[]{:S(2)}) collective-permute-start(bf16[128,1024]{1,0:T(8,128)(2,1)S(1)} %get-tuple-element.227), channel_id=1, source_target_pairs={{0,8},{8,0},{16,24},{24,16},{1,9},{9,1},{17,25},{25,17},{2,10},{10... | collective-permute-start | bytes 786440 | tf_op jit(solution)/shard_map/ppermute | solution.py:52
  72.1 21.2 %collective-permute-start.24 = (bf16[128,1024]{1,0:T(8,128)(2,1)S(1)}, bf16[128,1024]{1,0:T(8,128)(2,1)S(1)}, u32[]{:S(2)}, u32[]{:S(2)}) collective-permute-start(bf16[128,1024]{1,0:T(8,128)(2,1)S(1)} %get-tuple-element.228), channel_id=1, source_target_pairs={{0,16},{8,24},{16,0},{24,8},{1,17},{9,25},{17,1},{25,9},{2,18},{10... | collective-permute-start | bytes 786440 | tf_op jit(solution)/shard_map/ppermute | solution.py:52
  73.6 19.7 %collective-permute-start.25 = (bf16[128,1024]{1,0:T(8,128)(2,1)S(1)}, bf16[128,1024]{1,0:T(8,128)(2,1)S(1)}, u32[]{:S(2)}, u32[]{:S(2)}) collective-permute-start(bf16[128,1024]{1,0:T(8,128)(2,1)S(1)} %get-tuple-element.229), channel_id=1, source_target_pairs={{0,24},{8,16},{16,8},{24,0},{1,25},{9,17},{17,9},{25,1},{2,26},{10... | collective-permute-start | bytes 786440 | tf_op jit(solution)/shard_map/ppermute | solution.py:52
  74.2 25.3 %collective-permute-start.22 = (bf16[512,1024]{1,0:T(8,128)(2,1)S(1)}, bf16[512,1024]{1,0:T(8,128)(2,1)S(1)}, u32[]{:S(2)}, u32[]{:S(2)}) collective-permute-start(bf16[512,1024]{1,0:T(8,128)(2,1)S(1)} %add.91.refs_0_), channel_id=1, source_target_pairs={{0,2},{1,3},{6,4},{7,5},{8,10},{9,11},{14,12},{15,13},{16,18},{17,... | collective-permute-start | bytes 3145736 | tf_op jit(solution)/shard_map/ppermute | solution.py:92
  93.3 6.8 %collective-permute-start.26 = (bf16[4,128,768]{2,1,0:T(8,128)(2,1)S(1)}, bf16[4,128,768]{2,1,0:T(8,128)(2,1)S(1)}, u32[]{:S(2)}, u32[]{:S(2)}) collective-permute-start(bf16[4,128,768]{2,1,0:T(8,128)(2,1)S(1)} %get-tuple-element.248), channel_id=1, source_target_pairs={{0,1},{1,0},{2,3},{3,2},{4,5},{5,4},{6,7},{7,6},{8,9},{9,8},{10,11... | collective-permute-start | bytes 2359304 | tf_op jit(solution)/shard_map/ppermute | solution.py:72
  100.9 14.0 %collective-permute-start.30 = (bf16[256,768]{1,0:T(8,128)(2,1)S(1)}, bf16[256,768]{1,0:T(8,128)(2,1)S(1)}, u32[]{:S(2)}, u32[]{:S(2)}) collective-permute-start(bf16[256,768]{1,0:T(8,128)(2,1)S(1)} %get-tuple-element.264), channel_id=1, source_target_pairs={{0,8},{8,0},{16,24},{24,16},{1,9},{9,1},{17,25},{25,17},{2,10},{10... | collective-permute-start | bytes 1179656 | tf_op jit(solution)/shard_map/ppermute | solution.py:52
  102.5 25.7 %collective-permute-start.28 = (bf16[528,1024]{1,0:T(8,128)(2,1)S(1)}, bf16[528,1024]{1,0:T(8,128)(2,1)S(1)}, u32[]{:S(2)}, u32[]{:S(2)}) collective-permute-start(bf16[528,1024]{1,0:T(8,128)(2,1)S(1)} %broadcast_dynamic-update-slice_fusion.refs_0_), channel_id=1, source_target_pairs={{0,2},{1,3},{6,4},{7,5},{8,10},{9,11},{14,12},{15,13},{16,18},{17,... | collective-permute-start | bytes 3244040 | tf_op jit(solution)/shard_map/ppermute | solution.py:92
  106.9 19.1 %collective-permute-start.29 = (bf16[512,1024]{1,0:T(8,128)(2,1)S(1)}, bf16[512,1024]{1,0:T(8,128)(2,1)S(1)}, u32[]{:S(2)}, u32[]{:S(2)}) collective-permute-start(bf16[512,1024]{1,0:T(8,128)(2,1)S(1)} %shard_map.350.refs_2_), channel_id=1, source_target_pairs={{2,4},{3,5},{4,2},{5,3},{10,12},{11,13},{12,10},{13,11},{18,20},{1... | collective-permute-start | bytes 3145736 | tf_op jit(solution)/shard_map/ppermute | solution.py:92
  115.0 10.3 %collective-permute-start.31 = (bf16[256,768]{1,0:T(8,128)(2,1)S(1)}, bf16[256,768]{1,0:T(8,128)(2,1)S(1)}, u32[]{:S(2)}, u32[]{:S(2)}) collective-permute-start(bf16[256,768]{1,0:T(8,128)(2,1)S(1)} %pad_maximum_fusion.1), channel_id=1, source_target_pairs={{0,16},{8,24},{16,0},{24,8},{1,17},{9,25},{17,1},{25,9},{2,18},{10... | collective-permute-start | bytes 1179656 | tf_op jit(solution)/shard_map/ppermute | solution.py:52
  128.9 24.4 %collective-permute-start.34 = (bf16[528,1024]{1,0:T(8,128)(2,1)S(1)}, bf16[528,1024]{1,0:T(8,128)(2,1)S(1)}, u32[]{:S(2)}, u32[]{:S(2)}) collective-permute-start(bf16[528,1024]{1,0:T(8,128)(2,1)S(1)} %get-tuple-element.283.refs_4_), channel_id=1, source_target_pairs={{0,2},{1,3},{2,0},{3,1},{4,6},{5,7},{6,4},{7,5},{8,10},{9,11},{10,... | collective-permute-start | bytes 3244040 | tf_op jit(solution)/shard_map/ppermute | solution.py:92
  132.1 21.2 %collective-permute-start.35 = (bf16[528,1024]{1,0:T(8,128)(2,1)S(1)}, bf16[528,1024]{1,0:T(8,128)(2,1)S(1)}, u32[]{:S(2)}, u32[]{:S(2)}) collective-permute-start(bf16[528,1024]{1,0:T(8,128)(2,1)S(1)} %get-tuple-element.284.refs_2_), channel_id=1, source_target_pairs={{2,4},{3,5},{4,2},{5,3},{10,12},{11,13},{12,10},{13,11},{18,20},{1... | collective-permute-start | bytes 3244040 | tf_op jit(solution)/shard_map/ppermute | solution.py:92
  132.9 22.0 %collective-permute-start.36 = (bf16[256,2048]{1,0:T(8,128)(2,1)S(1)}, bf16[256,2048]{1,0:T(8,128)(2,1)S(1)}, u32[]{:S(2)}, u32[]{:S(2)}) collective-permute-start(bf16[256,2048]{1,0:T(8,128)(2,1)S(1)} %get-tuple-element.288), channel_id=1, source_target_pairs={{0,8},{8,0},{16,24},{24,16},{1,9},{9,1},{17,25},{25,17},{2,10},{10... | collective-permute-start | bytes 3145736 | tf_op jit(solution)/shard_map/ppermute | solution.py:52
  133.5 21.7 %collective-permute-start.37 = (bf16[256,2048]{1,0:T(8,128)(2,1)S(1)}, bf16[256,2048]{1,0:T(8,128)(2,1)S(1)}, u32[]{:S(2)}, u32[]{:S(2)}) collective-permute-start(bf16[256,2048]{1,0:T(8,128)(2,1)S(1)} %get-tuple-element.289), channel_id=1, source_target_pairs={{0,16},{8,24},{16,0},{24,8},{1,17},{9,25},{17,1},{25,9},{2,18},{10... | collective-permute-start | bytes 3145736 | tf_op jit(solution)/shard_map/ppermute | solution.py:52
  156.1 12.7 %collective-permute-start.38 = (bf16[528,1024]{1,0:T(8,128)(2,1)S(1)}, bf16[528,1024]{1,0:T(8,128)(2,1)S(1)}, u32[]{:S(2)}, u32[]{:S(2)}) collective-permute-start(bf16[528,1024]{1,0:T(8,128)(2,1)S(1)} %get-tuple-element.291.refs_0_), channel_id=1, source_target_pairs={{2,4},{3,5},{4,2},{5,3},{10,12},{11,13},{12,10},{13,11},{18,20},{1... | collective-permute-start | bytes 3244040 | tf_op jit(solution)/shard_map/ppermute | solution.py:92
  156.9 27.0 %collective-permute-start.39 = (bf16[528,1024]{1,0:T(8,128)(2,1)S(1)}, bf16[528,1024]{1,0:T(8,128)(2,1)S(1)}, u32[]{:S(2)}, u32[]{:S(2)}) collective-permute-start(bf16[528,1024]{1,0:T(8,128)(2,1)S(1)} %get-tuple-element.292.refs_2_), channel_id=1, source_target_pairs={{2,0},{3,1},{4,6},{5,7},{10,8},{11,9},{12,14},{13,15},{18,16},{19,... | collective-permute-start | bytes 3244040 | tf_op jit(solution)/shard_map/ppermute | solution.py:92
  158.3 26.3 %collective-permute-start.41 = (bf16[256,1024]{1,0:T(8,128)(2,1)S(1)}, bf16[256,1024]{1,0:T(8,128)(2,1)S(1)}, u32[]{:S(2)}, u32[]{:S(2)}) collective-permute-start(bf16[256,1024]{1,0:T(8,128)(2,1)S(1)} %slice.96), channel_id=1, source_target_pairs={{0,24},{8,16},{16,8},{24,0},{1,25},{9,17},{17,9},{25,1},{2,26},{10... | collective-permute-start | bytes 1572872 | tf_op jit(solution)/shard_map/ppermute | solution.py:52
  184.7 28.1 %collective-permute-start.42 = (bf16[528,1024]{1,0:T(8,128)(2,1)S(1)}, bf16[528,1024]{1,0:T(8,128)(2,1)S(1)}, u32[]{:S(2)}, u32[]{:S(2)}) collective-permute-start(bf16[528,1024]{1,0:T(8,128)(2,1)S(1)} %get-tuple-element.301.refs_0_), channel_id=1, source_target_pairs={{2,0},{3,1},{4,6},{5,7},{10,8},{11,9},{12,14},{13,15},{18,16},{19,... | collective-permute-start | bytes 3244040 | tf_op jit(solution)/shard_map/ppermute | solution.py:92
  186.3 15.3 %collective-permute-start.44 = (bf16[256,1024]{1,0:T(8,128)(2,1)S(1)}, bf16[256,1024]{1,0:T(8,128)(2,1)S(1)}, u32[]{:S(2)}, u32[]{:S(2)}) collective-permute-start(bf16[256,1024]{1,0:T(8,128)(2,1)S(1)} %slice.97), channel_id=1, source_target_pairs={{0,24},{8,16},{16,8},{24,0},{1,25},{9,17},{17,9},{25,1},{2,26},{10... | collective-permute-start | bytes 1572872 | tf_op jit(solution)/shard_map/ppermute | solution.py:52
  (42 other events, 572.7 us)

commit v6 on v5

--- a/solution.py
+++ b/solution.py
@@ -543,12 +543,14 @@
 
         @pl.when(block == groups - 1)
         def _():
-            def piece(i, carry):
-                grad = (dot_lt(mlp_ref[:, part((me ^ i) * (2 * half), 2 * half)], up_ref[...]) * scale).astype(BF)
-                keep_ref[i], away_ref[i] = halves(grad, core)
+            def pair(i, carry):
+                grad = (dot_lt(mlp_ref[:, part(i * (4 * half), 4 * half)], up_ref[...]) * scale).astype(BF)
+                for j in range(2):
+                    step = me ^ (2 * i + j)
+                    keep_ref[step], away_ref[step] = halves(grad[j * 2 * half : (j + 1) * 2 * half], core)
                 return carry
 
-            lax.fori_loop(0, groups, piece, 0)
+            lax.fori_loop(0, groups // 2, pair, 0)
 
     in_specs = [full(None)] * (n_c + 1) + [by_row((rows, ff)), full(w_down.shape), full(in_mlp.shape)]
     outs = [
@@ -734,12 +736,14 @@
     def body(s_ref, a_ref, proj_ref, heads_ref, branch_ref, out_away, out_keep, qkv_away, qkv_keep):
         me, core = s_ref[0], s_ref[1]
 
-        def piece(i, carry):
-            grad = (dot_lt(a_ref[:, part((me ^ i) * wide, wide)], proj_ref[...]) * scale).astype(BF)
-            qkv_keep[i], qkv_away[i] = halves(grad, core)
+        def pair(i, carry):
+            grad = (dot_lt(a_ref[:, part(i * (2 * wide), 2 * wide)], proj_ref[...]) * scale).astype(BF)
+            for j in range(2):
+                step = me ^ (2 * i + j)
+                qkv_keep[step], qkv_away[step] = halves(grad[j * wide : (j + 1) * wide], core)
             return carry
 
-        lax.fori_loop(0, groups, piece, 0)
+        lax.fori_loop(0, groups // 2, pair, 0)
         grad = (dot_lt(heads_ref[...], branch_ref[...]) * scale).astype(BF)
         out_keep[...], out_away[...] = halves(grad, core)
 

time: 226 us -> 226 us (level)
  waiting for transfers between devices: 84.3 us -> 86.9 us
  transfers between devices with their start and end apart: 46 -> 46, of which waited for: 20 -> 22; matrix products, arithmetic and copies ran while one was open for 0% -> 0% of each run, Pallas kernels for 33% -> 32%
where the time goes in v6:
time: 226 us; the launch traced here: 225 us
  waiting for transfers between devices  86.9 us (38%)
  Pallas kernels  75.4 us (33%)
  starting transfers between devices  49.3 us (22%)
  other arithmetic  9.75 us (4%)
  local copies, waits for them, and re-layouts  2.49 us (1%)
    ppermute x9, waiting for transfers between devices, place_send(): lax.ppermute(value, 'dp', [(2 * a + core, 2 * b + core) for a, b in pairs...  49.5 us
    ppermute x23, starting transfers between devices, shard_swap(): return lax.ppermute(value, 'shard', [(i, i ^ step) for i in range(size)])  27.7 us
    ppermute x23, waiting for transfers between devices, shard_swap(): return lax.ppermute(value, 'shard', [(i, i ^ step) for i in range(size)])  23.9 us
    ppermute x9, starting transfers between devices, place_send(): lax.ppermute(value, 'dp', [(2 * a + core, 2 * b + core) for a, b in pairs...  17.9 us
    pallas_call x2, Pallas kernels, adam_blocks(): kernel_call(body, grid, [full(None)] * len(grads) + [spec] * 3, [(shape,...  15.9 us
    pallas_call x1, Pallas kernels, attention(): kernel_call(body, (groups,), in_specs, outs, (), 0.0)  11.4 us
    sub x3, other arithmetic, adam_terms(): return (weight - rate * (step_size + decay * weight), first_new, second_new)  8.57 us
    pallas_call x1, Pallas kernels, backward_up(): kernel_call(body, (groups,), in_specs, outs, [pltpu.VMEM((rows, width), B...  7.58 us
  transfers between devices with their start and end apart: 46, of which 22 were waited for; matrix products, arithmetic and copies ran while one was open for 0% of the time, Pallas kernels for 32%

profile of v6, /device:TPU:0, one launch (start us, length us, event | category | flops | bytes accessed | tf_op | source)
XLA Modules:
  0.0 225.2 jit_solution(1308840946578732882)
XLA Ops:
  0.7 3.0 %collective-permute-start = (bf16[256,1024]{1,0:T(8,128)(2,1)}, bf16[256,1024]{1,0:T(8,128)(2,1)S(1)}, u32[]{:S(2)}, u32[]{:S(2)}) collective-permute-start(bf16[256,1024]{1,0:T(8,128)(2,1)} %refs_4_.5), channel_id=1, source_target_pairs={{0,8},{8,0},{16,24},{24,16},{1,9},{9,1},{17,25},{25,17},{2,10},{10... | collective-permute-start | bytes 1572872 | tf_op jit(solution)/shard_map/ppermute | solution.py:52
  5.8 7.5 %shard_map.345 = (bf16[256,1024]{1,0:T(8,128)(2,1)}, bf16[256,768]{1,0:T(8,128)(2,1)}, bf16[80,1024]{1,0:T(8,128)(2,1)}, bf16[128,768]{1,0:T(8,128)(2,1)}, bf16[...) custom-call(s32[4]{0:T(128)} %pad_add_fusion.s_ref, ...), custom_call_target="tpu_custom_call" | custom-call | bytes 22400000 | tf_op jit(solution)/shard_map/pallas_call | solution.py:381
  16.8 7.5 %collective-permute-done.7.refs_7_ = bf16[80,1024]{1,0:T(8,128)(2,1)S(1)} collective-permute-done((bf16[80,1024]{1,0:T(8,128)(2,1)}, bf16[80,1024]{1,0:T(8,128)(2,1)S(1)}, u32[]{:S(2)}, u32[]{:S(2)}) %collective-permute-start.7) | collective-permute-done | bytes 163872 | tf_op jit(solution)/shard_map/ppermute | solution.py:52
  28.3 3.0 %collective-permute-done.3.refs_3_ = bf16[128,1024]{1,0:T(8,128)(2,1)S(1)} collective-permute-done((bf16[128,1024]{1,0:T(8,128)(2,1)S(1)}, bf16[128,1024]{1,0:T(8,128)(2,1)S(1)}, u32[]{:S(2)}, u32[]{:S(2)}) %collective-permute-start.3) | collective-permute-done | bytes 262176 | tf_op jit(solution)/shard_map/ppermute | solution.py:52
  33.9 2.0 collective-permute-done.9.refs_9_
  38.7 6.6 %shard_map.346 = (bf16[1024,1024]{1,0:T(8,128)(2,1)S(1)}, bf16[1024,1024]{1,0:T(8,128)(2,1)S(1)}, bf16[1024,1024]{1,0:T(8,128)(2,1)S(1)}, f32[1024,1024]{1,0:T(8...) custom-call(s32[4]{0:T(128)S(1)} %copy-done.14, ...), custom_call_target="tpu_custom_call" | custom-call | bytes 20800000 | tf_op jit(solution)/shard_map/pallas_call | solution.py:480
  50.9 3.6 %collective-permute-done.12.refs_3_ = bf16[128,1024]{1,0:T(8,128)(2,1)S(1)} collective-permute-done((bf16[128,1024]{1,0:T(8,128)(2,1)S(1)}, bf16[128,1024]{1,0:T(8,128)(2,1)S(1)}, u32[]{:S(2)}, u32[]{:S(2)}) %collective-permute-start.12) | collective-permute-done | bytes 262176 | tf_op jit(solution)/shard_map/ppermute | solution.py:52
  55.3 7.6 %shard_map.347 = (bf16[1024,1024]{1,0:T(8,128)(2,1)S(1)}, f32[8,1024]{1,0:T(8,128)S(1)}, bf16[4,128,1024]{2,1,0:T(8,128)(2,1)S(1)}, bf16[4,128,1024]{2,1,0:T(8,1...) custom-call(s32[4]{0:T(128)S(1)} %copy-done.14, bf16[256,1024]{1,0:T(8,128)(2,1)S(1)} %copy-done.9, ...), custom_call_target="tpu_custom_call" | custom-call | bytes 21760000 | tf_op jit(solution)/shard_map/pallas_call | solution.py:564
  64.4 2.9 %shard_map.348 = (bf16[512,1024]{1,0:T(8,128)(2,1)S(1)}, bf16[512,1024]{1,0:T(8,128)(2,1)S(1)}) custom-call(s32[4]{0:T(128)S(1)} %copy-done.14, bf16[1024,1024]{1,0:T(8,128)(2,1)S(1)} %get-tuple-element.231.branch_ref.refs_1_, bf16[1024,1024]{1,0:T(8,128)(2,1)S(1)} %get-tuple-element.250.act_ref), custom_call_target="tpu_custom_call" | custom-call | bytes 9600000 | tf_op jit(solution)/shard_map/pallas_call | solution.py:495
  67.5 1.8 shard_map.349
  74.2 3.7 %collective-permute-start.22 = (bf16[512,1024]{1,0:T(8,128)(2,1)S(1)}, bf16[512,1024]{1,0:T(8,128)(2,1)S(1)}, u32[]{:S(2)}, u32[]{:S(2)}) collective-permute-start(bf16[512,1024]{1,0:T(8,128)(2,1)S(1)} %add.91.refs_0_), channel_id=1, source_target_pairs={{0,2},{1,3},{6,4},{7,5},{8,10},{9,11},{14,12},{15,13},{16,18},{17,... | collective-permute-start | bytes 3145736 | tf_op jit(solution)/shard_map/ppermute | solution.py:92
  77.9 11.4 %shard_map.351 = (bf16[1024,256]{1,0:T(8,128)(2,1)S(1)}, bf16[1024,768]{1,0:T(8,128)(2,1)S(1)}, f32[8,768]{1,0:T(8,128)S(1)}, bf16[1024,768]{1,0:T(8,128)(2,1)S(1)}) custom-call(s32[4]{0:T(128)S(1)} %copy-done.14, bf16[1024,1024]{1,0:T(8,128)(2,1)S(1)} %get-tuple-element.230.refs_0_.a_ref, bf16[1024,1024]{1,0:T(8,128)(2,1)S(1)} %get-tuple-element.231.branch_ref.refs_1_, ...), custom_call_target="tpu_custom_call" | custom-call | tf_op jit(solution)/shard_map/pallas_call | solution.py:656
  89.3 3.5 %shard_map.352 = (bf16[128,1024]{1,0:T(8,128)(2,1)S(1)}, bf16[128,1024]{1,0:T(8,128)(2,1)S(1)}, bf16[4,128,768]{2,1,0:T(8,128)(2,1)S(1)}, bf16[4,128,768]{2,1,0:T(8,128)(2,1)S(1)}) custom-call(s32[4]{0:T(128)S(1)} %copy-done.14, bf16[1024,1024]{1,0:T(8,128)(2,1)S(1)} %get-tuple-element.230.refs_0_.a_ref, ...), custom_call_target="tpu_custom_call" | custom-call | tf_op jit(solution)/shard_map/pallas_call | solution.py:753
  93.4 3.4 %shard_map.353.refs_6_ = bf16[1024,1024]{1,0:T(8,128)(2,1)S(1)} custom-call(s32[4]{0:T(128)S(1)} %copy-done.14, bf16[1024,1024]{1,0:T(8,128)(2,1)S(1)} %get-tuple-element.250.act_ref, bf16[1024,1024]{1,0:T(8,128)(2,1)S(1)} %copy-done.2), custom_call_target="tpu_custom_call" | custom-call | bytes 9600000 | tf_op jit(solution)/shard_map/pallas_call | solution.py:507
  96.8 2.7 %collective-permute-done.22.refs_1_ = bf16[512,1024]{1,0:T(8,128)(2,1)S(1)} collective-permute-done((bf16[512,1024]{1,0:T(8,128)(2,1)S(1)}, bf16[512,1024]{1,0:T(8,128)(2,1)S(1)}, u32[]{:S(2)}, u32[]{:S(2)}) %collective-permute-start.22) | collective-permute-done | bytes 1048608 | tf_op jit(solution)/shard_map/ppermute | solution.py:92
  102.5 4.4 %collective-permute-start.28 = (bf16[528,1024]{1,0:T(8,128)(2,1)S(1)}, bf16[528,1024]{1,0:T(8,128)(2,1)S(1)}, u32[]{:S(2)}, u32[]{:S(2)}) collective-permute-start(bf16[528,1024]{1,0:T(8,128)(2,1)S(1)} %broadcast_dynamic-update-slice_fusion.refs_0_), channel_id=1, source_target_pairs={{0,2},{1,3},{6,4},{7,5},{8,10},{9,11},{14,12},{15,13},{16,18},{17,... | collective-permute-start | bytes 3244040 | tf_op jit(solution)/shard_map/ppermute | solution.py:92
  107.6 7.2 %shard_map.355 = (bf16[256,2048]{1,0:T(8,128)(2,1)S(1)}, bf16[256,2048]{1,0:T(8,128)(2,1)S(1)}, bf16[256,2048]{1,0:T(8,128)(2,1)S(1)}, bf16[256,2048]{1,0:T(8,128)(2,1)S(1)}, f32[16,1024]{1,0:T(8,128)S(1)}) custom-call(s32[4]{0:T(128)S(1)} %copy-done.14, bf16[256,1024]{1,0:T(8,128)(2,1)S(1)} %copy-done.3, ...), custom_call_target="tpu_custom_call" | custom-call | tf_op jit(solution)/shard_map/pallas_call | solution.py:720
  116.7 3.7 %collective-permute-done.32 = f32[16,1024]{1,0:T(8,128)S(1)} collective-permute-done((f32[16,1024]{1,0:T(8,128)S(1)}, f32[16,1024]{1,0:T(8,128)S(1)}, u32[]{:S(2)}, u32[]{:S(2)}) %collective-permute-start.32) | collective-permute-done | bytes 65568 | tf_op jit(solution)/shard_map/ppermute | solution.py:792
  121.5 3.8 %collective-permute-done.33 = f32[16,1024]{1,0:T(8,128)S(1)} collective-permute-done((f32[16,1024]{1,0:T(8,128)S(1)}, f32[16,1024]{1,0:T(8,128)S(1)}, u32[]{:S(2)}, u32[]{:S(2)}) %collective-permute-start.33) | collective-permute-done | bytes 65568 | tf_op jit(solution)/shard_map/ppermute | solution.py:792
  126.0 2.2 collective-permute-done.28.refs_1_
  128.9 3.2 %collective-permute-start.34 = (bf16[528,1024]{1,0:T(8,128)(2,1)S(1)}, bf16[528,1024]{1,0:T(8,128)(2,1)S(1)}, u32[]{:S(2)}, u32[]{:S(2)}) collective-permute-start(bf16[528,1024]{1,0:T(8,128)(2,1)S(1)} %get-tuple-element.283.refs_4_), channel_id=1, source_target_pairs={{0,2},{1,3},{2,0},{3,1},{4,6},{5,7},{6,4},{7,5},{8,10},{9,11},{10,... | collective-permute-start | bytes 3244040 | tf_op jit(solution)/shard_map/ppermute | solution.py:92
  134.5 18.9 %collective-permute-done.34.refs_1_.refs_5_ = bf16[528,1024]{1,0:T(8,128)(2,1)S(1)} collective-permute-done((bf16[528,1024]{1,0:T(8,128)(2,1)S(1)}, bf16[528,1024]{1,0:T(8,128)(2,1)S(1)}, u32[]{:S(2)}, u32[]{:S(2)}) %collective-permute-start.34) | collective-permute-done | bytes 1081376 | tf_op jit(solution)/shard_map/ppermute | solution.py:92
  158.3 1.9 collective-permute-start.41
  160.9 7.9 %shard_map.360 = (f32[1024,1024]{1,0:T(8,128)}, f32[1024,1024]{1,0:T(8,128)}, f32[1024,1024]{1,0:T(8,128)}, f32[1024,1024]{1,0:T(8,128)}) custom-call(s32[4]{0:T(128)S(1)} %copy-done.14, bf16[512,1024]{1,0:T(8,128)(2,1)S(1)} %get-tuple-element.295.refs_0_, bf16[512,1024]{1,0:T(8,128)(2,1)S(1)} %collective-permute-done.40.refs_1_, f32[1024,1024]{1,0:T(8,128)S(1)} %copy-done, ...), custom_call_target="tpu_custom_call" | custom-call | tf_op jit(solution)/shard_map/pallas_call | solution.py:867
  168.9 15.0 %collective-permute-done.39.refs_3_ = bf16[528,1024]{1,0:T(8,128)(2,1)S(1)} collective-permute-done((bf16[528,1024]{1,0:T(8,128)(2,1)S(1)}, bf16[528,1024]{1,0:T(8,128)(2,1)S(1)}, u32[]{:S(2)}, u32[]{:S(2)}) %collective-permute-start.39) | collective-permute-done | bytes 1081376 | tf_op jit(solution)/shard_map/ppermute | solution.py:92
  187.4 8.0 %shard_map.362 = (f32[256,4096]{1,0:T(8,128)}, f32[256,4096]{1,0:T(8,128)}, f32[256,4096]{1,0:T(8,128)}, f32[256,4096]{1,0:T(8,128)}) custom-call(s32[4]{0:T(128)S(1)} %copy-done.14, bf16[528,1024]{1,0:T(8,128)(2,1)S(1)} %get-tuple-element.302.refs_0_, bf16[528,1024]{1,0:T(8,128)(2,1)S(1)} %collective-permute-done.43.refs_1_, f32[256,4096]{1,0:T(8,128)S(1)} %copy-done.1, ...), custom_call_target="tpu_custom_call" | custom-call | tf_op jit(solution)/shard_map/pallas_call | solution.py:867
  195.4 6.2 %collective-permute-done.44.refs_3_ = bf16[256,1024]{1,0:T(8,128)(2,1)S(1)} collective-permute-done((bf16[256,1024]{1,0:T(8,128)(2,1)S(1)}, bf16[256,1024]{1,0:T(8,128)(2,1)S(1)}, u32[]{:S(2)}, u32[]{:S(2)}) %collective-permute-start.44) | collective-permute-done | bytes 524320 | tf_op jit(solution)/shard_map/ppermute | solution.py:52
  201.6 2.5 %shard_map.363 = (bf16[256,1024]{1,0:T(8,128)(2,1)}, bf16[256,1024]{1,0:T(8,128)(2,1)}) custom-call(s32[4]{0:T(128)S(1)} %copy-done.14, bf16[256,2048]{1,0:T(8,128)(2,1)S(1)} %get-tuple-element.307.own_ref, bf16[256,2048]{1,0:T(8,128)(2,1)S(1)} %collective-permute-done.36.refs_0_, bf16[256,2048]{1,0:T(8,128)(2,1)S(1)} %copy-done.11, ...), custom_call_target="tpu_custom_call" | custom-call | bytes 7680000 | tf_op jit(solution)/shard_map/pallas_call | solution.py:832
  204.0 8.8 %collective-permute-done.42.refs_1_ = bf16[528,1024]{1,0:T(8,128)(2,1)S(1)} collective-permute-done((bf16[528,1024]{1,0:T(8,128)(2,1)S(1)}, bf16[528,1024]{1,0:T(8,128)(2,1)S(1)}, u32[]{:S(2)}, u32[]{:S(2)}) %collective-permute-start.42) | collective-permute-done | bytes 1081376 | tf_op jit(solution)/shard_map/ppermute | solution.py:92
  213.5 2.7 %collective-permute-done.45.refs_1_ = bf16[528,1024]{1,0:T(8,128)(2,1)S(1)} collective-permute-done((bf16[528,1024]{1,0:T(8,128)(2,1)S(1)}, bf16[528,1024]{1,0:T(8,128)(2,1)S(1)}, u32[]{:S(2)}, u32[]{:S(2)}) %collective-permute-start.45) | collective-permute-done | bytes 1081376 | tf_op jit(solution)/shard_map/ppermute | solution.py:72
  216.6 5.6 %multiply_subtract_fusion = (f32[256,3072]{1,0:T(8,128)}, f32[256,3072]{1,0:T(8,128)}, f32[256,3072]{1,0:T(8,128)}, f32[256,3072]{1,0:T(8,128)}) fusion(f32[256,3072]{1,0:T(8,128)S(1)} %copy-done.17, f32[256,3072]{1,0:T(8,128)S(1)} %copy-done.19, f32[256,3072]{1,0:T(8,128)S(1)} %copy-done.20, bf16[256,3072]{1,0:T(8,128)(2,1)S(1)} %get-tuple-element.318), kind=kLoop, calls=%fused_computation.2 | loop fusion | flops 12582912 | bytes 23592960 | tf_op jit(solution)/shard_map/sub | solution.py:309
  222.2 2.3 %multiply_subtract_fusion.1 = (f32[256,1024]{1,0:T(8,128)}, f32[256,1024]{1,0:T(8,128)}, f32[256,1024]{1,0:T(8,128)}, f32[256,1024]{1,0:T(8,128)}) fusion(f32[256,1024]{1,0:T(8,128)S(1)} %copy-done.18, f32[256,1024]{1,0:T(8,128)S(1)} %copy-done.21, f32[256,1024]{1,0:T(8,128)S(1)} %copy-done.22, bf16[256,1024]{1,0:T(8,128)(2,1)S(1)} %get-tuple-element.319), kind=kLoop, calls=%fused_computation.6 | loop fusion | flops 4194304 | bytes 7864320 | tf_op jit(solution)/shard_map/sub | solution.py:309
  (164 shorter events, 49.4 us)
Async XLA Ops:
  0.7 23.7 %collective-permute-start = (bf16[256,1024]{1,0:T(8,128)(2,1)}, bf16[256,1024]{1,0:T(8,128)(2,1)S(1)}, u32[]{:S(2)}, u32[]{:S(2)}) collective-permute-start(bf16[256,1024]{1,0:T(8,128)(2,1)} %refs_4_.5), channel_id=1, source_target_pairs={{0,8},{8,0},{16,24},{24,16},{1,9},{9,1},{17,25},{25,17},{2,10},{10... | collective-permute-start | bytes 1572872 | tf_op jit(solution)/shard_map/ppermute | solution.py:52
  3.7 20.7 %collective-permute-start.1 = (bf16[256,1024]{1,0:T(8,128)(2,1)}, bf16[256,1024]{1,0:T(8,128)(2,1)S(1)}, u32[]{:S(2)}, u32[]{:S(2)}) collective-permute-start(bf16[256,1024]{1,0:T(8,128)(2,1)} %refs_4_.5), channel_id=1, source_target_pairs={{0,16},{8,24},{16,0},{24,8},{1,17},{9,25},{17,1},{25,9},{2,18},{10... | collective-permute-start | bytes 1572872 | tf_op jit(solution)/shard_map/ppermute | solution.py:52
  13.3 11.0 %collective-permute-start.7 = (bf16[80,1024]{1,0:T(8,128)(2,1)}, bf16[80,1024]{1,0:T(8,128)(2,1)S(1)}, u32[]{:S(2)}, u32[]{:S(2)}) collective-permute-start(bf16[80,1024]{1,0:T(8,128)(2,1)} %get-tuple-element.185), channel_id=1, source_target_pairs={{0,16},{8,24},{16,0},{24,8},{1,17},{9,25},{17,1},{25,9},{2,18},{10... | collective-permute-start | bytes 491528 | tf_op jit(solution)/shard_map/ppermute | solution.py:52
  13.8 10.5 %collective-permute-start.8 = (bf16[80,1024]{1,0:T(8,128)(2,1)}, bf16[80,1024]{1,0:T(8,128)(2,1)S(1)}, u32[]{:S(2)}, u32[]{:S(2)}) collective-permute-start(bf16[80,1024]{1,0:T(8,128)(2,1)} %get-tuple-element.186), channel_id=1, source_target_pairs={{0,24},{8,16},{16,8},{24,0},{1,25},{9,17},{17,9},{25,1},{2,26},{10... | collective-permute-start | bytes 491528 | tf_op jit(solution)/shard_map/ppermute | solution.py:52
  15.3 9.0 %collective-permute-start.2 = (bf16[80,1024]{1,0:T(8,128)(2,1)}, bf16[80,1024]{1,0:T(8,128)(2,1)S(1)}, u32[]{:S(2)}, u32[]{:S(2)}) collective-permute-start(bf16[80,1024]{1,0:T(8,128)(2,1)} %get-tuple-element.175), channel_id=1, source_target_pairs={{0,8},{8,0},{16,24},{24,16},{1,9},{9,1},{17,25},{25,17},{2,10},{10... | collective-permute-start | bytes 491528 | tf_op jit(solution)/shard_map/ppermute | solution.py:52
  26.7 9.2 %collective-permute-start.9 = (bf16[192,1024]{1,0:T(8,128)(2,1)S(1)}, bf16[192,1024]{1,0:T(8,128)(2,1)S(1)}, u32[]{:S(2)}, u32[]{:S(2)}) collective-permute-start(bf16[192,1024]{1,0:T(8,128)(2,1)S(1)} %pad_maximum_fusion), channel_id=1, source_target_pairs={{0,2},{1,3},{2,0},{3,1},{4,6},{5,7},{6,4},{7,5},{8,10},{9,11},{10,... | collective-permute-start | bytes 1179656 | tf_op jit(solution)/shard_map/ppermute | solution.py:92
  32.7 12.5 %collective-permute-start.5 = (bf16[256,1024]{1,0:T(8,128)(2,1)S(1)}, bf16[256,1024]{1,0:T(8,128)(2,1)S(1)}, u32[]{:S(2)}, u32[]{:S(2)}) collective-permute-start(bf16[256,1024]{1,0:T(8,128)(2,1)S(1)} %copy-done.9), channel_id=1, source_target_pairs={{0,8},{8,0},{16,24},{24,16},{1,9},{9,1},{17,25},{25,17},{2,10},{10... | collective-permute-start | bytes 1572872 | tf_op jit(solution)/shard_map/ppermute | solution.py:52
  33.2 12.0 %collective-permute-start.6 = (bf16[256,1024]{1,0:T(8,128)(2,1)S(1)}, bf16[256,1024]{1,0:T(8,128)(2,1)S(1)}, u32[]{:S(2)}, u32[]{:S(2)}) collective-permute-start(bf16[256,1024]{1,0:T(8,128)(2,1)S(1)} %copy-done.9), channel_id=1, source_target_pairs={{0,16},{8,24},{16,0},{24,8},{1,17},{9,25},{17,1},{25,9},{2,18},{10... | collective-permute-start | bytes 1572872 | tf_op jit(solution)/shard_map/ppermute | solution.py:52
  45.3 9.2 %collective-permute-start.12 = (bf16[128,1024]{1,0:T(8,128)(2,1)S(1)}, bf16[128,1024]{1,0:T(8,128)(2,1)S(1)}, u32[]{:S(2)}, u32[]{:S(2)}) collective-permute-start(bf16[128,1024]{1,0:T(8,128)(2,1)S(1)} %slice.80), channel_id=1, source_target_pairs={{0,16},{8,24},{16,0},{24,8},{1,17},{9,25},{17,1},{25,9},{2,18},{10... | collective-permute-start | bytes 786440 | tf_op jit(solution)/shard_map/ppermute | solution.py:52
  46.0 9.3 %collective-permute-start.13 = (bf16[128,1024]{1,0:T(8,128)(2,1)S(1)}, bf16[128,1024]{1,0:T(8,128)(2,1)S(1)}, u32[]{:S(2)}, u32[]{:S(2)}) collective-permute-start(bf16[128,1024]{1,0:T(8,128)(2,1)S(1)} %slice.81), channel_id=1, source_target_pairs={{0,8},{8,0},{16,24},{24,16},{1,9},{9,1},{17,25},{25,17},{2,10},{10... | collective-permute-start | bytes 786440 | tf_op jit(solution)/shard_map/ppermute | solution.py:52
  47.4 15.5 %collective-permute-start.14 = (bf16[128,768]{1,0:T(8,128)(2,1)S(1)}, bf16[128,768]{1,0:T(8,128)(2,1)S(1)}, u32[]{:S(2)}, u32[]{:S(2)}) collective-permute-start(bf16[128,768]{1,0:T(8,128)(2,1)S(1)} %copy-done.27), channel_id=1, source_target_pairs={{0,8},{8,0},{16,24},{24,16},{1,9},{9,1},{17,25},{25,17},{2,10},{10... | collective-permute-start | bytes 589832 | tf_op jit(solution)/shard_map/ppermute | solution.py:52
  48.1 14.8 %collective-permute-start.15 = (bf16[128,768]{1,0:T(8,128)(2,1)S(1)}, bf16[128,768]{1,0:T(8,128)(2,1)S(1)}, u32[]{:S(2)}, u32[]{:S(2)}) collective-permute-start(bf16[128,768]{1,0:T(8,128)(2,1)S(1)} %copy-done.26), channel_id=1, source_target_pairs={{0,16},{8,24},{16,0},{24,8},{1,17},{9,25},{17,1},{25,9},{2,18},{10... | collective-permute-start | bytes 589832 | tf_op jit(solution)/shard_map/ppermute | solution.py:52
  49.5 13.9 %collective-permute-start.16 = (bf16[128,768]{1,0:T(8,128)(2,1)S(1)}, bf16[128,768]{1,0:T(8,128)(2,1)S(1)}, u32[]{:S(2)}, u32[]{:S(2)}) collective-permute-start(bf16[128,768]{1,0:T(8,128)(2,1)S(1)} %copy-done.25), channel_id=1, source_target_pairs={{0,24},{8,16},{16,8},{24,0},{1,25},{9,17},{17,9},{25,1},{2,26},{10... | collective-permute-start | bytes 589832 | tf_op jit(solution)/shard_map/ppermute | solution.py:52
  70.6 22.2 %collective-permute-start.23 = (bf16[128,1024]{1,0:T(8,128)(2,1)S(1)}, bf16[128,1024]{1,0:T(8,128)(2,1)S(1)}, u32[]{:S(2)}, u32[]{:S(2)}) collective-permute-start(bf16[128,1024]{1,0:T(8,128)(2,1)S(1)} %get-tuple-element.227), channel_id=1, source_target_pairs={{0,8},{8,0},{16,24},{24,16},{1,9},{9,1},{17,25},{25,17},{2,10},{10... | collective-permute-start | bytes 786440 | tf_op jit(solution)/shard_map/ppermute | solution.py:52
  72.1 20.7 %collective-permute-start.24 = (bf16[128,1024]{1,0:T(8,128)(2,1)S(1)}, bf16[128,1024]{1,0:T(8,128)(2,1)S(1)}, u32[]{:S(2)}, u32[]{:S(2)}) collective-permute-start(bf16[128,1024]{1,0:T(8,128)(2,1)S(1)} %get-tuple-element.228), channel_id=1, source_target_pairs={{0,16},{8,24},{16,0},{24,8},{1,17},{9,25},{17,1},{25,9},{2,18},{10... | collective-permute-start | bytes 786440 | tf_op jit(solution)/shard_map/ppermute | solution.py:52
  73.1 19.7 %collective-permute-start.25 = (bf16[128,1024]{1,0:T(8,128)(2,1)S(1)}, bf16[128,1024]{1,0:T(8,128)(2,1)S(1)}, u32[]{:S(2)}, u32[]{:S(2)}) collective-permute-start(bf16[128,1024]{1,0:T(8,128)(2,1)S(1)} %get-tuple-element.229), channel_id=1, source_target_pairs={{0,24},{8,16},{16,8},{24,0},{1,25},{9,17},{17,9},{25,1},{2,26},{10... | collective-permute-start | bytes 786440 | tf_op jit(solution)/shard_map/ppermute | solution.py:52
  74.2 25.3 %collective-permute-start.22 = (bf16[512,1024]{1,0:T(8,128)(2,1)S(1)}, bf16[512,1024]{1,0:T(8,128)(2,1)S(1)}, u32[]{:S(2)}, u32[]{:S(2)}) collective-permute-start(bf16[512,1024]{1,0:T(8,128)(2,1)S(1)} %add.91.refs_0_), channel_id=1, source_target_pairs={{0,2},{1,3},{6,4},{7,5},{8,10},{9,11},{14,12},{15,13},{16,18},{17,... | collective-permute-start | bytes 3145736 | tf_op jit(solution)/shard_map/ppermute | solution.py:92
  92.8 7.4 %collective-permute-start.26 = (bf16[4,128,768]{2,1,0:T(8,128)(2,1)S(1)}, bf16[4,128,768]{2,1,0:T(8,128)(2,1)S(1)}, u32[]{:S(2)}, u32[]{:S(2)}) collective-permute-start(bf16[4,128,768]{2,1,0:T(8,128)(2,1)S(1)} %get-tuple-element.248), channel_id=1, source_target_pairs={{0,1},{1,0},{2,3},{3,2},{4,5},{5,4},{6,7},{7,6},{8,9},{9,8},{10,11... | collective-permute-start | bytes 2359304 | tf_op jit(solution)/shard_map/ppermute | solution.py:72
  92.9 7.3 %collective-permute-start.27 = (bf16[128,1024]{1,0:T(8,128)(2,1)S(1)}, bf16[128,1024]{1,0:T(8,128)(2,1)S(1)}, u32[]{:S(2)}, u32[]{:S(2)}) collective-permute-start(bf16[128,1024]{1,0:T(8,128)(2,1)S(1)} %get-tuple-element.249), channel_id=1, source_target_pairs={{0,1},{1,0},{2,3},{3,2},{4,5},{5,4},{6,7},{7,6},{8,9},{9,8},{10,11... | collective-permute-start | bytes 786440 | tf_op jit(solution)/shard_map/ppermute | solution.py:72
  100.9 14.0 %collective-permute-start.30 = (bf16[256,768]{1,0:T(8,128)(2,1)S(1)}, bf16[256,768]{1,0:T(8,128)(2,1)S(1)}, u32[]{:S(2)}, u32[]{:S(2)}) collective-permute-start(bf16[256,768]{1,0:T(8,128)(2,1)S(1)} %get-tuple-element.264), channel_id=1, source_target_pairs={{0,8},{8,0},{16,24},{24,16},{1,9},{9,1},{17,25},{25,17},{2,10},{10... | collective-permute-start | bytes 1179656 | tf_op jit(solution)/shard_map/ppermute | solution.py:52
  102.5 25.7 %collective-permute-start.28 = (bf16[528,1024]{1,0:T(8,128)(2,1)S(1)}, bf16[528,1024]{1,0:T(8,128)(2,1)S(1)}, u32[]{:S(2)}, u32[]{:S(2)}) collective-permute-start(bf16[528,1024]{1,0:T(8,128)(2,1)S(1)} %broadcast_dynamic-update-slice_fusion.refs_0_), channel_id=1, source_target_pairs={{0,2},{1,3},{6,4},{7,5},{8,10},{9,11},{14,12},{15,13},{16,18},{17,... | collective-permute-start | bytes 3244040 | tf_op jit(solution)/shard_map/ppermute | solution.py:92
  106.9 19.1 %collective-permute-start.29 = (bf16[512,1024]{1,0:T(8,128)(2,1)S(1)}, bf16[512,1024]{1,0:T(8,128)(2,1)S(1)}, u32[]{:S(2)}, u32[]{:S(2)}) collective-permute-start(bf16[512,1024]{1,0:T(8,128)(2,1)S(1)} %shard_map.350.refs_2_), channel_id=1, source_target_pairs={{2,4},{3,5},{4,2},{5,3},{10,12},{11,13},{12,10},{13,11},{18,20},{1... | collective-permute-start | bytes 3145736 | tf_op jit(solution)/shard_map/ppermute | solution.py:92
  115.0 10.3 %collective-permute-start.31 = (bf16[256,768]{1,0:T(8,128)(2,1)S(1)}, bf16[256,768]{1,0:T(8,128)(2,1)S(1)}, u32[]{:S(2)}, u32[]{:S(2)}) collective-permute-start(bf16[256,768]{1,0:T(8,128)(2,1)S(1)} %pad_maximum_fusion.1), channel_id=1, source_target_pairs={{0,16},{8,24},{16,0},{24,8},{1,17},{9,25},{17,1},{25,9},{2,18},{10... | collective-permute-start | bytes 1179656 | tf_op jit(solution)/shard_map/ppermute | solution.py:52
  128.9 24.4 %collective-permute-start.34 = (bf16[528,1024]{1,0:T(8,128)(2,1)S(1)}, bf16[528,1024]{1,0:T(8,128)(2,1)S(1)}, u32[]{:S(2)}, u32[]{:S(2)}) collective-permute-start(bf16[528,1024]{1,0:T(8,128)(2,1)S(1)} %get-tuple-element.283.refs_4_), channel_id=1, source_target_pairs={{0,2},{1,3},{2,0},{3,1},{4,6},{5,7},{6,4},{7,5},{8,10},{9,11},{10,... | collective-permute-start | bytes 3244040 | tf_op jit(solution)/shard_map/ppermute | solution.py:92
  132.1 21.2 %collective-permute-start.35 = (bf16[528,1024]{1,0:T(8,128)(2,1)S(1)}, bf16[528,1024]{1,0:T(8,128)(2,1)S(1)}, u32[]{:S(2)}, u32[]{:S(2)}) collective-permute-start(bf16[528,1024]{1,0:T(8,128)(2,1)S(1)} %get-tuple-element.284.refs_2_), channel_id=1, source_target_pairs={{2,4},{3,5},{4,2},{5,3},{10,12},{11,13},{12,10},{13,11},{18,20},{1... | collective-permute-start | bytes 3244040 | tf_op jit(solution)/shard_map/ppermute | solution.py:92
  132.9 22.0 %collective-permute-start.36 = (bf16[256,2048]{1,0:T(8,128)(2,1)S(1)}, bf16[256,2048]{1,0:T(8,128)(2,1)S(1)}, u32[]{:S(2)}, u32[]{:S(2)}) collective-permute-start(bf16[256,2048]{1,0:T(8,128)(2,1)S(1)} %get-tuple-element.288), channel_id=1, source_target_pairs={{0,8},{8,0},{16,24},{24,16},{1,9},{9,1},{17,25},{25,17},{2,10},{10... | collective-permute-start | bytes 3145736 | tf_op jit(solution)/shard_map/ppermute | solution.py:52
  133.5 21.7 %collective-permute-start.37 = (bf16[256,2048]{1,0:T(8,128)(2,1)S(1)}, bf16[256,2048]{1,0:T(8,128)(2,1)S(1)}, u32[]{:S(2)}, u32[]{:S(2)}) collective-permute-start(bf16[256,2048]{1,0:T(8,128)(2,1)S(1)} %get-tuple-element.289), channel_id=1, source_target_pairs={{0,16},{8,24},{16,0},{24,8},{1,17},{9,25},{17,1},{25,9},{2,18},{10... | collective-permute-start | bytes 3145736 | tf_op jit(solution)/shard_map/ppermute | solution.py:52
  156.1 12.7 %collective-permute-start.38 = (bf16[528,1024]{1,0:T(8,128)(2,1)S(1)}, bf16[528,1024]{1,0:T(8,128)(2,1)S(1)}, u32[]{:S(2)}, u32[]{:S(2)}) collective-permute-start(bf16[528,1024]{1,0:T(8,128)(2,1)S(1)} %get-tuple-element.291.refs_0_), channel_id=1, source_target_pairs={{2,4},{3,5},{4,2},{5,3},{10,12},{11,13},{12,10},{13,11},{18,20},{1... | collective-permute-start | bytes 3244040 | tf_op jit(solution)/shard_map/ppermute | solution.py:92
  156.9 27.0 %collective-permute-start.39 = (bf16[528,1024]{1,0:T(8,128)(2,1)S(1)}, bf16[528,1024]{1,0:T(8,128)(2,1)S(1)}, u32[]{:S(2)}, u32[]{:S(2)}) collective-permute-start(bf16[528,1024]{1,0:T(8,128)(2,1)S(1)} %get-tuple-element.292.refs_2_), channel_id=1, source_target_pairs={{2,0},{3,1},{4,6},{5,7},{10,8},{11,9},{12,14},{13,15},{18,16},{19,... | collective-permute-start | bytes 3244040 | tf_op jit(solution)/shard_map/ppermute | solution.py:92
  158.3 26.3 %collective-permute-start.41 = (bf16[256,1024]{1,0:T(8,128)(2,1)S(1)}, bf16[256,1024]{1,0:T(8,128)(2,1)S(1)}, u32[]{:S(2)}, u32[]{:S(2)}) collective-permute-start(bf16[256,1024]{1,0:T(8,128)(2,1)S(1)} %slice.96), channel_id=1, source_target_pairs={{0,24},{8,16},{16,8},{24,0},{1,25},{9,17},{17,9},{25,1},{2,26},{10... | collective-permute-start | bytes 1572872 | tf_op jit(solution)/shard_map/ppermute | solution.py:52
  184.7 28.1 %collective-permute-start.42 = (bf16[528,1024]{1,0:T(8,128)(2,1)S(1)}, bf16[528,1024]{1,0:T(8,128)(2,1)S(1)}, u32[]{:S(2)}, u32[]{:S(2)}) collective-permute-start(bf16[528,1024]{1,0:T(8,128)(2,1)S(1)} %get-tuple-element.301.refs_0_), channel_id=1, source_target_pairs={{2,0},{3,1},{4,6},{5,7},{10,8},{11,9},{12,14},{13,15},{18,16},{19,... | collective-permute-start | bytes 3244040 | tf_op jit(solution)/shard_map/ppermute | solution.py:92
  186.3 15.3 %collective-permute-start.44 = (bf16[256,1024]{1,0:T(8,128)(2,1)S(1)}, bf16[256,1024]{1,0:T(8,128)(2,1)S(1)}, u32[]{:S(2)}, u32[]{:S(2)}) collective-permute-start(bf16[256,1024]{1,0:T(8,128)(2,1)S(1)} %slice.97), channel_id=1, source_target_pairs={{0,24},{8,16},{16,8},{24,0},{1,25},{9,17},{17,9},{25,1},{2,26},{10... | collective-permute-start | bytes 1572872 | tf_op jit(solution)/shard_map/ppermute | solution.py:52
  (42 other events, 572.0 us)
